TPU v7x, 32 devices: a whole 2x2x4 slice. The times are simulated.
32 devices in a mesh: dp: 16 (over z, y, core), chan: 2 (over x).
Axes of the slice: x: 2, y: 2, z: 4, core: 2. Of those that a mesh axis runs over, the one named last changes fastest.
Arguments:
- h_in: bfloat16 [16, 1280, 1024], P('dp', 'chan'), may hold values from -40 to 40
- skip: bfloat16 [16, 1280, 1024], P('dp', 'chan'), may hold values from -6 to 6
- emb: bfloat16 [16, 1280], P('dp'), may hold values from -6 to 6
- w_emb: bfloat16 [1280, 1280], P('dp', 'chan'), may hold values from -0.15625 to 0.15625
- b_emb: float32 [1280], P('chan'), may hold values from -3 to 3
- gn_gain: float32 [1280], P('chan'), may hold values from 0.1 to 1.9
- gn_bias: float32 [1280], P('chan'), may hold values from -3 to 3
- w_conv: bfloat16 [9, 1280, 1280], P(None, 'dp', 'chan'), may hold values from -0.0546875 to 0.0546875
- b_conv: float32 [1280], P('chan'), may hold values from -3 to 3
Outputs:
- block_out: bfloat16 [16, 1280, 1024], P('dp', 'chan')
All inputs are finite; a program needn't handle non-finite values.
Results may differ from a plain program's by a relative error of at most 0.0036.
Values may be sent and summed in bfloat16 or wider, within the bound.
No kernel may reach another device: no remote copies, remote signals or barrier semaphores. Data moves between devices by JAX's collectives and lax.ppermute only.
A program may use at most 128 MiB of HBM per device.

v0:
```python
import jax
import jax.numpy as jnp
from jax import lax
from jax.sharding import PartitionSpec as P

C = 1280
GROUPS = 32
HEIGHT = 32
WIDTH = 32


def add_taps(total, rows, weights):
    images = rows.shape[0]
    count = rows.shape[1]
    grid = rows.reshape(images, count, HEIGHT, WIDTH)
    padded = jnp.pad(grid, ((0, 0), (0, 0), (1, 1), (1, 1)))
    for row_off in range(3):
        for col_off in range(3):
            window = padded[:, :, row_off : row_off + HEIGHT, col_off : col_off + WIDTH].reshape(
                images, count, HEIGHT * WIDTH
            )
            total = total + jnp.einsum(
                "bip,io->bop",
                window,
                weights[3 * row_off + col_off],
                preferred_element_type=jnp.float32,
            )
    return total


def body(h_in, skip, emb, w_emb, b_emb, gn_gain, gn_bias, w_conv, b_conv):
    images = h_in.shape[0]
    panel = h_in.shape[1]
    cells = h_in.shape[2]
    act = jax.nn.silu(emb.astype(jnp.float32)).astype(jnp.bfloat16)
    emb_full = lax.all_gather(w_emb, "dp", axis=0, tiled=True)
    shift = jnp.dot(act, emb_full, preferred_element_type=jnp.float32) + b_emb
    hidden = h_in.astype(jnp.float32) + shift[:, :, None]
    group_size = C // GROUPS
    grouped = hidden.reshape(images, panel // group_size, group_size, cells)
    mean = jnp.mean(grouped, axis=(2, 3), keepdims=True)
    var = jnp.mean((grouped - mean) ** 2, axis=(2, 3), keepdims=True)
    scaled = ((grouped - mean) * lax.rsqrt(var + 1e-05)).reshape(images, panel, cells)
    normed = jax.nn.silu(scaled * gn_gain[:, None] + gn_bias[:, None]).astype(jnp.bfloat16)
    empty = jnp.zeros((images, panel, cells), jnp.float32)
    weight_full = lax.all_gather(w_conv, "dp", axis=1, tiled=True)
    conv = add_taps(empty, lax.all_gather(normed, "chan", axis=1, tiled=True), weight_full)
    conv = conv + b_conv[None, :, None]
    return (skip.astype(jnp.float32) + conv).astype(jnp.bfloat16)


def solution(mesh):
    return jax.shard_map(
        body,
        mesh=mesh,
        in_specs=(
            P("dp", "chan", None),
            P("dp", "chan", None),
            P("dp", None),
            P("dp", "chan"),
            P("chan"),
            P("chan"),
            P("chan"),
            P(None, "dp", "chan"),
            P("chan"),
        ),
        out_specs=P("dp", "chan", None),
        check_vma=False,
    )
```

profile of v0, /device:TPU:0, one launch (start us, length us, event | category | flops | bytes accessed | tf_op | source)
XLA Modules:
  0.0 251.6 jit_solution(10070383482449908139)
XLA Ops:
  6.5 0.7 all-gather.4.cloned.1.call-update
  7.3 0.0 all-gather.6.cloned.1.call-start
  7.3 1.7 copy.16
  9.0 43.1 %all-gather.4.cloned.1.call-done = bf16[1280,640]{1,0:T(8,128)(2,1)} async-done(((bf16[80,640]{1,0:T(8,128)(2,1)}), bf16[1280,640]{1,0:T(8,128)(2,1)}) %all-gather.4.cloned.1.call-update) | async-done | bytes 1638416 | tf_op jit(solution)/shard_map/all_gather | solution.py:36
  52.2 1.8 convolution_reduce_fusion
  54.0 0.3 fusion.4
  54.3 0.1 reduce_sum.24
  54.4 0.1 reduce_sum.25
  54.5 0.1 sub.22
  54.6 0.1 sub.23
  54.7 0.5 multiply_reduce_fusion
  55.2 0.1 reduce_sum.36
  55.2 0.1 reduce_sum.37
  55.4 0.1 mul.37
  55.4 0.1 mul.38
  55.6 2.1 multiply_convert_fusion
  57.6 0.0 all-gather.8.cloned.1.call-start
  57.7 0.7 all-gather.8.cloned.1.call-update
  58.4 1.4 copy.15
  59.8 35.9 %all-gather.6.cloned.1.call-done = bf16[1,1280,1024]{1,2,0:T(8,128)(2,1)} async-done(((bf16[1,640,1024]{1,2,0:T(8,128)(2,1)}), bf16[1,1280,1024]{1,2,0:T(8,128)(2,1)}) %all-gather.6.cloned.1.call-update) | async-done | bytes 2621456 | tf_op jit(solution)/shard_map/all_gather | solution.py:47
  95.7 16.2 %pad_slice_fusion.7 = (bf16[1,1280,32,32]{1,3,2,0:T(8,128)(2,1)S(1)}, bf16[1,1280,32,32]{1,3,2,0:T(8,128)(2,1)}, bf16[1,1280,32,32]{1,3,2,0:T(8,128)(2,1)}, bf16...) fusion(bf16[1,1280,32,32]{1,3,2,0:T(8,128)(2,1)} %bitcast.60), kind=kLoop, calls=%fused_computation.7 | loop fusion | bytes 23592960 | tf_op jit(solution)/shard_map/slice | solution.py:19
  111.9 100.3 %all-gather.8.cloned.1.call-done = bf16[9,1280,640]{2,1,0:T(8,128)(2,1)} async-done(((bf16[9,80,640]{2,1,0:T(8,128)(2,1)}), bf16[9,1280,640]{2,1,0:T(8,128)(2,1)}) %all-gather.8.cloned.1.call-update) | async-done | bytes 14745616 | tf_op jit(solution)/shard_map/all_gather | solution.py:46
  212.2 4.6 %fusion.1 = f32[1024,640]{1,0:T(8,128)S(1)} fusion(bf16[1,1280,1024]{1,2,0:T(8,128)(2,1)} %all-gather.6.cloned.1.call-done, bf16[9,1280,640]{2,1,0:T(8,128)(2,1)} %all-gather.8.cloned.1.call-done), kind=kOutput, calls=%fused_computation.10 | convolution fusion | flops 1677721600 | bytes 6881280 | tf_op jit(solution)/shard_map/bip,io->bop/dot_general | solution.py:22
  216.8 4.4 %fusion.10 = f32[1024,640]{1,0:T(8,128)S(1)} fusion(bf16[1280,1024]{0,1:T(8,128)(2,1)S(1)} %bitcast.67, bf16[9,1280,640]{2,1,0:T(8,128)(2,1)} %all-gather.8.cloned.1.call-done), kind=kOutput, calls=%fused_computation.29 | convolution fusion | flops 1677721600 | bytes 6881280 | tf_op jit(solution)/shard_map/bip,io->bop/dot_general | solution.py:22
  221.3 2.2 fusion.11
  223.5 2.2 fusion.5
  225.7 2.2 fusion.6
  227.9 2.2 fusion.7
  230.1 2.2 fusion.8
  232.4 3.9 %fusion.9 = f32[1024,640]{1,0:T(8,128)} fusion(bf16[1280,1024]{0,1:T(8,128)(2,1)S(1)} %bitcast.61, bf16[9,1280,640]{2,1,0:T(8,128)(2,1)S(1)} %copy-done.9), kind=kOutput, calls=%fused_computation.27 | convolution fusion | flops 1677721600 | bytes 6881280 | tf_op jit(solution)/shard_map/bip,io->bop/dot_general | solution.py:22
  236.3 6.4 %fusion = bf16[1,640,1024]{1,2,0:T(8,128)(2,1)} fusion(f32[1024,640]{1,0:T(8,128)S(1)} %fusion.5, f32[1024,640]{1,0:T(8,128)S(1)} %fusion.6, f32[1024,640]{1,0:T(8,128)S(1)} %fusion.7, f32[1024,640]{1,0:T(8,128)S(1)} %fusion.8, f32[1024,640]{1,0:T(8,128)S(1)} %fusion.1, f32[1024,640]{1,0:T(8,128)} %fusion.9, f32[1024,640]{1,0:T(8,128)S(1)} %fusion.10, ...), kind=kOutput, calls=%fused_computation.9 | convolution fusion | flops 1685585920 | bytes 27855360 | tf_op jit(solution)/shard_map/bip,io->bop/dot_general | solution.py:22
  242.7 2.4 copy.17
  (35 shorter events, 0.1 us)
Async XLA Ops:
  6.5 45.6 %copy-start.10 = (bf16[1,1280]{1,0:T(2,128)(2,1)S(1)}, bf16[1,1280]{1,0:T(2,128)(2,1)}, u32[]{:S(2)}) copy-start(bf16[1,1280]{1,0:T(2,128)(2,1)} %param.11) | copy-start | bytes 7684
  6.5 47.4 %copy-start.14 = (f32[640]{0:T(1024)S(1)}, f32[640]{0:T(1024)}, u32[]{:S(2)}) copy-start(f32[640]{0:T(1024)} %param.13) | copy-start | bytes 7684
  6.5 45.6 %all-gather.4.cloned.1.call-start = ((), (), s32[]{:S(2)}) async-start(), calls=%async_computation | async-start | bytes 1740800 | tf_op jit(solution)/shard_map/all_gather | solution.py:36
  7.3 88.5 %all-gather.6.cloned.1.call-start = ((), (), s32[]{:S(2)}) async-start(), calls=%async_computation.1 | async-start | bytes 3932160 | tf_op jit(solution)/shard_map/all_gather | solution.py:47
  9.0 46.5 %copy-start.11 = (f32[640]{0:T(1024)S(1)}, f32[640]{0:T(1024)}, u32[]{:S(2)}) copy-start(f32[640]{0:T(1024)} %param.15) | copy-start | bytes 7684
  9.0 46.5 %copy-start.12 = (f32[640]{0:T(1024)S(1)}, f32[640]{0:T(1024)}, u32[]{:S(2)}) copy-start(f32[640]{0:T(1024)} %param.14) | copy-start | bytes 7684
  55.1 3.2 %copy-start.8 = (bf16[1,640,1024]{2,1,0:T(8,128)(2,1)S(1)}, bf16[1,640,1024]{2,1,0:T(8,128)(2,1)}, u32[]{:S(2)}) copy-start(bf16[1,640,1024]{2,1,0:T(8,128)(2,1)} %param.10) | copy-start | bytes 3932164
  57.6 154.6 %all-gather.8.cloned.1.call-start = ((), (), s32[]{:S(2)}) async-start(), calls=%async_computation.2 | async-start | bytes 15667200 | tf_op jit(solution)/shard_map/all_gather | solution.py:46
  212.2 4.6 %copy-start.7 = (bf16[1,1280,32,32]{1,3,2,0:T(8,128)(2,1)S(1)}, bf16[1,1280,32,32]{1,3,2,0:T(8,128)(2,1)}, u32[]{:S(2)}) copy-start(bf16[1,1280,32,32]{1,3,2,0:T(8,128)(2,1)} %get-tuple-element.7) | copy-start | bytes 7864324
  212.2 9.0 %copy-start.9 = (bf16[9,1280,640]{2,1,0:T(8,128)(2,1)S(1)}, bf16[9,1280,640]{2,1,0:T(8,128)(2,1)}, u32[]{:S(2)}) copy-start(bf16[9,1280,640]{2,1,0:T(8,128)(2,1)} %all-gather.8.cloned.1.call-done) | copy-start | bytes 44236804
  216.8 4.5 %copy-start.6 = (bf16[1,1280,32,32]{1,3,2,0:T(8,128)(2,1)S(1)}, bf16[1,1280,32,32]{1,3,2,0:T(8,128)(2,1)}, u32[]{:S(2)}) copy-start(bf16[1,1280,32,32]{1,3,2,0:T(8,128)(2,1)} %get-tuple-element.6) | copy-start | bytes 7864324
  221.3 2.2 copy-start.5
  223.5 2.2 copy-start.4
  225.7 2.2 copy-start.3
  227.9 2.2 copy-start.2
  230.1 2.2 copy-start.1
  232.4 3.9 %copy-start = (bf16[1,640,1024]{1,2,0:T(8,128)(2,1)S(1)}, bf16[1,640,1024]{1,2,0:T(8,128)(2,1)}, u32[]{:S(2)}) copy-start(bf16[1,640,1024]{1,2,0:T(8,128)(2,1)} %copy.15) | copy-start | bytes 3932164
  232.4 3.9 %copy-start.13 = (f32[640]{0:T(1024)S(1)}, f32[640]{0:T(1024)}, u32[]{:S(2)}) copy-start(f32[640]{0:T(1024)} %param.17) | copy-start | bytes 7684
Sparse Core Ops, SparseCore 0:
  9.5 42.6 all-gather.3
  57.8 37.9 all-gather.5
  97.9 114.2 all-gather.7
where the time goes:
time: 252 us
  waiting for transfers between devices  181 us (72%)
  matrix products  32 us (13%)
  local copies, waits for them, and re-layouts  22.3 us (9%)
  between operations  13.4 us (5%)
  other arithmetic  3.11 us (1%)
    all_gather x1, waiting for transfers between devices, body(): weight_full = lax.all_gather(w_conv, 'dp', axis=1, tiled=True)  100 us
    all_gather x1, waiting for transfers between devices, body(): emb_full = lax.all_gather(w_emb, 'dp', axis=0, tiled=True)  43.1 us
    all_gather x1, waiting for transfers between devices, body(): lax.all_gather(normed, 'chan', axis=1, tiled=True)  35.9 us
    dot_general x9, matrix products, add_taps(): jnp.einsum('bip,io->bop', window, weights[3 * row_off + col_off], preferr...  30.3 us
    slice x1, local copies, waits for them, and re-layouts, add_taps(): padded[:, :, row_off:row_off + HEIGHT, col_off:col_off + WIDTH]  16.2 us
  transfers between devices with their start and end apart: 3, of which 3 were waited for; matrix products, arithmetic and copies ran while one was open for 8% of the time, Pallas kernels for 0%

commit v1 on v0

v1 whole, which is shorter than its diff:
```python
import functools

import jax
import jax.numpy as jnp
import numpy as np
from jax import lax
from jax.experimental import pallas as pl
from jax.experimental.pallas import tpu as pltpu
from jax.sharding import PartitionSpec as P

C = 1280
GROUPS = 32
HEIGHT = 32
WIDTH = 32
CELLS = HEIGHT * WIDTH
PADDED = CELLS + 2 * WIDTH
TILE = 256
ANY = pl.BlockSpec(memory_space=pl.ANY)


def chip_order(chips):
    if chips % 2:
        return list(range(chips))
    half = chips // 2
    return [2 * z for z in range(half)] + [2 * z + 1 for z in reversed(range(half))]


class Ring:
    def __init__(self, dp):
        self.dp = dp
        self.chips = dp // 2
        self.order = chip_order(self.chips)
        self.core_pairs = [(i, i ^ 1) for i in range(dp)]
        n, order = self.chips, self.order
        self.pairs = [(2 * order[k], 2 * order[(k + 1) % n]) for k in range(n)]
        self.pairs += [(2 * order[k] + 1, 2 * order[(k - 1) % n] + 1) for k in range(n)]
        full = (n - 1) // 2
        self.hops = [(s, h) for s in range(1, full + 1) for h in range(2)]
        if n % 2 == 0:
            self.hops.append((full + 1, 0))
        self.blocks = np.zeros((dp, dp), np.int32)
        for k in range(n):
            for core in range(2):
                me = 2 * order[k] + core
                units = [me, me ^ 1]
                for s, h in self.hops:
                    for c in (core, 1 - core):
                        chip = order[(k - s) % n] if c == 0 else order[(k + s) % n]
                        units.append(2 * chip + (c if h == 0 else 1 - c))
                self.blocks[me] = units
        self.places = np.argsort(self.blocks, axis=1).astype(np.int32)


def norm_kernel(place_ref, h_ref, ab_ref, *rest):
    x_ref = rest[-1]
    ab = ab_ref[0]
    v = h_ref[0].astype(jnp.float32) * ab[:, 0:1] + ab[:, 1:2]
    normed = v / (1.0 + jnp.exp(-v))
    column = lax.broadcasted_iota(jnp.int32, normed.shape, 1) % WIDTH
    left = jnp.where(column > 0, pltpu.roll(normed, 1, 1), 0.0)
    right = jnp.where(column < WIDTH - 1, pltpu.roll(normed, CELLS - 1, 1), 0.0)
    stack = jnp.concatenate([left, normed, right], axis=0)
    edge = jnp.zeros((WIDTH, x_ref.shape[2]), jnp.bfloat16)
    x_ref[0, :WIDTH, :] = edge
    x_ref[0, WIDTH + CELLS :, :] = edge
    x_ref[0, WIDTH : WIDTH + CELLS, :] = stack.T.astype(jnp.bfloat16)


def norm_call(units, places, h, ab, windows):
    blocks, rows, _ = h.shape
    shape = jax.ShapeDtypeStruct((units, PADDED, 3 * rows), jnp.bfloat16)
    more = () if windows is None else (windows,)
    return pl.pallas_call(
        norm_kernel,
        grid_spec=pltpu.PrefetchScalarGridSpec(
            num_scalar_prefetch=1,
            grid=(blocks,),
            in_specs=[
                pl.BlockSpec((1, rows, CELLS), lambda j, place: (j, 0, 0)),
                pl.BlockSpec((1, rows, 2), lambda j, place: (j, 0, 0)),
            ]
            + [ANY] * len(more),
            out_specs=pl.BlockSpec((1, PADDED, 3 * rows), lambda j, place: (place[j], 0, 0)),
        ),
        out_shape=shape,
        input_output_aliases={3: 0} if more else {},
        cost_estimate=pl.CostEstimate(
            flops=20 * blocks * rows * CELLS,
            transcendentals=2 * blocks * rows * CELLS,
            bytes_accessed=8 * blocks * rows * CELLS,
        ),
        name="norm_windows",
    )(places, h, ab, *more)


def conv_kernel(count, first, last, *refs):
    start = first == 0
    total_ref, x_ref = refs[:2]
    weight_refs = refs[2 : 2 + count]
    rest = refs[2 + count :]
    if last:
        skip_ref, rest = rest[0], rest[1:]
    out_ref, xs, ws, total, x_sem, w_sem, in_sem, out_sem = rest
    tiles = CELLS // TILE
    x_copies = [pltpu.make_async_copy(x_ref.at[first + u], xs.at[u], x_sem.at[u]) for u in range(count)]
    w_copies = [pltpu.make_async_copy(weight_refs[u], ws.at[u], w_sem.at[u]) for u in range(count)]
    rows = [pl.ds(t * TILE, TILE) for t in range(tiles)]
    in_copies = [] if start else [
        pltpu.make_async_copy(total_ref.at[rows[t]], total.at[rows[t]], in_sem.at[t]) for t in range(tiles)
    ]
    out_copies = [] if last else [
        pltpu.make_async_copy(total.at[rows[t]], out_ref.at[rows[t]], out_sem.at[t]) for t in range(tiles)
    ]
    for u in range(count):
        w_copies[u].start()
        x_copies[u].start()
    for copy in in_copies:
        copy.start()
    for t in range(tiles):
        base = t * TILE
        part = total_ref[...] if start else None
        for u in range(count):
            if t == 0:
                w_copies[u].wait()
                x_copies[u].wait()
            for dy in range(3):
                window = xs[u, base + WIDTH * dy : base + WIDTH * dy + TILE, :]
                term = jnp.dot(window, ws[u, dy], preferred_element_type=jnp.float32)
                part = term if part is None else part + term
        if not start:
            in_copies[t].wait()
            part = part + total[base : base + TILE, :]
        if last:
            skipped = skip_ref[:, base : base + TILE].astype(jnp.float32)
            out_ref[:, base : base + TILE] = (skipped + part.T).astype(jnp.bfloat16)
        else:
            total[base : base + TILE, :] = part
            out_copies[t].start()
    for copy in out_copies:
        copy.wait()


def conv_call(first, total, windows, weights, skip=None):
    count = len(weights)
    _, depth, outs = weights[0].shape
    last = skip is not None
    whole = pl.BlockSpec(memory_space=pltpu.VMEM)
    start = first == 0
    out_shape = (
        jax.ShapeDtypeStruct((outs, CELLS), jnp.bfloat16) if last else jax.ShapeDtypeStruct((CELLS, outs), jnp.float32)
    )
    tiles = CELLS // TILE
    return pl.pallas_call(
        functools.partial(conv_kernel, count, first, last),
        out_shape=out_shape,
        in_specs=[whole if start else ANY, ANY] + [ANY] * count + [whole] * last,
        out_specs=whole if last else ANY,
        scratch_shapes=[
            pltpu.VMEM((count, PADDED, depth), jnp.bfloat16),
            pltpu.VMEM((count, 3, depth, outs), jnp.bfloat16),
            pltpu.VMEM((CELLS, outs), jnp.float32),
            pltpu.SemaphoreType.DMA((count,)),
            pltpu.SemaphoreType.DMA((count,)),
            pltpu.SemaphoreType.DMA((tiles,)),
            pltpu.SemaphoreType.DMA((tiles,)),
        ],
        input_output_aliases={0: 0} if not (start or last) else {},
        compiler_params=pltpu.CompilerParams(vmem_limit_bytes=36 * 2**20),
        cost_estimate=pl.CostEstimate(
            flops=2 * CELLS * 3 * depth * outs * count,
            transcendentals=0,
            bytes_accessed=2 * count * 3 * depth * outs + 8 * CELLS * outs,
        ),
        name="conv_units",
    )(total, windows, *weights, *([skip] if last else []))


def make_body(dp, chan):
    ring = Ring(dp)
    chan_pairs = [(i, (i + 1) % chan) for i in range(chan)]

    def body(h_in, skip, emb, w_emb, b_emb, gn_gain, gn_bias, w_conv, b_conv):
        panel = h_in.shape[1]
        rows, outs = w_conv.shape[1], w_conv.shape[2]
        blocks = panel // rows
        me = lax.axis_index("dp")
        side = lax.axis_index("chan")

        own = w_conv.reshape(3, 3 * rows, outs)
        other = lax.ppermute(own, "dp", ring.core_pairs)
        units = [own, other]
        moving = [own, other]
        for _, half in ring.hops:
            moving[half] = lax.ppermute(moving[half], "dp", ring.pairs)
            units.append(moving[half])
            units.append(lax.ppermute(moving[half], "dp", ring.core_pairs))

        slices = [h_in.reshape(blocks, rows, CELLS)]
        for _ in range(chan - 1):
            slices.append(lax.ppermute(slices[-1], "chan", chan_pairs))

        act = jax.nn.silu(emb.astype(jnp.float32)).astype(jnp.bfloat16)
        act_rows = lax.all_to_all(act.reshape(dp, rows), "dp", 0, 0, tiled=True)
        terms = jnp.dot(act_rows, w_emb, preferred_element_type=jnp.float32)
        shift = jnp.sum(lax.all_to_all(terms, "dp", 0, 0, tiled=True), axis=0) + b_emb

        values = h_in[0].astype(jnp.float32)
        channel_mean = jnp.mean(values, axis=1, keepdims=True)
        channel_var = jnp.mean((values - channel_mean) ** 2, axis=1)
        size = C // GROUPS
        centers = (channel_mean[:, 0] + shift).reshape(panel // size, size)
        mean = jnp.mean(centers, axis=1, keepdims=True)
        var = jnp.mean(channel_var.reshape(panel // size, size) + (centers - mean) ** 2, axis=1, keepdims=True)
        scale = jnp.broadcast_to(lax.rsqrt(var + 1e-05), centers.shape).reshape(panel) * gn_gain
        offset = (shift - jnp.broadcast_to(mean, centers.shape).reshape(panel)) * scale + gn_bias
        affines = [jnp.stack([scale, offset])]
        for _ in range(chan - 1):
            affines.append(lax.ppermute(affines[-1], "chan", chan_pairs))

        windows = None
        table = jnp.asarray(ring.places)
        for turn in range(chan):
            place = lax.dynamic_slice(table, (me, ((side - turn) % chan) * blocks), (1, blocks))[0]
            ab = affines[turn].T.reshape(blocks, rows, 2)
            windows = norm_call(dp, place, slices[turn], ab, windows)

        total = b_conv.reshape(1, outs)
        cuts = [0, 4, 8, 12, dp - 2, dp] if dp == 16 else list(range(0, dp, 4)) + [dp]
        for first, stop in zip(cuts[:-2], cuts[1:-1]):
            total = conv_call(first, total, windows, units[first:stop])
        first = cuts[-2]
        out = conv_call(first, total, windows, units[first:], skip[0])
        return out[None]

    return body


def solution(mesh):
    return jax.shard_map(
        make_body(mesh.shape["dp"], mesh.shape["chan"]),
        mesh=mesh,
        in_specs=(
            P("dp", "chan", None),
            P("dp", "chan", None),
            P("dp", None),
            P("dp", "chan"),
            P("chan"),
            P("chan"),
            P("chan"),
            P(None, "dp", "chan"),
            P("chan"),
        ),
        out_specs=P("dp", "chan", None),
        check_vma=False,
    )
```

time: 252 us -> 143 us (0.57)
  waiting for transfers between devices: 181 us -> 41.4 us
  Pallas kernels: 0 us -> 59.1 us
  matrix products: 32 us -> 0.13 us
  starting transfers between devices: 0.08 us -> 21.8 us
  between operations: 13.4 us -> 0.45 us
  local copies, waits for them, and re-layouts: 22.3 us -> 14 us
    all_gather x3 -> x0, waiting for transfers between devices: 179 us -> none  [the longest x1 100 us: body(): weight_full = lax.all_gather(w_conv, 'dp', axis=1, tiled=True)]
    pallas_call x0 -> x7, Pallas kernels: none -> 59.1 us  [the longest x5 42.2 us: conv_call(): pl.pallas_call(functools.partial(conv_kernel, count, first, last), out_sh...]
    dot_general x10 -> x1, matrix products: 32 us -> 0.13 us  [body(): terms = jnp.dot(act_rows, w_emb, preferred_element_type=jnp.float32)]
    ppermute x0 -> x17, waiting for transfers between devices: none -> 23.9 us  [the longest x7 21.7 us: body(): moving[half] = lax.ppermute(moving[half], 'dp', ring.pairs)]
    all_to_all x0 -> x2, waiting for transfers between devices: none -> 17.5 us  [the longest x1 17.5 us: body(): lax.all_to_all(terms, 'dp', 0, 0, tiled=True)]
    slice x1 -> x0, local copies, waits for them, and re-layouts: 16.2 us -> none  [add_taps(): padded[:, :, row_off:row_off + HEIGHT, col_off:col_off + WIDTH]]
    ppermute x0 -> x17, starting transfers between devices: none -> 12.9 us  [the longest x7 8.71 us: body(): moving[half] = lax.ppermute(moving[half], 'dp', ring.pairs)]
    all_to_all x0 -> x2, starting transfers between devices: none -> 8.89 us  [the longest x1 5.04 us: body(): act_rows = lax.all_to_all(act.reshape(dp, rows), 'dp', 0, 0, tiled=True)]
  transfers between devices with their start and end apart: 3 -> 19, of which waited for: 3 -> 4; matrix products, arithmetic and copies ran while one was open for 8% -> 7% of each run, Pallas kernels for 0% -> 37%
where the time goes in v1:
time: 143 us; the launch traced here: 142 us
  Pallas kernels  59.1 us (41%)
  waiting for transfers between devices  41.4 us (29%)
  starting transfers between devices  21.8 us (15%)
  local copies, waits for them, and re-layouts  14 us (10%)
  other arithmetic  5.15 us (4%)
    pallas_call x5, Pallas kernels, conv_call(): pl.pallas_call(functools.partial(conv_kernel, count, first, last), out_sh...  42.2 us
    ppermute x7, waiting for transfers between devices, body(): moving[half] = lax.ppermute(moving[half], 'dp', ring.pairs)  21.7 us
    all_to_all x1, waiting for transfers between devices, body(): lax.all_to_all(terms, 'dp', 0, 0, tiled=True)  17.5 us
    pallas_call x2, Pallas kernels, norm_call(): pl.pallas_call(norm_kernel, grid_spec=pltpu.PrefetchScalarGridSpec(num_sc...  16.9 us
    unnamed x26, local copies, waits for them, and re-layouts  8.98 us
    ppermute x7, starting transfers between devices, body(): moving[half] = lax.ppermute(moving[half], 'dp', ring.pairs)  8.71 us
    all_to_all x1, starting transfers between devices, body(): act_rows = lax.all_to_all(act.reshape(dp, rows), 'dp', 0, 0, tiled=True)  5.04 us
    all_to_all x1, starting transfers between devices, body(): lax.all_to_all(terms, 'dp', 0, 0, tiled=True)  3.85 us
  transfers between devices with their start and end apart: 19, of which 4 were waited for; matrix products, arithmetic and copies ran while one was open for 7% of the time, Pallas kernels for 37%

profile of v1, /device:TPU:0, one launch (start us, length us, event | category | flops | bytes accessed | tf_op | source)
XLA Modules:
  0.0 142.0 jit_solution(9128828659070424991)
XLA Ops:
  0.0 3.1 %collective-permute-start.3 = (bf16[3,240,640]{2,1,0:T(8,128)(2,1)}, bf16[3,240,640]{2,1,0:T(8,128)(2,1)S(1)}, u32[]{:S(2)}, u32[]{:S(2)}) collective-permute-start(bf16[3,240,640]{2,1,0:T(8,128)(2,1)} %bitcast.28), channel_id=1, source_target_pairs={{0,8},{8,16},{16,24},{24,28},{28,20},{20,12},{12,4},{4,0},{2,6},{1... | collective-permute-start | bytes 2764808 | tf_op jit(solution)/shard_map/ppermute | solution.py:194
  3.1 0.7 convert_reduce_fusion.1
  3.8 0.7 all_to_all.19
  4.5 5.0 %all-to-all-start = ((bf16[16,1,80]{2,1,0:T(2,128)(2,1)}), bf16[16,1,80]{2,1,0:T(2,128)(2,1)S(1)}, u32[]{:S(2)}, u32[]{:S(2)}) async-start(bf16[16,1,80]{2,1,0:T(2,128)(2,1)} %all_to_all.19), calls=%async_computation | async-start | bytes 16384 | tf_op jit(solution)/shard_map/all_to_all | solution.py:203
  9.6 1.6 %collective-permute-start = (bf16[8,80,1024]{2,1,0:T(8,128)(2,1)}, bf16[8,80,1024]{2,1,0:T(8,128)(2,1)}, u32[]{:S(2)}, u32[]{:S(2)}) collective-permute-start(bf16[8,80,1024]{2,1,0:T(8,128)(2,1)} %bitcast.31), channel_id=1, source_target_pairs={{0,1},{1,0},{2,3},{3,2},{4,5},{5,4},{6,7},{7,6},{8,9},{9,8},{10,11... | collective-permute-start | bytes 3932168 | tf_op jit(solution)/shard_map/ppermute | solution.py:200
  11.1 3.6 %collective-permute-done.3.refs_4_ = bf16[3,240,640]{2,1,0:T(8,128)(2,1)S(1)} collective-permute-done((bf16[3,240,640]{2,1,0:T(8,128)(2,1)}, bf16[3,240,640]{2,1,0:T(8,128)(2,1)S(1)}, u32[]{:S(2)}, u32[]{:S(2)}) %collective-permute-start.3) | collective-permute-done | bytes 921632 | tf_op jit(solution)/shard_map/ppermute | solution.py:194
  14.7 2.1 %collective-permute-start.7 = (bf16[3,240,640]{2,1,0:T(8,128)(2,1)S(1)}, bf16[3,240,640]{2,1,0:T(8,128)(2,1)S(1)}, u32[]{:S(2)}, u32[]{:S(2)}) collective-permute-start(bf16[3,240,640]{2,1,0:T(8,128)(2,1)S(1)} %collective-permute-done.3.refs_4_), channel_id=1, source_target_pairs={{0,8},{8,16},{16,24},{24,28},{28,20},{20,12},{12,4},{4,0},{2,6},{1... | collective-permute-start | bytes 2764808 | tf_op jit(solution)/shard_map/ppermute | solution.py:194
  16.8 1.6 %collective-permute-start.5 = (bf16[3,240,640]{2,1,0:T(8,128)(2,1)}, bf16[3,240,640]{2,1,0:T(8,128)(2,1)S(1)}, u32[]{:S(2)}, u32[]{:S(2)}) collective-permute-start(bf16[3,240,640]{2,1,0:T(8,128)(2,1)} %collective-permute-done.2.refs_3_), channel_id=1, source_target_pairs={{0,8},{8,16},{16,24},{24,28},{28,20},{20,12},{12,4},{4,0},{2,6},{1... | collective-permute-start | bytes 2764808 | tf_op jit(solution)/shard_map/ppermute | solution.py:194
  19.3 3.9 %all-to-all-start.1 = ((f32[16,1,640]{2,1,0:T(1,128)}), f32[16,1,640]{2,1,0:T(1,128)S(1)}, u32[]{:S(2)}, u32[]{:S(2)}) async-start(f32[16,1,640]{2,1,0:T(1,128)} %copy.25), calls=%async_computation.1 | async-start | bytes 81920 | tf_op jit(solution)/shard_map/all_to_all | solution.py:205
  23.1 1.6 %convert_reduce_fusion = f32[640]{0:T(1024)S(1)} fusion(bf16[1,640,1024]{2,1,0:T(8,128)(2,1)} %param.10), kind=kLoop, calls=%fused_computation | loop fusion | flops 1310080 | bytes 1313280 | tf_op jit(solution)/shard_map/reduce_sum | solution.py:208
  24.7 17.5 %all-to-all-done.1 = f32[16,1,640]{2,1,0:T(1,128)S(1)} async-done(((f32[16,1,640]{2,1,0:T(1,128)}), f32[16,1,640]{2,1,0:T(1,128)S(1)}, u32[]{:S(2)}, u32[]{:S(2)}) %all-to-all-start.1) | async-done | bytes 40992 | tf_op jit(solution)/shard_map/all_to_all | solution.py:205
  42.2 0.7 fusion.5
  43.1 1.8 %fusion.2 = f32[640]{0:T(1024)S(1)} fusion(bf16[1,640,1024]{2,1,0:T(8,128)(2,1)} %param.10, f32[640]{0:T(1024)S(1)} %get-tuple-element.13), kind=kLoop, calls=%fused_computation.4 | loop fusion | flops 2620800 | bytes 1315840 | tf_op jit(solution)/shard_map/reduce_sum | solution.py:209
  46.6 1.6 %collective-permute-start.1 = (f32[2,640]{1,0:T(2,128)S(1)}, f32[2,640]{1,0:T(2,128)S(1)}, u32[]{:S(2)}, u32[]{:S(2)}) collective-permute-start(f32[2,640]{1,0:T(2,128)S(1)} %get-tuple-element.12), channel_id=1, source_target_pairs={{0,1},{1,0},{2,3},{3,2},{4,5},{5,4},{6,7},{7,6},{8,9},{9,8},{10,11... | collective-permute-start | bytes 15368 | tf_op jit(solution)/shard_map/ppermute | solution.py:218
  48.2 2.1 %collective-permute-done.1 = f32[2,640]{1,0:T(2,128)S(1)} collective-permute-done((f32[2,640]{1,0:T(2,128)S(1)}, f32[2,640]{1,0:T(2,128)S(1)}, u32[]{:S(2)}, u32[]{:S(2)}) %collective-permute-start.1) | collective-permute-done | bytes 5152 | tf_op jit(solution)/shard_map/ppermute | solution.py:218
  50.3 18.1 %collective-permute-done.9.refs_2_ = bf16[3,240,640]{2,1,0:T(8,128)(2,1)} collective-permute-done((bf16[3,240,640]{2,1,0:T(8,128)(2,1)S(1)}, bf16[3,240,640]{2,1,0:T(8,128)(2,1)}, u32[]{:S(2)}, u32[]{:S(2)}) %collective-permute-start.9) | collective-permute-done | bytes 921632 | tf_op jit(solution)/shard_map/ppermute | solution.py:194
  69.4 0.9 copy-done.8
  70.8 1.0 copy-done.3
  71.8 1.4 dynamic-slice_bitcast_fusion
  73.2 0.9 copy.27
  74.1 8.5 %norm_windows.2.rest_0_ = bf16[16,1088,240]{2,1,0:T(8,128)(2,1)} custom-call(s32[8]{0:T(128)} %get-tuple-element.9.place_ref, bf16[8,80,1024]{2,1,0:T(8,128)(2,1)} %bitcast.32, f32[8,80,2]{2,1,0:T(8,128)} %bitcast.34), custom_call_target="tpu_custom_call" | custom-call | flops 13107200 | bytes 5242880 | tf_op jit(solution)/shard_map/norm_windows/pallas_call | solution.py:73
  82.6 0.9 copy.26
  83.5 8.4 %norm_windows.3.refs_1_ = bf16[16,1088,240]{2,1,0:T(8,128)(2,1)} custom-call(s32[8]{0:T(128)} %get-tuple-element.10.place_ref, bf16[8,80,1024]{2,1,0:T(8,128)(2,1)} %collective-permute-done.h_ref, f32[8,80,2]{2,1,0:T(8,128)} %bitcast.33, bf16[16,1088,240]{2,1,0:T(8,128)(2,1)} %norm_windows.2.rest_0_), custom_call_target="tpu_custom_call", output_to_operand_aliasing={{}: (3, {})} | custom-call | flops 13107200 | bytes 5242880 | tf_op jit(solution)/shard_map/norm_windows/pallas_call | solution.py:73
  92.4 3.5 %copy-done.1 = bf16[16,1088,240]{2,1,0:T(8,128)(2,1)S(1)} copy-done((bf16[16,1088,240]{2,1,0:T(8,128)(2,1)S(1)}, bf16[16,1088,240]{2,1,0:T(8,128)(2,1)}, u32[]{:S(2)}) %copy-start.1) | copy-done | bytes 8355864
  95.9 1.2 copy-done.5
  97.1 1.2 copy-done.7
  98.3 1.2 copy-done.9
  99.5 12.3 %conv_units.5.refs_0_ = f32[1024,640]{1,0:T(8,128)S(1)} custom-call(f32[1,640]{1,0:T(1,128)S(1)} %reshape.51.refs_0_, bf16[16,1088,240]{2,1,0:T(8,128)(2,1)S(1)} %copy-done.1, bf16[3,240,640]{2,1,0:T(8,128)(2,1)S(1)} %bitcast.30, bf16[3,240,640]{2,1,0:T(8,128)(2,1)} %collective-permute-done.2.refs_3_, bf16[3,240,640]{2,1,0:T(8,128)(2,1)S(1)} %copy-done.7, ...), custom_call_target="tpu_custom_call" | custom-call | flops 3774873600 | bytes 8929280 | tf_op jit(solution)/shard_map/conv_units/pallas_call | solution.py:153
  111.9 9.2 %conv_units.6.refs_0_ = f32[1024,640]{1,0:T(8,128)S(1)} custom-call(f32[1024,640]{1,0:T(8,128)S(1)} %conv_units.5.refs_0_, bf16[16,1088,240]{2,1,0:T(8,128)(2,1)S(1)} %copy-done.1, bf16[3,240,640]{2,1,0:T(8,128)(2,1)S(1)} %collective-permute-done.5.refs_2_, bf16[3,240,640]{2,1,0:T(8,128)(2,1)} %collective-permute-done.6.refs_3_, ...), custom_call_target="tpu_custom_call", output_to_operand_aliasing={{}: (0, {})} | custom-call | flops 3774873600 | bytes 8929280 | tf_op jit(solution)/shard_map/conv_units/pallas_call | solution.py:153
  121.1 9.0 %conv_units.7.refs_0_ = f32[1024,640]{1,0:T(8,128)S(1)} custom-call(f32[1024,640]{1,0:T(8,128)S(1)} %conv_units.6.refs_0_, bf16[16,1088,240]{2,1,0:T(8,128)(2,1)S(1)} %copy-done.1, bf16[3,240,640]{2,1,0:T(8,128)(2,1)} %collective-permute-done.9.refs_2_, bf16[3,240,640]{2,1,0:T(8,128)(2,1)} %collective-permute-done.10.refs_3_, ...), custom_call_target="tpu_custom_call", output_to_operand_aliasing={{}: (0, {})} | custom-call | flops 3774873600 | bytes 8929280 | tf_op jit(solution)/shard_map/conv_units/pallas_call | solution.py:153
  130.1 5.8 %conv_units.8.refs_0_ = f32[1024,640]{1,0:T(8,128)S(1)} custom-call(f32[1024,640]{1,0:T(8,128)S(1)} %conv_units.7.refs_0_, bf16[16,1088,240]{2,1,0:T(8,128)(2,1)S(1)} %copy-done.1, bf16[3,240,640]{2,1,0:T(8,128)(2,1)} %collective-permute-done.13.refs_2_, bf16[3,240,640]{2,1,0:T(8,128)(2,1)S(1)} %collective-permute-done.14.refs_3_), custom_call_target="tpu_custom_call", output_to_operand_aliasing={{}: (0, {})} | custom-call | flops 1887436800 | bytes 7086080 | tf_op jit(solution)/shard_map/conv_units/pallas_call | solution.py:153
  135.9 6.0 %conv_units.9 = bf16[640,1024]{1,0:T(8,128)(2,1)} custom-call(f32[1024,640]{1,0:T(8,128)S(1)} %conv_units.8.refs_0_, bf16[16,1088,240]{2,1,0:T(8,128)(2,1)S(1)} %copy-done.1, bf16[3,240,640]{2,1,0:T(8,128)(2,1)} %collective-permute-done.15.refs_2_, bf16[3,240,640]{2,1,0:T(8,128)(2,1)S(1)} %collective-permute-done.16.refs_3_, bf16[640,1024]{1,0:T(8,128)(2,1)S(1)} %bitcast.27), custom_call_target="tpu_custom_call" | custom-call | flops 1887436800 | bytes 7086080 | tf_op jit(solution)/shard_map/conv_units/pallas_call | solution.py:153
  (66 shorter events, 4.7 us)
Async XLA Ops:
  0.0 18.5 %copy-start = (bf16[80,640]{1,0:T(8,128)(2,1)S(1)}, bf16[80,640]{1,0:T(8,128)(2,1)}, u32[]{:S(2)}) copy-start(bf16[80,640]{1,0:T(8,128)(2,1)} %param.13) | copy-start | bytes 307204
  0.0 46.5 %copy-start.11 = (f32[640]{0:T(1024)S(1)}, f32[640]{0:T(1024)}, u32[]{:S(2)}) copy-start(f32[640]{0:T(1024)} %param.15) | copy-start | bytes 7684
  0.0 46.5 %copy-start.10 = (f32[640]{0:T(1024)S(1)}, f32[640]{0:T(1024)}, u32[]{:S(2)}) copy-start(f32[640]{0:T(1024)} %param.16) | copy-start | bytes 7684
  0.0 71.8 %copy-start.12 = (f32[640]{0:T(1024)S(1)}, f32[640]{0:T(1024)}, u32[]{:S(2)}) copy-start(f32[640]{0:T(1024)} %param.18) | copy-start | bytes 7684
  0.0 14.7 %collective-permute-start.3 = (bf16[3,240,640]{2,1,0:T(8,128)(2,1)}, bf16[3,240,640]{2,1,0:T(8,128)(2,1)S(1)}, u32[]{:S(2)}, u32[]{:S(2)}) collective-permute-start(bf16[3,240,640]{2,1,0:T(8,128)(2,1)} %bitcast.28), channel_id=1, source_target_pairs={{0,8},{8,16},{16,24},{24,28},{28,20},{20,12},{12,4},{4,0},{2,6},{1... | collective-permute-start | bytes 2764808 | tf_op jit(solution)/shard_map/ppermute | solution.py:194
  3.1 13.7 %collective-permute-start.2 = (bf16[3,240,640]{2,1,0:T(8,128)(2,1)}, bf16[3,240,640]{2,1,0:T(8,128)(2,1)}, u32[]{:S(2)}, u32[]{:S(2)}) collective-permute-start(bf16[3,240,640]{2,1,0:T(8,128)(2,1)} %bitcast.29), channel_id=1, source_target_pairs={{0,2},{2,0},{4,6},{6,4},{8,10},{10,8},{12,14},{14,12},{16,18},{18,... | collective-permute-start | bytes 2764808 | tf_op jit(solution)/shard_map/ppermute | solution.py:190
  4.5 13.9 %all-to-all-start = ((bf16[16,1,80]{2,1,0:T(2,128)(2,1)}), bf16[16,1,80]{2,1,0:T(2,128)(2,1)S(1)}, u32[]{:S(2)}, u32[]{:S(2)}) async-start(bf16[16,1,80]{2,1,0:T(2,128)(2,1)} %all_to_all.19), calls=%async_computation | async-start | bytes 16384 | tf_op jit(solution)/shard_map/all_to_all | solution.py:203
  9.6 59.8 %collective-permute-start = (bf16[8,80,1024]{2,1,0:T(8,128)(2,1)}, bf16[8,80,1024]{2,1,0:T(8,128)(2,1)}, u32[]{:S(2)}, u32[]{:S(2)}) collective-permute-start(bf16[8,80,1024]{2,1,0:T(8,128)(2,1)} %bitcast.31), channel_id=1, source_target_pairs={{0,1},{1,0},{2,3},{3,2},{4,5},{5,4},{6,7},{7,6},{8,9},{9,8},{10,11... | collective-permute-start | bytes 3932168 | tf_op jit(solution)/shard_map/ppermute | solution.py:200
  14.7 30.2 %copy-start.6 = (bf16[3,240,640]{2,1,0:T(8,128)(2,1)}, bf16[3,240,640]{2,1,0:T(8,128)(2,1)S(1)}, u32[]{:S(2)}) copy-start(bf16[3,240,640]{2,1,0:T(8,128)(2,1)S(1)} %collective-permute-done.3.refs_4_) | copy-start | bytes 2764804
  14.7 30.2 %collective-permute-start.7 = (bf16[3,240,640]{2,1,0:T(8,128)(2,1)S(1)}, bf16[3,240,640]{2,1,0:T(8,128)(2,1)S(1)}, u32[]{:S(2)}, u32[]{:S(2)}) collective-permute-start(bf16[3,240,640]{2,1,0:T(8,128)(2,1)S(1)} %collective-permute-done.3.refs_4_), channel_id=1, source_target_pairs={{0,8},{8,16},{16,24},{24,28},{28,20},{20,12},{12,4},{4,0},{2,6},{1... | collective-permute-start | bytes 2764808 | tf_op jit(solution)/shard_map/ppermute | solution.py:194
  16.8 28.5 %collective-permute-start.5 = (bf16[3,240,640]{2,1,0:T(8,128)(2,1)}, bf16[3,240,640]{2,1,0:T(8,128)(2,1)S(1)}, u32[]{:S(2)}, u32[]{:S(2)}) collective-permute-start(bf16[3,240,640]{2,1,0:T(8,128)(2,1)} %collective-permute-done.2.refs_3_), channel_id=1, source_target_pairs={{0,8},{8,16},{16,24},{24,28},{28,20},{20,12},{12,4},{4,0},{2,6},{1... | collective-permute-start | bytes 2764808 | tf_op jit(solution)/shard_map/ppermute | solution.py:194
  19.3 22.9 %all-to-all-start.1 = ((f32[16,1,640]{2,1,0:T(1,128)}), f32[16,1,640]{2,1,0:T(1,128)S(1)}, u32[]{:S(2)}, u32[]{:S(2)}) async-start(f32[16,1,640]{2,1,0:T(1,128)} %copy.25), calls=%async_computation.1 | async-start | bytes 81920 | tf_op jit(solution)/shard_map/all_to_all | solution.py:205
  45.0 23.8 %collective-permute-start.11 = (bf16[3,240,640]{2,1,0:T(8,128)(2,1)S(1)}, bf16[3,240,640]{2,1,0:T(8,128)(2,1)S(1)}, u32[]{:S(2)}, u32[]{:S(2)}) collective-permute-start(bf16[3,240,640]{2,1,0:T(8,128)(2,1)S(1)} %collective-permute-done.7.refs_4_), channel_id=1, source_target_pairs={{0,8},{8,16},{16,24},{24,28},{28,20},{20,12},{12,4},{4,0},{2,6},{1... | collective-permute-start | bytes 2764808 | tf_op jit(solution)/shard_map/ppermute | solution.py:194
  45.3 23.1 %collective-permute-start.9 = (bf16[3,240,640]{2,1,0:T(8,128)(2,1)S(1)}, bf16[3,240,640]{2,1,0:T(8,128)(2,1)}, u32[]{:S(2)}, u32[]{:S(2)}) collective-permute-start(bf16[3,240,640]{2,1,0:T(8,128)(2,1)S(1)} %collective-permute-done.5.refs_2_), channel_id=1, source_target_pairs={{0,8},{8,16},{16,24},{24,28},{28,20},{20,12},{12,4},{4,0},{2,6},{1... | collective-permute-start | bytes 2764808 | tf_op jit(solution)/shard_map/ppermute | solution.py:194
  46.6 3.7 %collective-permute-start.1 = (f32[2,640]{1,0:T(2,128)S(1)}, f32[2,640]{1,0:T(2,128)S(1)}, u32[]{:S(2)}, u32[]{:S(2)}) collective-permute-start(f32[2,640]{1,0:T(2,128)S(1)} %get-tuple-element.12), channel_id=1, source_target_pairs={{0,1},{1,0},{2,3},{3,2},{4,5},{5,4},{6,7},{7,6},{8,9},{9,8},{10,11... | collective-permute-start | bytes 15368 | tf_op jit(solution)/shard_map/ppermute | solution.py:218
  48.2 21.2 %collective-permute-start.4 = (bf16[3,240,640]{2,1,0:T(8,128)(2,1)}, bf16[3,240,640]{2,1,0:T(8,128)(2,1)S(1)}, u32[]{:S(2)}, u32[]{:S(2)}) collective-permute-start(bf16[3,240,640]{2,1,0:T(8,128)(2,1)} %copy-done.6), channel_id=1, source_target_pairs={{0,2},{2,0},{4,6},{6,4},{8,10},{10,8},{12,14},{14,12},{16,18},{18,... | collective-permute-start | bytes 2764808 | tf_op jit(solution)/shard_map/ppermute | solution.py:196
  50.3 20.5 %collective-permute-start.8 = (bf16[3,240,640]{2,1,0:T(8,128)(2,1)S(1)}, bf16[3,240,640]{2,1,0:T(8,128)(2,1)S(1)}, u32[]{:S(2)}, u32[]{:S(2)}) collective-permute-start(bf16[3,240,640]{2,1,0:T(8,128)(2,1)S(1)} %collective-permute-done.7.refs_4_), channel_id=1, source_target_pairs={{0,2},{2,0},{4,6},{6,4},{8,10},{10,8},{12,14},{14,12},{16,18},{18,... | collective-permute-start | bytes 2764808 | tf_op jit(solution)/shard_map/ppermute | solution.py:196
  68.4 23.4 %collective-permute-start.13 = (bf16[3,240,640]{2,1,0:T(8,128)(2,1)}, bf16[3,240,640]{2,1,0:T(8,128)(2,1)}, u32[]{:S(2)}, u32[]{:S(2)}) collective-permute-start(bf16[3,240,640]{2,1,0:T(8,128)(2,1)} %collective-permute-done.9.refs_2_), channel_id=1, source_target_pairs={{0,8},{8,16},{16,24},{24,28},{28,20},{20,12},{12,4},{4,0},{2,6},{1... | collective-permute-start | bytes 2764808 | tf_op jit(solution)/shard_map/ppermute | solution.py:194
  68.7 23.6 %collective-permute-start.15 = (bf16[3,240,640]{2,1,0:T(8,128)(2,1)S(1)}, bf16[3,240,640]{2,1,0:T(8,128)(2,1)}, u32[]{:S(2)}, u32[]{:S(2)}) collective-permute-start(bf16[3,240,640]{2,1,0:T(8,128)(2,1)S(1)} %collective-permute-done.11.refs_4_), channel_id=1, source_target_pairs={{0,8},{8,16},{16,24},{24,28},{28,20},{20,12},{12,4},{4,0},{2,6},{1... | collective-permute-start | bytes 2764808 | tf_op jit(solution)/shard_map/ppermute | solution.py:194
  69.3 42.5 %collective-permute-start.6 = (bf16[3,240,640]{2,1,0:T(8,128)(2,1)S(1)}, bf16[3,240,640]{2,1,0:T(8,128)(2,1)}, u32[]{:S(2)}, u32[]{:S(2)}) collective-permute-start(bf16[3,240,640]{2,1,0:T(8,128)(2,1)S(1)} %collective-permute-done.5.refs_2_), channel_id=1, source_target_pairs={{0,2},{2,0},{4,6},{6,4},{8,10},{10,8},{12,14},{14,12},{16,18},{18,... | collective-permute-start | bytes 2764808 | tf_op jit(solution)/shard_map/ppermute | solution.py:196
  69.4 0.9 copy-start.8
  70.3 50.8 %collective-permute-start.12 = (bf16[3,240,640]{2,1,0:T(8,128)(2,1)S(1)}, bf16[3,240,640]{2,1,0:T(8,128)(2,1)}, u32[]{:S(2)}, u32[]{:S(2)}) collective-permute-start(bf16[3,240,640]{2,1,0:T(8,128)(2,1)S(1)} %collective-permute-done.11.refs_4_), channel_id=1, source_target_pairs={{0,2},{2,0},{4,6},{6,4},{8,10},{10,8},{12,14},{14,12},{16,18},{18,... | collective-permute-start | bytes 2764808 | tf_op jit(solution)/shard_map/ppermute | solution.py:196
  70.8 1.0 copy-start.3
  71.8 49.3 %collective-permute-start.10 = (bf16[3,240,640]{2,1,0:T(8,128)(2,1)}, bf16[3,240,640]{2,1,0:T(8,128)(2,1)}, u32[]{:S(2)}, u32[]{:S(2)}) collective-permute-start(bf16[3,240,640]{2,1,0:T(8,128)(2,1)} %collective-permute-done.9.refs_2_), channel_id=1, source_target_pairs={{0,2},{2,0},{4,6},{6,4},{8,10},{10,8},{12,14},{14,12},{16,18},{18,... | collective-permute-start | bytes 2764808 | tf_op jit(solution)/shard_map/ppermute | solution.py:196
  91.9 38.2 %collective-permute-start.14 = (bf16[3,240,640]{2,1,0:T(8,128)(2,1)}, bf16[3,240,640]{2,1,0:T(8,128)(2,1)S(1)}, u32[]{:S(2)}, u32[]{:S(2)}) collective-permute-start(bf16[3,240,640]{2,1,0:T(8,128)(2,1)} %collective-permute-done.13.refs_2_), channel_id=1, source_target_pairs={{0,2},{2,0},{4,6},{6,4},{8,10},{10,8},{12,14},{14,12},{16,18},{18,... | collective-permute-start | bytes 2764808 | tf_op jit(solution)/shard_map/ppermute | solution.py:196
  92.3 43.5 %collective-permute-start.16 = (bf16[3,240,640]{2,1,0:T(8,128)(2,1)}, bf16[3,240,640]{2,1,0:T(8,128)(2,1)S(1)}, u32[]{:S(2)}, u32[]{:S(2)}) collective-permute-start(bf16[3,240,640]{2,1,0:T(8,128)(2,1)} %collective-permute-done.15.refs_2_), channel_id=1, source_target_pairs={{0,2},{2,0},{4,6},{6,4},{8,10},{10,8},{12,14},{14,12},{16,18},{18,... | collective-permute-start | bytes 2764808 | tf_op jit(solution)/shard_map/ppermute | solution.py:196
  92.4 3.5 %copy-start.1 = (bf16[16,1088,240]{2,1,0:T(8,128)(2,1)S(1)}, bf16[16,1088,240]{2,1,0:T(8,128)(2,1)}, u32[]{:S(2)}) copy-start(bf16[16,1088,240]{2,1,0:T(8,128)(2,1)} %norm_windows.3.refs_1_) | copy-start | bytes 25067524
  95.9 1.2 copy-start.5
  97.1 1.2 copy-start.7
  98.3 1.2 copy-start.9
  99.5 12.4 %copy-start.4 = (bf16[3,240,640]{2,1,0:T(8,128)(2,1)S(1)}, bf16[3,240,640]{2,1,0:T(8,128)(2,1)}, u32[]{:S(2)}) copy-start(bf16[3,240,640]{2,1,0:T(8,128)(2,1)} %copy-done.3) | copy-start | bytes 2764804
  130.1 5.8 %copy-start.2 = (bf16[1,640,1024]{2,1,0:T(8,128)(2,1)S(1)}, bf16[1,640,1024]{2,1,0:T(8,128)(2,1)}, u32[]{:S(2)}) copy-start(bf16[1,640,1024]{2,1,0:T(8,128)(2,1)} %param.11) | copy-start | bytes 3932164

commit v2 on v0

v2 whole, which is shorter than its diff:
```python
import functools

import jax
import jax.numpy as jnp
import numpy as np
from jax import lax
from jax.experimental import pallas as pl
from jax.experimental.pallas import tpu as pltpu
from jax.sharding import PartitionSpec as P

C = 1280
GROUPS = 32
HEIGHT = 32
WIDTH = 32
CELLS = HEIGHT * WIDTH
VMEM_BYTES = 28 * 2**20
ANY = pl.BlockSpec(memory_space=pl.ANY)
HBM = pl.BlockSpec(memory_space=pltpu.HBM)
WHOLE = pl.BlockSpec(memory_space=pltpu.VMEM)


def chip_order(chips):
    if chips % 2:
        return list(range(chips))
    half = chips // 2
    return [2 * z for z in range(half)] + [2 * z + 1 for z in reversed(range(half))]


class Ring:
    def __init__(self, dp):
        self.dp = dp
        n = dp // 2
        order = chip_order(n)
        self.core_pairs = [(i, i ^ 1) for i in range(dp)]
        self.pairs = [(2 * order[k], 2 * order[(k + 1) % n]) for k in range(n)]
        self.pairs += [(2 * order[k] + 1, 2 * order[(k - 1) % n] + 1) for k in range(n)]
        full = (n - 1) // 2
        self.hops = [(s, h) for s in range(1, full + 1) for h in range(2)]
        if n % 2 == 0:
            self.hops.append((full + 1, 0))
        self.blocks = np.zeros((dp, dp), np.int32)
        for k in range(n):
            for core in range(2):
                me = 2 * order[k] + core
                units = [me, me ^ 1]
                for s, h in self.hops:
                    for c in (core, 1 - core):
                        chip = order[(k - s) % n] if c == 0 else order[(k + s) % n]
                        units.append(2 * chip + (c if h == 0 else 1 - c))
                self.blocks[me] = units


def act_kernel(emb_ref, piece_ref, out_ref, passed_ref):
    del piece_ref, passed_ref
    v = emb_ref[...].astype(jnp.float32)
    act = (v / (1.0 + jnp.exp(-v))).astype(jnp.bfloat16)
    rows = out_ref.shape[2]
    for d in range(out_ref.shape[0]):
        out_ref[d] = act[:, d * rows : (d + 1) * rows]


def act_call(emb, count, piece):
    return pl.pallas_call(
        act_kernel,
        out_shape=(
            jax.ShapeDtypeStruct((count, 1, emb.shape[1] // count), jnp.bfloat16),
            jax.ShapeDtypeStruct(piece.shape, piece.dtype),
        ),
        in_specs=[WHOLE, ANY],
        out_specs=(WHOLE, ANY),
        input_output_aliases={1: 1},
        compiler_params=pltpu.CompilerParams(vmem_limit_bytes=VMEM_BYTES),
        name="act_rows",
    )(emb, piece)


def emb_kernel(act_ref, w_ref, piece_ref, out_ref, passed_ref):
    del piece_ref, passed_ref
    out_ref[:, 0, :] = jnp.dot(act_ref[:, 0, :], w_ref[...], preferred_element_type=jnp.float32)


def emb_call(act_rows, w_emb, piece):
    shape = (act_rows.shape[0], 1, w_emb.shape[1])
    return pl.pallas_call(
        emb_kernel,
        out_shape=(jax.ShapeDtypeStruct(shape, jnp.float32), jax.ShapeDtypeStruct(piece.shape, piece.dtype)),
        in_specs=[WHOLE, WHOLE, ANY],
        out_specs=(WHOLE, ANY),
        input_output_aliases={2: 1},
        compiler_params=pltpu.CompilerParams(vmem_limit_bytes=VMEM_BYTES),
        name="emb_terms",
    )(act_rows, w_emb, piece)


def stats_kernel(h_ref, *refs):
    out_ref = refs[-1]
    panel = h_ref.shape[0]
    step = 80 if panel % 80 == 0 else panel
    count = len(refs) - 1
    for i in range(count):
        out_ref[i : i + 1, :] = refs[i][...]
    means, variances = [], []
    for start in range(0, panel, step):
        values = h_ref[start : start + step, :].astype(jnp.float32)
        mean = jnp.mean(values, axis=1, keepdims=True)
        means.append(mean)
        variances.append(jnp.mean((values - mean) ** 2, axis=1, keepdims=True))
    for i, columns in ((count, means), (count + 1, variances)):
        column = jnp.concatenate(columns, axis=0)
        out_ref[i : i + 1, :] = jnp.broadcast_to(column, (panel, 128)).T[0:1, :]


def stats_call(h, rows):
    shape = jax.ShapeDtypeStruct((len(rows) + 2, h.shape[0]), jnp.float32)
    return pl.pallas_call(
        stats_kernel,
        out_shape=shape,
        in_specs=[WHOLE] * (1 + len(rows)),
        out_specs=WHOLE,
        compiler_params=pltpu.CompilerParams(vmem_limit_bytes=VMEM_BYTES),
        cost_estimate=pl.CostEstimate(flops=5 * h.size, transcendentals=0, bytes_accessed=2 * h.size),
        name="channel_stats",
    )(h, *[row.reshape(1, -1) for row in rows])


def affine_kernel(size, terms_ref, table_ref, out_ref):
    rows = out_ref.shape[2]
    b_emb, gain, bias, channel_mean, channel_var = (table_ref[i : i + 1, :] for i in range(5))
    shift = jnp.sum(terms_ref[...], axis=0) + b_emb
    width = shift.shape[1]
    group = lax.broadcasted_iota(jnp.int32, (width, width // size), 0) // size
    member = (group == lax.broadcasted_iota(jnp.int32, group.shape, 1)).astype(jnp.float32)

    def per_group(row):
        row = jnp.broadcast_to(row, (8, row.shape[1]))
        return jnp.dot(row, member, precision=lax.Precision.HIGHEST, preferred_element_type=jnp.float32) / size

    def per_channel(groups):
        back = (((1,), (1,)), ((), ()))
        spread = lax.dot_general(
            groups, member, back, precision=lax.Precision.HIGHEST, preferred_element_type=jnp.float32
        )
        return spread[0:1, :]

    center = channel_mean + shift
    mean = per_channel(per_group(center))
    var = per_group(channel_var + (center - mean) ** 2)
    scale = per_channel(lax.rsqrt(var + 1e-05)) * gain
    offset = (shift - mean) * scale + bias
    both = jnp.concatenate([scale, offset], axis=0)
    for d in range(out_ref.shape[0]):
        out_ref[d] = both[:, d * rows : (d + 1) * rows]


def affine_call(size, rows, terms, table):
    channels = terms.shape[2]
    return pl.pallas_call(
        functools.partial(affine_kernel, size),
        out_shape=jax.ShapeDtypeStruct((channels // rows, 2, rows), jnp.float32),
        in_specs=[WHOLE, WHOLE],
        out_specs=WHOLE,
        compiler_params=pltpu.CompilerParams(vmem_limit_bytes=VMEM_BYTES),
        name="affine",
    )(terms, table)


def shifted(values, amount):
    edge = jnp.zeros((values.shape[0], abs(amount)), values.dtype)
    if amount > 0:
        return jnp.concatenate([values[:, amount:], edge], axis=1)
    return jnp.concatenate([edge, values[:, :amount]], axis=1)


def conv_kernel(ids, turns, tile, first, last, passing, *refs):
    refs = list(refs)
    count = len(ids)
    place_ref = refs.pop(0)
    base_ref = refs.pop(0)
    bias_ref = refs.pop(0) if first else None
    h_refs = [refs.pop(0) for _ in range(turns)]
    ab_ref = refs.pop(0)
    weight_refs = [refs.pop(0) for _ in range(count - (passing == 2))]
    if passing == 2:
        weight_refs.append(refs[0])
    passing = min(passing, 1)
    del refs[:passing]
    out_ref = refs.pop(0)
    del refs[:passing]
    hs, ws, base, total, even, odd, h_sem, w_sem, in_sem, out_sem = refs[:10]
    stacks = (even, odd)
    result = refs[10] if last else total
    blocks, rows, _ = h_refs[0].shape
    outs = total.shape[0]
    tiles = outs // tile
    cuts = [pl.ds(t * tile, tile) for t in range(tiles)]
    w_copies = [pltpu.make_async_copy(weight_refs[u], ws.at[u], w_sem.at[u]) for u in range(count)]
    in_copies = [pltpu.make_async_copy(base_ref.at[c], base.at[c], in_sem.at[t]) for t, c in enumerate(cuts)]
    out_copies = [pltpu.make_async_copy(result.at[c], out_ref.at[c], out_sem.at[t]) for t, c in enumerate(cuts)]
    for u in range(count):
        place = place_ref[ids[u]]
        for turn in range(turns):

            @pl.when(place // blocks == turn)
            def _():
                pltpu.make_async_copy(h_refs[turn].at[place % blocks], hs.at[u], h_sem.at[u]).start()

    for copy in w_copies + in_copies:
        copy.start()
    column = lax.broadcasted_iota(jnp.int32, (1, CELLS), 1) % WIDTH
    inside = [(column > 0).astype(jnp.bfloat16), None, (column < WIDTH - 1).astype(jnp.bfloat16)]

    def build(u):
        ab = ab_ref[place_ref[ids[u]]].T
        v = hs[u].astype(jnp.float32) * ab[:, 0:1] + ab[:, 1:2]
        half = 0.5 * v
        normed = (half + half * jnp.tanh(half)).astype(jnp.bfloat16)
        for dx in range(3):
            moved = normed if dx == 1 else shifted(normed, dx - 1) * inside[dx]
            for dy in range(3):
                row = (3 * dy + dx) * rows
                stacks[u % 2][row : row + rows, :] = moved if dy == 1 else shifted(moved, WIDTH * (dy - 1))

    def product(u, here):
        weights = ws[u, :, :, here].reshape(9 * rows, here.stop - here.start)
        return lax.dot_general(
            weights, stacks[u % 2][...], (((0,), (0,)), ((), ())), preferred_element_type=jnp.float32
        )

    for u in range(count):
        pltpu.make_async_copy(h_refs[0].at[0], hs.at[u], h_sem.at[u]).wait()
    build(0)
    for copy in w_copies:
        copy.wait()
    for u in range(count - 1):
        build(u + 1)
        part = product(u, slice(0, outs))
        total[...] = part if u == 0 else part + total[...]
    for copy in in_copies:
        copy.wait()
    for t in range(tiles):
        here = slice(t * tile, (t + 1) * tile)
        part = product(count - 1, here) + base[here, :].astype(jnp.float32)
        if count > 1:
            part = part + total[here, :]
        if first:
            part = part + jnp.broadcast_to(bias_ref[:, here], (8, tile)).T[:, 0:1]
        result[here, :] = part.astype(result.dtype)
        out_copies[t].start()
    for copy in out_copies:
        copy.wait()


def conv_call(places, ids, base, bias, slices, affine, weights, last=False, passed=None):
    count, turns = len(ids), len(slices)
    rows = slices[0].shape[1]
    outs = weights[0].shape[2]
    first = bias is not None
    tile = 128 if outs % 128 == 0 else outs
    tiles = outs // tile
    out_shape = [jax.ShapeDtypeStruct((outs, CELLS), jnp.bfloat16 if last else jnp.float32)]
    operands = [places, base] + ([bias] if first else []) + list(slices) + [affine] + list(weights)
    specs = [pl.BlockSpec(memory_space=pltpu.SMEM), HBM] + [WHOLE] * first + [HBM] + [ANY] * (turns - 1) + [WHOLE]
    specs += [HBM if id == 0 else ANY for id in ids[: len(weights)]]
    aliases = {} if first or last else {1: 0}
    passing = 0
    if passed is not None:
        passing = 1 if len(weights) == count else 2
        aliases[len(operands)] = 1
        operands.append(passed)
        specs.append(ANY)
        out_shape.append(jax.ShapeDtypeStruct(passed.shape, passed.dtype))
    scratch = [
        pltpu.VMEM((count, rows, CELLS), jnp.bfloat16),
        pltpu.VMEM((count,) + weights[0].shape, jnp.bfloat16),
        pltpu.VMEM((outs, CELLS), base.dtype),
        pltpu.VMEM((outs, CELLS), jnp.float32),
        pltpu.VMEM((9 * rows, CELLS), jnp.bfloat16),
        pltpu.VMEM((9 * rows, CELLS), jnp.bfloat16),
        pltpu.SemaphoreType.DMA((count,)),
        pltpu.SemaphoreType.DMA((count,)),
        pltpu.SemaphoreType.DMA((tiles,)),
        pltpu.SemaphoreType.DMA((tiles,)),
    ]
    if last:
        scratch.append(pltpu.VMEM((outs, CELLS), jnp.bfloat16))
    return pl.pallas_call(
        functools.partial(conv_kernel, tuple(ids), turns, tile, first, last, passing),
        out_shape=out_shape,
        in_specs=specs,
        out_specs=[HBM] + [ANY] * (passed is not None),
        scratch_shapes=scratch,
        input_output_aliases=aliases,
        compiler_params=pltpu.CompilerParams(vmem_limit_bytes=VMEM_BYTES),
        cost_estimate=pl.CostEstimate(
            flops=2 * CELLS * 9 * rows * outs * count,
            transcendentals=count * rows * CELLS,
            bytes_accessed=2 * count * 9 * rows * outs + 8 * CELLS * outs,
        ),
        name="conv_units",
    )(*operands)


def make_body(dp, chan):
    ring = Ring(dp)
    chan_pairs = [(i, (i + 1) % chan) for i in range(chan)]

    def around(value):
        values = [value]
        for _ in range(chan - 1):
            values.append(lax.ppermute(values[-1], "chan", chan_pairs))
        return values

    def body(h_in, skip, emb, w_emb, b_emb, gn_gain, gn_bias, w_conv, b_conv):
        panel = h_in.shape[1]
        rows, outs = w_conv.shape[1], w_conv.shape[2]
        blocks = panel // rows
        me = lax.axis_index("dp")
        side = lax.axis_index("chan")

        own = w_conv.reshape(3, 3 * rows, outs)
        final = len(ring.hops) + 1
        pieces = {0: own, 1: lax.ppermute(own, "dp", ring.core_pairs)}
        pieces[2] = lax.ppermute(own, "dp", ring.pairs)

        table = stats_call(h_in[0], [b_emb, gn_gain, gn_bias])
        slices = around(h_in.reshape(blocks, rows, CELLS))

        act, pieces[1] = act_call(emb, dp, pieces[1])
        act_rows = lax.all_to_all(act, "dp", 0, 0, tiled=True)
        terms, pieces[2] = emb_call(act_rows, w_emb, pieces[2])
        terms = lax.all_to_all(terms, "dp", 0, 0, tiled=True)
        affine = jnp.concatenate(around(affine_call(C // GROUPS, rows, terms, table)), axis=0)

        block = lax.dynamic_slice(jnp.asarray(ring.blocks), (me, 0), (1, dp))[0]
        places = ((side - block // blocks) % chan) * blocks + block % blocks

        state = {"total": skip[0], "bias": b_conv.reshape(1, outs), "left": dp}
        units = [(0, own), (1, pieces[1])]

        def convolve(count, passed=None):
            here = [units.pop(0) for _ in range(min(count, len(units)))]
            ids, weights = [u for u, _ in here], [w for _, w in here]
            if passed is not None and len(ids) < count - 1:
                ids.append(passed[0])
            state["left"] -= len(ids)
            results = conv_call(
                places,
                ids,
                state["total"],
                state["bias"],
                slices,
                affine,
                weights,
                state["left"] == 0,
                None if passed is None else passed[1],
            )
            state.update(total=results[0], bias=None)
            return results[-1], len(ids) > len(weights)

        for i in range(2, final + 1):
            if i > 2:
                pieces[i] = lax.ppermute(pieces[i - 2], "dp", ring.pairs)
            done = False
            if 4 <= i <= final - 2:
                pieces[i], done = convolve(4, (2 * i - 2, pieces[i]))
            if i == final:
                while units:
                    convolve(4)
            if not done:
                units.append((2 * i - 2, pieces[i]))
            units.append((2 * i - 1, lax.ppermute(pieces[i], "dp", ring.core_pairs)))
        while units:
            convolve(4)
        return state["total"][None]

    return body


def solution(mesh):
    return jax.shard_map(
        make_body(mesh.shape["dp"], mesh.shape["chan"]),
        mesh=mesh,
        in_specs=(
            P("dp", "chan", None),
            P("dp", "chan", None),
            P("dp", None),
            P("dp", "chan"),
            P("chan"),
            P("chan"),
            P("chan"),
            P(None, "dp", "chan"),
            P("chan"),
        ),
        out_specs=P("dp", "chan", None),
        check_vma=False,
    )
```

time: 252 us -> 110 us (0.44)
  waiting for transfers between devices: 181 us -> 29.6 us
  Pallas kernels: 0 us -> 42.7 us
  matrix products: 32 us -> 0 us
  starting transfers between devices: 0.08 us -> 24 us
  between operations: 13.4 us -> 0.34 us
  local copies, waits for them, and re-layouts: 22.3 us -> 11.5 us
    all_gather x3 -> x0, waiting for transfers between devices: 179 us -> none  [the longest x1 100 us: body(): weight_full = lax.all_gather(w_conv, 'dp', axis=1, tiled=True)]
    pallas_call x0 -> x9, Pallas kernels: none -> 42.7 us  [the longest x5 38.7 us: conv_call(): pl.pallas_call(functools.partial(conv_kernel, tuple(ids), turns, tile, fi...]
    dot_general x10 -> x0, matrix products: 32 us -> none  [the longest x9 30.3 us: add_taps(): jnp.einsum('bip,io->bop', window, weights[3 * row_off + col_off], preferr...]
    slice x1 -> x0, local copies, waits for them, and re-layouts: 16.2 us -> none  [add_taps(): padded[:, :, row_off:row_off + HEIGHT, col_off:col_off + WIDTH]]
    all_to_all x0 -> x2, waiting for transfers between devices: none -> 15.2 us  [the longest x1 10.9 us: body(): terms = lax.all_to_all(terms, 'dp', 0, 0, tiled=True)]
    ppermute x0 -> x17, waiting for transfers between devices: none -> 14.4 us  [the longest x6 12.2 us: body(): pieces[i] = lax.ppermute(pieces[i - 2], 'dp', ring.pairs)]
    ppermute x0 -> x17, starting transfers between devices: none -> 14.3 us  [the longest x6 7.66 us: body(): pieces[i] = lax.ppermute(pieces[i - 2], 'dp', ring.pairs)]
    all_to_all x0 -> x2, starting transfers between devices: none -> 9.65 us  [the longest x1 5.51 us: body(): act_rows = lax.all_to_all(act, 'dp', 0, 0, tiled=True)]
  transfers between devices with their start and end apart: 3 -> 19, of which waited for: 3 -> 9; matrix products, arithmetic and copies ran while one was open for 8% -> 3% of each run, Pallas kernels for 0% -> 34%
where the time goes in v2:
time: 110 us; the launch traced here: 109 us
  Pallas kernels  42.7 us (39%)
  waiting for transfers between devices  29.6 us (27%)
  starting transfers between devices  24 us (22%)
  local copies, waits for them, and re-layouts  11.5 us (10%)
    pallas_call x5, Pallas kernels, conv_call(): pl.pallas_call(functools.partial(conv_kernel, tuple(ids), turns, tile, fi...  38.7 us
    ppermute x6, waiting for transfers between devices, body(): pieces[i] = lax.ppermute(pieces[i - 2], 'dp', ring.pairs)  12.2 us
    all_to_all x1, waiting for transfers between devices, body(): terms = lax.all_to_all(terms, 'dp', 0, 0, tiled=True)  10.9 us
    unnamed x22, local copies, waits for them, and re-layouts  8.72 us
    ppermute x6, starting transfers between devices, body(): pieces[i] = lax.ppermute(pieces[i - 2], 'dp', ring.pairs)  7.66 us
    all_to_all x1, starting transfers between devices, body(): act_rows = lax.all_to_all(act, 'dp', 0, 0, tiled=True)  5.51 us
    all_to_all x1, waiting for transfers between devices, body(): act_rows = lax.all_to_all(act, 'dp', 0, 0, tiled=True)  4.33 us
    all_to_all x1, starting transfers between devices, body(): terms = lax.all_to_all(terms, 'dp', 0, 0, tiled=True)  4.14 us
  transfers between devices with their start and end apart: 19, of which 9 were waited for; matrix products, arithmetic and copies ran while one was open for 3% of the time, Pallas kernels for 34%

profile of v2, /device:TPU:0, one launch (start us, length us, event | category | flops | bytes accessed | tf_op | source)
XLA Modules:
  0.0 108.7 jit_solution(10713204053310840396)
XLA Ops:
  0.5 2.6 %collective-permute-start.2 = (bf16[3,240,640]{2,1,0:T(8,128)(2,1)}, bf16[3,240,640]{2,1,0:T(8,128)(2,1)S(1)}, u32[]{:S(2)}, u32[]{:S(2)}) collective-permute-start(bf16[3,240,640]{2,1,0:T(8,128)(2,1)} %bitcast.27), channel_id=1, source_target_pairs={{0,8},{8,16},{16,24},{24,28},{28,20},{20,12},{12,4},{4,0},{2,6},{1... | collective-permute-start | bytes 2764808 | tf_op jit(solution)/shard_map/ppermute | solution.py:323
  3.1 1.5 %collective-permute-start = (bf16[8,80,1024]{2,1,0:T(8,128)(2,1)}, bf16[8,80,1024]{2,1,0:T(8,128)(2,1)S(1)}, u32[]{:S(2)}, u32[]{:S(2)}) collective-permute-start(bf16[8,80,1024]{2,1,0:T(8,128)(2,1)} %bitcast.18), channel_id=1, source_target_pairs={{0,1},{1,0},{2,3},{3,2},{4,5},{5,4},{6,7},{7,6},{8,9},{9,8},{10,11... | collective-permute-start | bytes 3932168 | tf_op jit(solution)/shard_map/ppermute | solution.py:310
  4.6 0.7 copy-done.8
  5.4 0.9 copy-done.1
  6.9 5.5 %all-to-all-start = ((bf16[16,1,80]{2,1,0:T(2,128)(2,1)}), bf16[16,1,80]{2,1,0:T(2,128)(2,1)S(1)}, u32[]{:S(2)}, u32[]{:S(2)}) async-start(bf16[16,1,80]{2,1,0:T(2,128)(2,1)} %copy-done.7), calls=%async_computation | async-start | bytes 16384 | tf_op jit(solution)/shard_map/all_to_all | solution.py:329
  12.4 1.9 %collective-permute-start.6 = (bf16[3,240,640]{2,1,0:T(8,128)(2,1)}, bf16[3,240,640]{2,1,0:T(8,128)(2,1)}, u32[]{:S(2)}, u32[]{:S(2)}) collective-permute-start(bf16[3,240,640]{2,1,0:T(8,128)(2,1)} %copy-done.1), channel_id=1, source_target_pairs={{0,8},{8,16},{16,24},{24,28},{28,20},{20,12},{12,4},{4,0},{2,6},{1... | collective-permute-start | bytes 2764808 | tf_op jit(solution)/shard_map/ppermute | solution.py:362
  14.7 4.3 %all-to-all-done.act_ref = bf16[16,1,80]{2,1,0:T(2,128)(2,1)S(1)} async-done(((bf16[16,1,80]{2,1,0:T(2,128)(2,1)}), bf16[16,1,80]{2,1,0:T(2,128)(2,1)S(1)}, u32[]{:S(2)}, u32[]{:S(2)}) %all-to-all-start) | async-done | bytes 2592 | tf_op jit(solution)/shard_map/all_to_all | solution.py:329
  19.0 0.9 copy-done.3
  21.0 4.1 %all-to-all-start.1 = ((f32[16,1,640]{2,1,0:T(1,128)}), f32[16,1,640]{2,1,0:T(1,128)}, u32[]{:S(2)}, u32[]{:S(2)}) async-start(f32[16,1,640]{2,1,0:T(1,128)} %copy-done.6), calls=%async_computation.1 | async-start | bytes 81920 | tf_op jit(solution)/shard_map/all_to_all | solution.py:331
  25.1 0.7 reshape.21.refs_0_
  27.2 1.2 %channel_stats.1.table_ref = f32[5,640]{1,0:T(8,128)S(1)} custom-call(bf16[640,1024]{1,0:T(8,128)(2,1)S(1)} %bitcast.19, f32[1,640]{1,0:T(1,128)S(1)} %reshape.21.refs_0_, f32[1,640]{1,0:T(1,128)S(1)} %reshape.22.refs_1_, f32[1,640]{1,0:T(1,128)S(1)} %reshape.23.refs_2_), custom_call_target="tpu_custom_call" | custom-call | flops 3276800 | bytes 1310720 | tf_op jit(solution)/shard_map/channel_stats/pallas_call | solution.py:115
  29.0 10.9 %all-to-all-done.1.terms_ref = f32[16,1,640]{2,1,0:T(1,128)} async-done(((f32[16,1,640]{2,1,0:T(1,128)}), f32[16,1,640]{2,1,0:T(1,128)}, u32[]{:S(2)}, u32[]{:S(2)}) %all-to-all-start.1) | async-done | bytes 40992 | tf_op jit(solution)/shard_map/all_to_all | solution.py:331
  39.9 0.7 copy-done.5
  40.6 2.6 %affine.1 = f32[8,2,80]{2,1,0:T(2,128)S(1)} custom-call(f32[16,1,640]{2,1,0:T(1,128)} %all-to-all-done.1.terms_ref, f32[5,640]{1,0:T(8,128)S(1)} %copy-done.5), custom_call_target="tpu_custom_call" | custom-call | tf_op jit(solution)/shard_map/affine/pallas_call | solution.py:157
  43.2 1.5 %collective-permute-start.3 = (f32[8,2,80]{2,1,0:T(2,128)S(1)}, f32[8,2,80]{2,1,0:T(2,128)S(1)}, u32[]{:S(2)}, u32[]{:S(2)}) collective-permute-start(f32[8,2,80]{2,1,0:T(2,128)S(1)} %affine.1), channel_id=1, source_target_pairs={{0,1},{1,0},{2,3},{3,2},{4,5},{5,4},{6,7},{7,6},{8,9},{9,8},{10,11... | collective-permute-start | bytes 15368 | tf_op jit(solution)/shard_map/ppermute | solution.py:310
  44.7 0.7 fusion.refs_0_
  45.4 0.7 reshape.18.refs_2_
  46.1 0.8 collective-permute-done.3
  47.3 1.2 %copy-done.2 = bf16[3,240,640]{2,1,0:T(8,128)(2,1)S(1)} copy-done((bf16[3,240,640]{2,1,0:T(8,128)(2,1)S(1)}, bf16[3,240,640]{2,1,0:T(8,128)(2,1)}, u32[]{:S(2)}) %copy-start.2) | copy-done | bytes 921624
  48.5 1.3 %copy-done.9 = bf16[1,640,1024]{2,1,0:T(8,128)(2,1)S(1)} copy-done((bf16[1,640,1024]{2,1,0:T(8,128)(2,1)S(1)}, bf16[1,640,1024]{2,1,0:T(8,128)(2,1)}, u32[]{:S(2)}) %copy-start.9) | copy-done | bytes 1310744
  49.8 1.2 %copy-done.10 = bf16[9,80,640]{2,1,0:T(8,128)(2,1)S(1)} copy-done((bf16[9,80,640]{2,1,0:T(8,128)(2,1)S(1)}, bf16[9,80,640]{2,1,0:T(8,128)(2,1)}, u32[]{:S(2)}) %copy-start.10) | copy-done | bytes 921624
  51.0 9.3 %conv_units.5 = (f32[640,1024]{1,0:T(8,128)S(1)}, bf16[3,240,640]{2,1,0:T(8,128)(2,1)}) custom-call(s32[16]{0:T(128)S(1)} %fusion.refs_0_, bf16[640,1024]{1,0:T(8,128)(2,1)S(1)} %bitcast.25, f32[1,640]{1,0:T(1,128)S(1)} %reshape.18.refs_2_, bf16[8,80,1024]{2,1,0:T(8,128)(2,1)S(1)} %bitcast.20, ...), custom_call_target="tpu_custom_call", output_to_operand_aliasing={{1}: (10, {})} | custom-call | flops 3774873600 | bytes 8929280 | tf_op jit(solution)/shard_map/conv_units/pallas_call | solution.py:286
  60.4 1.7 %collective-permute-start.11 = (bf16[3,240,640]{2,1,0:T(8,128)(2,1)}, bf16[3,240,640]{2,1,0:T(8,128)(2,1)S(1)}, u32[]{:S(2)}, u32[]{:S(2)}) collective-permute-start(bf16[3,240,640]{2,1,0:T(8,128)(2,1)} %get-tuple-element.20.refs_7_), channel_id=1, source_target_pairs={{0,8},{8,16},{16,24},{24,28},{28,20},{20,12},{12,4},{4,0},{2,6},{1... | collective-permute-start | bytes 2764808 | tf_op jit(solution)/shard_map/ppermute | solution.py:362
  62.2 0.8 collective-permute-done.8.refs_8_
  63.0 8.9 %conv_units.6 = (f32[640,1024]{1,0:T(8,128)S(1)}, bf16[3,240,640]{2,1,0:T(8,128)(2,1)S(1)}) custom-call(s32[16]{0:T(128)S(1)} %fusion.refs_0_, f32[640,1024]{1,0:T(8,128)S(1)} %get-tuple-element.19.refs_1_, bf16[8,80,1024]{2,1,0:T(8,128)(2,1)S(1)} %bitcast.21, ...), custom_call_target="tpu_custom_call", output_to_operand_aliasing={{0}: (1, {}), {1}: (9, {})} | custom-call | flops 3774873600 | bytes 8929280 | tf_op jit(solution)/shard_map/conv_units/pallas_call | solution.py:286
  72.1 1.7 %collective-permute-start.13 = (bf16[3,240,640]{2,1,0:T(8,128)(2,1)S(1)}, bf16[3,240,640]{2,1,0:T(8,128)(2,1)S(1)}, u32[]{:S(2)}, u32[]{:S(2)}) collective-permute-start(bf16[3,240,640]{2,1,0:T(8,128)(2,1)S(1)} %get-tuple-element.22.refs_5_), channel_id=1, source_target_pairs={{0,8},{8,16},{16,24},{24,28},{28,20},{20,12},{12,4},{4,0},{2,6},{1... | collective-permute-start | bytes 2764808 | tf_op jit(solution)/shard_map/ppermute | solution.py:362
  74.4 7.4 %conv_units.7 = (f32[640,1024]{1,0:T(8,128)S(1)}, bf16[3,240,640]{2,1,0:T(8,128)(2,1)S(1)}) custom-call(s32[16]{0:T(128)S(1)} %fusion.refs_0_, f32[640,1024]{1,0:T(8,128)S(1)} %get-tuple-element.21.refs_1_, bf16[8,80,1024]{2,1,0:T(8,128)(2,1)S(1)} %bitcast.22, ...), custom_call_target="tpu_custom_call", output_to_operand_aliasing={{0}: (1, {}), {1}: (7, {})} | custom-call | flops 2831155200 | bytes 8007680 | tf_op jit(solution)/shard_map/conv_units/pallas_call | solution.py:286
  81.9 1.6 %collective-permute-start.15 = (bf16[3,240,640]{2,1,0:T(8,128)(2,1)S(1)}, bf16[3,240,640]{2,1,0:T(8,128)(2,1)S(1)}, u32[]{:S(2)}, u32[]{:S(2)}) collective-permute-start(bf16[3,240,640]{2,1,0:T(8,128)(2,1)S(1)} %get-tuple-element.24), channel_id=1, source_target_pairs={{0,8},{8,16},{16,24},{24,28},{28,20},{20,12},{12,4},{4,0},{2,6},{1... | collective-permute-start | bytes 2764808 | tf_op jit(solution)/shard_map/ppermute | solution.py:362
  83.5 2.1 %collective-permute-done.13.refs_6_ = bf16[3,240,640]{2,1,0:T(8,128)(2,1)S(1)} collective-permute-done((bf16[3,240,640]{2,1,0:T(8,128)(2,1)S(1)}, bf16[3,240,640]{2,1,0:T(8,128)(2,1)S(1)}, u32[]{:S(2)}, u32[]{:S(2)}) %collective-permute-start.13) | collective-permute-done | bytes 921632 | tf_op jit(solution)/shard_map/ppermute | solution.py:362
  85.6 9.9 %collective-permute-done.15.refs_5_ = bf16[3,240,640]{2,1,0:T(8,128)(2,1)S(1)} collective-permute-done((bf16[3,240,640]{2,1,0:T(8,128)(2,1)S(1)}, bf16[3,240,640]{2,1,0:T(8,128)(2,1)S(1)}, u32[]{:S(2)}, u32[]{:S(2)}) %collective-permute-start.15) | collective-permute-done | bytes 921632 | tf_op jit(solution)/shard_map/ppermute | solution.py:362
  95.4 7.6 %conv_units.8.refs_1_ = f32[640,1024]{1,0:T(8,128)S(1)} custom-call(s32[16]{0:T(128)S(1)} %fusion.refs_0_, f32[640,1024]{1,0:T(8,128)S(1)} %get-tuple-element.23.refs_1_, bf16[8,80,1024]{2,1,0:T(8,128)(2,1)S(1)} %bitcast.23, bf16[8,80,1024]{2,1,0:T(8,128)(2,1)S(1)} %collective-permute-done.refs_4_.refs_3_, ...), custom_call_target="tpu_custom_call", output_to_operand_aliasing={{}: (1, {})} | custom-call | flops 2831155200 | bytes 8007680 | tf_op jit(solution)/shard_map/conv_units/pallas_call | solution.py:286
  103.1 5.5 %conv_units.9 = bf16[640,1024]{1,0:T(8,128)(2,1)} custom-call(s32[16]{0:T(128)S(1)} %fusion.refs_0_, f32[640,1024]{1,0:T(8,128)S(1)} %conv_units.8.refs_1_, bf16[8,80,1024]{2,1,0:T(8,128)(2,1)S(1)} %bitcast.24, bf16[8,80,1024]{2,1,0:T(8,128)(2,1)S(1)} %collective-permute-done.refs_4_.refs_3_, f32[16,2,80]{2,1,0:T(2,128)S(1)} %pad_maximum_fusion.refs_5_.refs_4_, ...), custom_call_target="tpu_custom_call" | custom-call | flops 1887436800 | bytes 7086080 | tf_op jit(solution)/shard_map/conv_units/pallas_call | solution.py:286
  (43 shorter events, 6.1 us)
Async XLA Ops:
  0.0 27.2 %copy-start = (bf16[1,640,1024]{2,1,0:T(8,128)(2,1)S(1)}, bf16[1,640,1024]{2,1,0:T(8,128)(2,1)}, u32[]{:S(2)}) copy-start(bf16[1,640,1024]{2,1,0:T(8,128)(2,1)} %param.10) | copy-start | bytes 3932164
  0.0 4.6 %collective-permute-start.1 = (bf16[3,240,640]{2,1,0:T(8,128)(2,1)}, bf16[3,240,640]{2,1,0:T(8,128)(2,1)S(1)}, u32[]{:S(2)}, u32[]{:S(2)}) collective-permute-start(bf16[3,240,640]{2,1,0:T(8,128)(2,1)} %bitcast.26), channel_id=1, source_target_pairs={{0,2},{2,0},{4,6},{6,4},{8,10},{10,8},{12,14},{14,12},{16,18},{18,... | collective-permute-start | bytes 2764808 | tf_op jit(solution)/shard_map/ppermute | solution.py:322
  0.5 14.2 %collective-permute-start.2 = (bf16[3,240,640]{2,1,0:T(8,128)(2,1)}, bf16[3,240,640]{2,1,0:T(8,128)(2,1)S(1)}, u32[]{:S(2)}, u32[]{:S(2)}) collective-permute-start(bf16[3,240,640]{2,1,0:T(8,128)(2,1)} %bitcast.27), channel_id=1, source_target_pairs={{0,8},{8,16},{16,24},{24,28},{28,20},{20,12},{12,4},{4,0},{2,6},{1... | collective-permute-start | bytes 2764808 | tf_op jit(solution)/shard_map/ppermute | solution.py:323
  3.1 44.2 %collective-permute-start = (bf16[8,80,1024]{2,1,0:T(8,128)(2,1)}, bf16[8,80,1024]{2,1,0:T(8,128)(2,1)S(1)}, u32[]{:S(2)}, u32[]{:S(2)}) collective-permute-start(bf16[8,80,1024]{2,1,0:T(8,128)(2,1)} %bitcast.18), channel_id=1, source_target_pairs={{0,1},{1,0},{2,3},{3,2},{4,5},{5,4},{6,7},{7,6},{8,9},{9,8},{10,11... | collective-permute-start | bytes 3932168 | tf_op jit(solution)/shard_map/ppermute | solution.py:310
  4.6 0.7 copy-start.8
  5.4 0.9 copy-start.1
  6.3 0.6 copy-start.7
  6.9 12.1 %all-to-all-start = ((bf16[16,1,80]{2,1,0:T(2,128)(2,1)}), bf16[16,1,80]{2,1,0:T(2,128)(2,1)S(1)}, u32[]{:S(2)}, u32[]{:S(2)}) async-start(bf16[16,1,80]{2,1,0:T(2,128)(2,1)} %copy-done.7), calls=%async_computation | async-start | bytes 16384 | tf_op jit(solution)/shard_map/all_to_all | solution.py:329
  12.4 34.4 %collective-permute-start.6 = (bf16[3,240,640]{2,1,0:T(8,128)(2,1)}, bf16[3,240,640]{2,1,0:T(8,128)(2,1)}, u32[]{:S(2)}, u32[]{:S(2)}) collective-permute-start(bf16[3,240,640]{2,1,0:T(8,128)(2,1)} %copy-done.1), channel_id=1, source_target_pairs={{0,8},{8,16},{16,24},{24,28},{28,20},{20,12},{12,4},{4,0},{2,6},{1... | collective-permute-start | bytes 2764808 | tf_op jit(solution)/shard_map/ppermute | solution.py:362
  19.0 0.9 copy-start.3
  20.0 0.6 copy-start.6
  20.6 26.6 %collective-permute-start.4 = (bf16[3,240,640]{2,1,0:T(8,128)(2,1)S(1)}, bf16[3,240,640]{2,1,0:T(8,128)(2,1)}, u32[]{:S(2)}, u32[]{:S(2)}) collective-permute-start(bf16[3,240,640]{2,1,0:T(8,128)(2,1)S(1)} %get-tuple-element.18.refs_8_), channel_id=1, source_target_pairs={{0,2},{2,0},{4,6},{6,4},{8,10},{10,8},{12,14},{14,12},{16,18},{18,... | collective-permute-start | bytes 2764808 | tf_op jit(solution)/shard_map/ppermute | solution.py:371
  20.6 26.6 %collective-permute-start.5 = (bf16[3,240,640]{2,1,0:T(8,128)(2,1)S(1)}, bf16[3,240,640]{2,1,0:T(8,128)(2,1)}, u32[]{:S(2)}, u32[]{:S(2)}) collective-permute-start(bf16[3,240,640]{2,1,0:T(8,128)(2,1)S(1)} %get-tuple-element.18.refs_8_), channel_id=1, source_target_pairs={{0,8},{8,16},{16,24},{24,28},{28,20},{20,12},{12,4},{4,0},{2,6},{1... | collective-permute-start | bytes 2764808 | tf_op jit(solution)/shard_map/ppermute | solution.py:362
  21.0 18.9 %all-to-all-start.1 = ((f32[16,1,640]{2,1,0:T(1,128)}), f32[16,1,640]{2,1,0:T(1,128)}, u32[]{:S(2)}, u32[]{:S(2)}) async-start(f32[16,1,640]{2,1,0:T(1,128)} %copy-done.6), calls=%async_computation.1 | async-start | bytes 81920 | tf_op jit(solution)/shard_map/all_to_all | solution.py:331
  28.4 0.6 copy-start.4
  39.9 0.7 copy-start.5
  43.2 3.7 %collective-permute-start.3 = (f32[8,2,80]{2,1,0:T(2,128)S(1)}, f32[8,2,80]{2,1,0:T(2,128)S(1)}, u32[]{:S(2)}, u32[]{:S(2)}) collective-permute-start(f32[8,2,80]{2,1,0:T(2,128)S(1)} %affine.1), channel_id=1, source_target_pairs={{0,1},{1,0},{2,3},{3,2},{4,5},{5,4},{6,7},{7,6},{8,9},{9,8},{10,11... | collective-permute-start | bytes 15368 | tf_op jit(solution)/shard_map/ppermute | solution.py:310
  46.9 15.3 %collective-permute-start.7 = (bf16[3,240,640]{2,1,0:T(8,128)(2,1)}, bf16[3,240,640]{2,1,0:T(8,128)(2,1)S(1)}, u32[]{:S(2)}, u32[]{:S(2)}) collective-permute-start(bf16[3,240,640]{2,1,0:T(8,128)(2,1)} %collective-permute-done.6.refs_5_), channel_id=1, source_target_pairs={{0,2},{2,0},{4,6},{6,4},{8,10},{10,8},{12,14},{14,12},{16,18},{18,... | collective-permute-start | bytes 2764808 | tf_op jit(solution)/shard_map/ppermute | solution.py:371
  46.9 15.3 %collective-permute-start.9 = (bf16[3,240,640]{2,1,0:T(8,128)(2,1)}, bf16[3,240,640]{2,1,0:T(8,128)(2,1)S(1)}, u32[]{:S(2)}, u32[]{:S(2)}) collective-permute-start(bf16[3,240,640]{2,1,0:T(8,128)(2,1)} %collective-permute-done.6.refs_5_), channel_id=1, source_target_pairs={{0,8},{8,16},{16,24},{24,28},{28,20},{20,12},{12,4},{4,0},{2,6},{1... | collective-permute-start | bytes 2764808 | tf_op jit(solution)/shard_map/ppermute | solution.py:362
  47.3 1.2 %copy-start.2 = (bf16[3,240,640]{2,1,0:T(8,128)(2,1)S(1)}, bf16[3,240,640]{2,1,0:T(8,128)(2,1)}, u32[]{:S(2)}) copy-start(bf16[3,240,640]{2,1,0:T(8,128)(2,1)} %copy-done.1) | copy-start | bytes 2764804
  48.5 1.3 %copy-start.9 = (bf16[1,640,1024]{2,1,0:T(8,128)(2,1)S(1)}, bf16[1,640,1024]{2,1,0:T(8,128)(2,1)}, u32[]{:S(2)}) copy-start(bf16[1,640,1024]{2,1,0:T(8,128)(2,1)} %param.11) | copy-start | bytes 3932164
  49.8 1.2 %copy-start.10 = (bf16[9,80,640]{2,1,0:T(8,128)(2,1)S(1)}, bf16[9,80,640]{2,1,0:T(8,128)(2,1)}, u32[]{:S(2)}) copy-start(bf16[9,80,640]{2,1,0:T(8,128)(2,1)} %param.17) | copy-start | bytes 2764804
  60.2 2.8 %collective-permute-start.8 = (bf16[3,240,640]{2,1,0:T(8,128)(2,1)}, bf16[3,240,640]{2,1,0:T(8,128)(2,1)S(1)}, u32[]{:S(2)}, u32[]{:S(2)}) collective-permute-start(bf16[3,240,640]{2,1,0:T(8,128)(2,1)} %get-tuple-element.20.refs_7_), channel_id=1, source_target_pairs={{0,2},{2,0},{4,6},{6,4},{8,10},{10,8},{12,14},{14,12},{16,18},{18,... | collective-permute-start | bytes 2764808 | tf_op jit(solution)/shard_map/ppermute | solution.py:371
  60.4 13.6 %collective-permute-start.11 = (bf16[3,240,640]{2,1,0:T(8,128)(2,1)}, bf16[3,240,640]{2,1,0:T(8,128)(2,1)S(1)}, u32[]{:S(2)}, u32[]{:S(2)}) collective-permute-start(bf16[3,240,640]{2,1,0:T(8,128)(2,1)} %get-tuple-element.20.refs_7_), channel_id=1, source_target_pairs={{0,8},{8,16},{16,24},{24,28},{28,20},{20,12},{12,4},{4,0},{2,6},{1... | collective-permute-start | bytes 2764808 | tf_op jit(solution)/shard_map/ppermute | solution.py:362
  71.9 2.5 %collective-permute-start.10 = (bf16[3,240,640]{2,1,0:T(8,128)(2,1)S(1)}, bf16[3,240,640]{2,1,0:T(8,128)(2,1)S(1)}, u32[]{:S(2)}, u32[]{:S(2)}) collective-permute-start(bf16[3,240,640]{2,1,0:T(8,128)(2,1)S(1)} %get-tuple-element.22.refs_5_), channel_id=1, source_target_pairs={{0,2},{2,0},{4,6},{6,4},{8,10},{10,8},{12,14},{14,12},{16,18},{18,... | collective-permute-start | bytes 2764808 | tf_op jit(solution)/shard_map/ppermute | solution.py:371
  72.1 13.4 %collective-permute-start.13 = (bf16[3,240,640]{2,1,0:T(8,128)(2,1)S(1)}, bf16[3,240,640]{2,1,0:T(8,128)(2,1)S(1)}, u32[]{:S(2)}, u32[]{:S(2)}) collective-permute-start(bf16[3,240,640]{2,1,0:T(8,128)(2,1)S(1)} %get-tuple-element.22.refs_5_), channel_id=1, source_target_pairs={{0,8},{8,16},{16,24},{24,28},{28,20},{20,12},{12,4},{4,0},{2,6},{1... | collective-permute-start | bytes 2764808 | tf_op jit(solution)/shard_map/ppermute | solution.py:362
  81.9 13.6 %collective-permute-start.15 = (bf16[3,240,640]{2,1,0:T(8,128)(2,1)S(1)}, bf16[3,240,640]{2,1,0:T(8,128)(2,1)S(1)}, u32[]{:S(2)}, u32[]{:S(2)}) collective-permute-start(bf16[3,240,640]{2,1,0:T(8,128)(2,1)S(1)} %get-tuple-element.24), channel_id=1, source_target_pairs={{0,8},{8,16},{16,24},{24,28},{28,20},{20,12},{12,4},{4,0},{2,6},{1... | collective-permute-start | bytes 2764808 | tf_op jit(solution)/shard_map/ppermute | solution.py:362
  83.4 12.0 %collective-permute-start.12 = (bf16[3,240,640]{2,1,0:T(8,128)(2,1)S(1)}, bf16[3,240,640]{2,1,0:T(8,128)(2,1)S(1)}, u32[]{:S(2)}, u32[]{:S(2)}) collective-permute-start(bf16[3,240,640]{2,1,0:T(8,128)(2,1)S(1)} %get-tuple-element.24), channel_id=1, source_target_pairs={{0,2},{2,0},{4,6},{6,4},{8,10},{10,8},{12,14},{14,12},{16,18},{18,... | collective-permute-start | bytes 2764808 | tf_op jit(solution)/shard_map/ppermute | solution.py:371
  85.6 9.9 %collective-permute-start.14 = (bf16[3,240,640]{2,1,0:T(8,128)(2,1)S(1)}, bf16[3,240,640]{2,1,0:T(8,128)(2,1)S(1)}, u32[]{:S(2)}, u32[]{:S(2)}) collective-permute-start(bf16[3,240,640]{2,1,0:T(8,128)(2,1)S(1)} %collective-permute-done.13.refs_6_), channel_id=1, source_target_pairs={{0,2},{2,0},{4,6},{6,4},{8,10},{10,8},{12,14},{14,12},{16,18},{18,... | collective-permute-start | bytes 2764808 | tf_op jit(solution)/shard_map/ppermute | solution.py:371
  95.4 7.6 %collective-permute-start.16 = (bf16[3,240,640]{2,1,0:T(8,128)(2,1)S(1)}, bf16[3,240,640]{2,1,0:T(8,128)(2,1)S(1)}, u32[]{:S(2)}, u32[]{:S(2)}) collective-permute-start(bf16[3,240,640]{2,1,0:T(8,128)(2,1)S(1)} %collective-permute-done.15.refs_5_), channel_id=1, source_target_pairs={{0,2},{2,0},{4,6},{6,4},{8,10},{10,8},{12,14},{14,12},{16,18},{18,... | collective-permute-start | bytes 2764808 | tf_op jit(solution)/shard_map/ppermute | solution.py:371

commit v3 on v2

v3 whole, which is shorter than its diff:
```python
import functools

import jax
import jax.numpy as jnp
import numpy as np
from jax import lax
from jax.experimental import pallas as pl
from jax.experimental.pallas import tpu as pltpu
from jax.sharding import PartitionSpec as P

C = 1280
GROUPS = 32
HEIGHT = 32
WIDTH = 32
CELLS = HEIGHT * WIDTH
VMEM_BYTES = 28 * 2**20
ANY = pl.BlockSpec(memory_space=pl.ANY)
WHOLE = pl.BlockSpec(memory_space=pltpu.VMEM)


def chip_order(chips):
    if chips % 2:
        return list(range(chips))
    half = chips // 2
    return [2 * z for z in range(half)] + [2 * z + 1 for z in reversed(range(half))]


class Ring:
    def __init__(self, dp):
        self.dp = dp
        n = dp // 2
        order = chip_order(n)
        self.core_pairs = [(i, i ^ 1) for i in range(dp)]
        self.pairs = [(2 * order[k], 2 * order[(k + 1) % n]) for k in range(n)]
        self.pairs += [(2 * order[k] + 1, 2 * order[(k - 1) % n] + 1) for k in range(n)]
        full = (n - 1) // 2
        self.hops = [(s, h) for s in range(1, full + 1) for h in range(2)]
        if n % 2 == 0:
            self.hops.append((full + 1, 0))
        self.blocks = np.zeros((dp, dp), np.int32)
        for k in range(n):
            for core in range(2):
                me = 2 * order[k] + core
                units = [me, me ^ 1]
                for s, h in self.hops:
                    for c in (core, 1 - core):
                        chip = order[(k - s) % n] if c == 0 else order[(k + s) % n]
                        units.append(2 * chip + (c if h == 0 else 1 - c))
                self.blocks[me] = units


def weight(times):
    return pl.CostEstimate(flops=times * 10**9, transcendentals=0, bytes_accessed=times * 4 * 10**6)


def nothing(*refs):
    del refs


def gate(piece, *others):
    return pl.pallas_call(
        nothing,
        out_shape=jax.ShapeDtypeStruct(piece.shape, piece.dtype),
        in_specs=[ANY] * (1 + len(others)),
        out_specs=ANY,
        input_output_aliases={0: 0},
        compiler_params=pltpu.CompilerParams(vmem_limit_bytes=2**20),
        name="gate",
    )(piece, *others)


def act_kernel(emb_ref, out_ref):
    v = emb_ref[...].astype(jnp.float32)
    act = (v / (1.0 + jnp.exp(-v))).astype(jnp.bfloat16)
    rows = out_ref.shape[2]
    for d in range(out_ref.shape[0]):
        out_ref[d] = act[:, d * rows : (d + 1) * rows]


def act_call(emb, count):
    return pl.pallas_call(
        act_kernel,
        out_shape=jax.ShapeDtypeStruct((count, 1, emb.shape[1] // count), jnp.bfloat16),
        in_specs=[WHOLE],
        out_specs=WHOLE,
        compiler_params=pltpu.CompilerParams(vmem_limit_bytes=VMEM_BYTES),
        name="act_rows",
    )(emb)


def emb_kernel(act_ref, w_ref, out_ref):
    out_ref[:, 0, :] = jnp.dot(act_ref[:, 0, :], w_ref[...], preferred_element_type=jnp.float32)


def emb_call(act_rows, w_emb):
    return pl.pallas_call(
        emb_kernel,
        out_shape=jax.ShapeDtypeStruct((act_rows.shape[0], 1, w_emb.shape[1]), jnp.float32),
        in_specs=[WHOLE, WHOLE],
        out_specs=WHOLE,
        compiler_params=pltpu.CompilerParams(vmem_limit_bytes=VMEM_BYTES),
        name="emb_terms",
    )(act_rows, w_emb)


def stats_kernel(h_ref, params_ref, out_ref):
    panel = h_ref.shape[0]
    step = 80 if panel % 80 == 0 else panel
    count = params_ref.shape[0]
    out_ref[0:count, :] = params_ref[...]
    means, variances = [], []
    for start in range(0, panel, step):
        values = h_ref[start : start + step, :].astype(jnp.float32)
        mean = jnp.mean(values, axis=1, keepdims=True)
        means.append(mean)
        variances.append(jnp.mean((values - mean) ** 2, axis=1, keepdims=True))
    for i, columns in ((count, means), (count + 1, variances)):
        column = jnp.concatenate(columns, axis=0)
        out_ref[i : i + 1, :] = jnp.broadcast_to(column, (panel, 128)).T[0:1, :]


def stats_call(h, params):
    return pl.pallas_call(
        stats_kernel,
        out_shape=jax.ShapeDtypeStruct((params.shape[0] + 2, h.shape[0]), jnp.float32),
        in_specs=[WHOLE, WHOLE],
        out_specs=WHOLE,
        compiler_params=pltpu.CompilerParams(vmem_limit_bytes=VMEM_BYTES),
        cost_estimate=weight(10),
        name="channel_stats",
    )(h, params)


def start_kernel(skip_ref, bias_ref, after_ref, out_ref):
    del after_ref
    outs = skip_ref.shape[0]
    bias = jnp.broadcast_to(bias_ref[...], (128, outs)).T[:, 0:1]
    out_ref[...] = skip_ref[...].astype(jnp.float32) + bias


def start_call(skip, bias, after):
    return pl.pallas_call(
        start_kernel,
        out_shape=jax.ShapeDtypeStruct(skip.shape, jnp.float32),
        in_specs=[WHOLE, WHOLE, ANY],
        out_specs=WHOLE,
        compiler_params=pltpu.CompilerParams(vmem_limit_bytes=VMEM_BYTES),
        cost_estimate=weight(0),
        name="start_total",
    )(skip, bias, after)


def affine_kernel(size, terms_ref, table_ref, *refs):
    out_ref = refs[-1]
    rows = out_ref.shape[2]
    b_emb, gain, bias, _, channel_mean, channel_var = (table_ref[i : i + 1, :] for i in range(6))
    shift = jnp.sum(terms_ref[...], axis=0) + b_emb
    width = shift.shape[1]
    group = lax.broadcasted_iota(jnp.int32, (width, width // size), 0) // size
    member = (group == lax.broadcasted_iota(jnp.int32, group.shape, 1)).astype(jnp.float32)

    def per_group(row):
        row = jnp.broadcast_to(row, (8, row.shape[1]))
        return jnp.dot(row, member, precision=lax.Precision.HIGHEST, preferred_element_type=jnp.float32) / size

    def per_channel(groups):
        back = (((1,), (1,)), ((), ()))
        spread = lax.dot_general(
            groups, member, back, precision=lax.Precision.HIGHEST, preferred_element_type=jnp.float32
        )
        return spread[0:1, :]

    center = channel_mean + shift
    mean = per_channel(per_group(center))
    var = per_group(channel_var + (center - mean) ** 2)
    scale = per_channel(lax.rsqrt(var + 1e-05)) * gain
    offset = (shift - mean) * scale + bias
    both = jnp.concatenate([scale, offset], axis=0)
    for d in range(out_ref.shape[0]):
        out_ref[d] = both[:, d * rows : (d + 1) * rows]


def affine_call(size, rows, terms, table, *after):
    channels = terms.shape[2]
    return pl.pallas_call(
        functools.partial(affine_kernel, size),
        out_shape=jax.ShapeDtypeStruct((channels // rows, 2, rows), jnp.float32),
        in_specs=[WHOLE, WHOLE] + [ANY] * len(after),
        out_specs=WHOLE,
        compiler_params=pltpu.CompilerParams(vmem_limit_bytes=VMEM_BYTES),
        cost_estimate=weight(10),
        name="affine",
    )(terms, table, *after)


def norm_kernel(place_ref, ab_ref, *refs):
    h_refs, out_ref = refs[:-1], refs[-1]
    blocks = h_refs[0].shape[0]
    for u in range(out_ref.shape[0]):
        place = place_ref[u]
        ab = ab_ref[place].T
        h = h_refs[0][place % blocks]
        for turn in range(1, len(h_refs)):
            h = jnp.where(place // blocks == turn, h_refs[turn][place % blocks], h)
        v = h.astype(jnp.float32) * ab[:, 0:1] + ab[:, 1:2]
        half = 0.5 * v
        out_ref[u] = (half + half * jnp.tanh(half)).astype(jnp.bfloat16)


def norm_call(places, affine, slices):
    return pl.pallas_call(
        norm_kernel,
        out_shape=jax.ShapeDtypeStruct(places.shape + slices[0].shape[1:], jnp.bfloat16),
        in_specs=[pl.BlockSpec(memory_space=pltpu.SMEM)] + [WHOLE] * (1 + len(slices)),
        out_specs=WHOLE,
        compiler_params=pltpu.CompilerParams(vmem_limit_bytes=VMEM_BYTES),
        cost_estimate=weight(0),
        name="norm_units",
    )(places, affine, *slices)


def shifted(values, amount):
    edge = jnp.zeros((values.shape[0], abs(amount)), values.dtype)
    if amount > 0:
        return jnp.concatenate([values[:, amount:], edge], axis=1)
    return jnp.concatenate([edge, values[:, :amount]], axis=1)


def conv_kernel(ids, last, *refs):
    count = len(ids)
    total_ref, normed_ref = refs[:2]
    weight_refs = refs[2 : 2 + count]
    out_ref, token_ref, even, odd, rounded, sem = refs[2 + count :]
    stacks = (even, odd)
    rows = normed_ref.shape[1]
    outs = total_ref.shape[0]
    column = lax.broadcasted_iota(jnp.int32, (1, CELLS), 1) % WIDTH
    inside = [(column > 0).astype(jnp.bfloat16), None, (column < WIDTH - 1).astype(jnp.bfloat16)]
    token_ref[...] = jnp.zeros_like(token_ref)

    def build(u):
        normed = normed_ref[ids[u]]
        for dx in range(3):
            moved = normed if dx == 1 else shifted(normed, dx - 1) * inside[dx]
            for dy in range(3):
                row = (3 * dy + dx) * rows
                stacks[u % 2][row : row + rows, :] = moved if dy == 1 else shifted(moved, WIDTH * (dy - 1))

    def product(u, here):
        weights = weight_refs[u][:, :, here].reshape(9 * rows, here.stop - here.start)
        return lax.dot_general(
            weights, stacks[u % 2][...], (((0,), (0,)), ((), ())), preferred_element_type=jnp.float32
        )

    build(0)
    if not last:
        for u in range(count):
            if u + 1 < count:
                build(u + 1)
            source = total_ref if u == 0 else out_ref
            out_ref[...] = source[...] + product(u, slice(0, outs))
        return
    tile = 128 if outs % 128 == 0 else outs
    copies = []
    for start in range(0, outs, tile):
        here = slice(start, start + tile)
        rounded[here, :] = (total_ref[here, :] + product(0, here)).astype(jnp.bfloat16)
        part = pl.ds(start, tile)
        copies.append(pltpu.make_async_copy(rounded.at[part], out_ref.at[part], sem.at[start // tile]))
        copies[-1].start()
    for copy in copies:
        copy.wait()


def conv_call(ids, total, normed, weights, last=False):
    count = len(ids)
    _, rows, _ = normed.shape
    outs = weights[0].shape[2]
    tiles = outs // 128 if outs % 128 == 0 else 1
    return pl.pallas_call(
        functools.partial(conv_kernel, tuple(ids), last),
        out_shape=[
            jax.ShapeDtypeStruct((outs, CELLS), jnp.bfloat16 if last else jnp.float32),
            jax.ShapeDtypeStruct((8, 128), jnp.float32),
        ],
        in_specs=[WHOLE] * (2 + count),
        out_specs=[ANY if last else WHOLE, WHOLE],
        scratch_shapes=[
            pltpu.VMEM((9 * rows, CELLS), jnp.bfloat16),
            pltpu.VMEM((9 * rows, CELLS), jnp.bfloat16),
            pltpu.VMEM((outs, CELLS) if last else (16, 128), jnp.bfloat16),
            pltpu.SemaphoreType.DMA((tiles,)),
        ],
        input_output_aliases={} if last else {0: 0},
        compiler_params=pltpu.CompilerParams(vmem_limit_bytes=VMEM_BYTES),
        name="conv_units",
    )(total, normed, *weights)


def make_body(dp, chan):
    ring = Ring(dp)
    chan_pairs = [(i, (i + 1) % chan) for i in range(chan)]

    def around(value):
        values = [value]
        for _ in range(chan - 1):
            values.append(lax.ppermute(values[-1], "chan", chan_pairs))
        return values

    def body(h_in, skip, emb, w_emb, b_emb, gn_gain, gn_bias, w_conv, b_conv):
        panel = h_in.shape[1]
        rows, outs = w_conv.shape[1], w_conv.shape[2]
        blocks = panel // rows
        me = lax.axis_index("dp")
        side = lax.axis_index("chan")

        own = w_conv.reshape(3, 3 * rows, outs)
        final = len(ring.hops) + 1
        pieces = {0: own, 1: lax.ppermute(own, "dp", ring.core_pairs)}
        pieces[2] = lax.ppermute(own, "dp", ring.pairs)

        slices = around(h_in.reshape(blocks, rows, CELLS))

        block = lax.dynamic_slice(jnp.asarray(ring.blocks), (me, 0), (1, dp))[0]
        places = ((side - block // blocks) % chan) * blocks + block % blocks

        def hop(i, *after):
            if after:
                pieces[i - 2] = gate(pieces[i - 2], *after)
            pieces[i] = lax.ppermute(pieces[i - 2], "dp", ring.pairs)

        act = act_call(emb, dp)
        act_rows = lax.all_to_all(act, "dp", 0, 0, tiled=True)
        params = jnp.concatenate([b_emb, gn_gain, gn_bias, b_conv]).reshape(4, panel)
        table = stats_call(h_in[0], params)
        if final >= 3:
            hop(3, act)
        terms = emb_call(act_rows, w_emb)
        total = start_call(skip[0], table[3:4], terms)
        if final >= 4:
            hop(4, terms)
        terms = lax.all_to_all(terms, "dp", 0, 0, tiled=True)
        affine = affine_call(C // GROUPS, rows, terms, table, total, places, pieces[min(3, final)], *slices[1:])
        affine = jnp.concatenate(around(affine), axis=0)
        if final >= 5:
            hop(5)

        normed = norm_call(places, affine, slices)

        units = [(0, own), (1, pieces[1])]
        tokens = []

        def arrived(i):
            units.append((2 * i - 2, pieces[i]))

        def swap(i):
            units.append((2 * i - 1, lax.ppermute(pieces[i], "dp", ring.core_pairs)))

        def convolve(total, count, last=False):
            here = [units.pop(0) for _ in range(min(count, len(units)))]
            total, token = conv_call([u for u, _ in here], total, normed, [w for _, w in here], last)
            tokens.append(token)
            return total

        for i in range(2, min(final, 3) + 1):
            arrived(i)
            swap(i)
        if final >= 4:
            total = convolve(total, 4)
        for i in range(6, final + 1):
            hop(i, tokens[-2] if len(tokens) > 1 else normed)
            arrived(i - 2)
            total = convolve(total, 4)
            swap(i - 2)
        if final >= 5:
            arrived(final - 1)
        while len(units) > 4:
            total = convolve(total, 4)
        if final >= 4:
            total = convolve(total, len(units))
            if final >= 5:
                swap(final - 1)
            pieces[final] = gate(pieces[final], tokens[-1])
            arrived(final)
            swap(final)
        while len(units) > 1:
            total = convolve(total, min(4, len(units) - 1))
        total = convolve(total, 1, last=True)
        return total[None]

    return body


def solution(mesh):
    return jax.shard_map(
        make_body(mesh.shape["dp"], mesh.shape["chan"]),
        mesh=mesh,
        in_specs=(
            P("dp", "chan", None),
            P("dp", "chan", None),
            P("dp", None),
            P("dp", "chan"),
            P("chan"),
            P("chan"),
            P("chan"),
            P(None, "dp", "chan"),
            P("chan"),
        ),
        out_specs=P("dp", "chan", None),
        check_vma=False,
    )
```

time: 110 us -> 88.7 us (0.81)
  waiting for transfers between devices: 29.6 us -> 18.8 us
  local copies, waits for them, and re-layouts: 11.5 us -> 4.09 us
  Pallas kernels: 42.7 us -> 37.2 us
  starting transfers between devices: 24 us -> 26.1 us
    all_to_all x1, waiting for transfers between devices: 10.9 us -> 2.49 us  [body(): terms = lax.all_to_all(terms, 'dp', 0, 0, tiled=True)]
    pallas_call x8 -> x18, Pallas kernels: 40.1 us -> 34.6 us  [the longest x7 28.5 us: conv_call(): pl.pallas_call(functools.partial(conv_kernel, tuple(ids), last), out_shap...]
    unnamed x22 -> x16, local copies, waits for them, and re-layouts: 8.72 us -> 4.06 us
    reshape x4 -> x1, local copies, waits for them, and re-layouts: 2.76 us -> 0.01 us  [body(): jnp.concatenate([b_emb, gn_gain, gn_bias, b_conv]).reshape(4, panel)]
    ppermute x13, starting transfers between devices: 8.26 us -> 10.7 us  [the longest x6 10.2 us: hop(): pieces[i] = lax.ppermute(pieces[i - 2], 'dp', ring.pairs)]
    ppermute x13, waiting for transfers between devices: 13.3 us -> 11.4 us  [the longest x6 11.4 us: hop(): pieces[i] = lax.ppermute(pieces[i - 2], 'dp', ring.pairs)]
    ppermute x2, starting transfers between devices: 3 us -> 4.25 us  [around(): values.append(lax.ppermute(values[-1], 'chan', chan_pairs))]
  transfers between devices with their start and end apart: 19 -> 19, of which waited for: 9 -> 7; matrix products, arithmetic and copies ran while one was open for 3% -> 2% of each run, Pallas kernels for 34% -> 39%
where the time goes in v3:
time: 88.7 us; the launch traced here: 88 us
  Pallas kernels  37.2 us (42%)
  starting transfers between devices  26.1 us (29%)
  waiting for transfers between devices  18.8 us (21%)
  local copies, waits for them, and re-layouts  4.09 us (5%)
  other arithmetic  1.47 us (2%)
    pallas_call x7, Pallas kernels, conv_call(): pl.pallas_call(functools.partial(conv_kernel, tuple(ids), last), out_shap...  28.5 us
    ppermute x6, waiting for transfers between devices, hop(): pieces[i] = lax.ppermute(pieces[i - 2], 'dp', ring.pairs)  11.4 us
    ppermute x6, starting transfers between devices, hop(): pieces[i] = lax.ppermute(pieces[i - 2], 'dp', ring.pairs)  10.2 us
    all_to_all x1, starting transfers between devices, body(): act_rows = lax.all_to_all(act, 'dp', 0, 0, tiled=True)  4.93 us
    ppermute x2, starting transfers between devices, around(): values.append(lax.ppermute(values[-1], 'chan', chan_pairs))  4.25 us
    all_to_all x1, starting transfers between devices, body(): terms = lax.all_to_all(terms, 'dp', 0, 0, tiled=True)  4.15 us
    unnamed x16, local copies, waits for them, and re-layouts  4.06 us
    all_to_all x1, waiting for transfers between devices, body(): act_rows = lax.all_to_all(act, 'dp', 0, 0, tiled=True)  3.74 us
  transfers between devices with their start and end apart: 19, of which 7 were waited for; matrix products, arithmetic and copies ran while one was open for 2% of the time, Pallas kernels for 39%

profile of v3, /device:TPU:0, one launch (start us, length us, event | category | flops | bytes accessed | tf_op | source)
XLA Modules:
  0.0 88.0 jit_solution(8232956167685583)
XLA Ops:
  0.5 2.5 %collective-permute-start.2 = (bf16[8,80,1024]{2,1,0:T(8,128)(2,1)}, bf16[8,80,1024]{2,1,0:T(8,128)(2,1)}, u32[]{:S(2)}, u32[]{:S(2)}) collective-permute-start(bf16[8,80,1024]{2,1,0:T(8,128)(2,1)} %bitcast.19), channel_id=1, source_target_pairs={{0,1},{1,0},{2,3},{3,2},{4,5},{5,4},{6,7},{7,6},{8,9},{9,8},{10,11... | collective-permute-start | bytes 3932168 | tf_op jit(solution)/shard_map/ppermute | solution.py:307
  2.9 1.6 %collective-permute-start.4 = (bf16[3,240,640]{2,1,0:T(8,128)(2,1)}, bf16[3,240,640]{2,1,0:T(8,128)(2,1)S(1)}, u32[]{:S(2)}, u32[]{:S(2)}) collective-permute-start(bf16[3,240,640]{2,1,0:T(8,128)(2,1)} %bitcast.23), channel_id=1, source_target_pairs={{0,8},{8,16},{16,24},{24,28},{28,20},{20,12},{12,4},{4,0},{2,6},{1... | collective-permute-start | bytes 2764808 | tf_op jit(solution)/shard_map/ppermute | solution.py:320
  5.9 4.9 %all-to-all-start = ((bf16[16,1,80]{2,1,0:T(2,128)(2,1)}), bf16[16,1,80]{2,1,0:T(2,128)(2,1)S(1)}, u32[]{:S(2)}, u32[]{:S(2)}) async-start(bf16[16,1,80]{2,1,0:T(2,128)(2,1)} %act_rows.1.refs_1_), calls=%async_computation | async-start | bytes 16384 | tf_op jit(solution)/shard_map/all_to_all | solution.py:333
  10.8 0.7 pad_maximum_fusion.1
  11.6 2.0 %collective-permute-start.1 = (bf16[3,240,640]{2,1,0:T(8,128)(2,1)}, bf16[3,240,640]{2,1,0:T(8,128)(2,1)}, u32[]{:S(2)}, u32[]{:S(2)}) collective-permute-start(bf16[3,240,640]{2,1,0:T(8,128)(2,1)} %gate.6.refs_3_), channel_id=1, source_target_pairs={{0,8},{8,16},{16,24},{24,28},{28,20},{20,12},{12,4},{4,0},{2,6},{1... | collective-permute-start | bytes 2764808 | tf_op jit(solution)/shard_map/ppermute | solution.py:330
  13.6 1.3 %copy-done.1 = bf16[1,640,1024]{2,1,0:T(8,128)(2,1)S(1)} copy-done((bf16[1,640,1024]{2,1,0:T(8,128)(2,1)S(1)}, bf16[1,640,1024]{2,1,0:T(8,128)(2,1)}, u32[]{:S(2)}) %copy-start.1) | copy-done | bytes 1310744
  14.9 1.2 %channel_stats.1.table_ref = f32[6,640]{1,0:T(8,128)S(1)} custom-call(bf16[640,1024]{1,0:T(8,128)(2,1)S(1)} %bitcast.20, f32[4,640]{1,0:T(4,128)S(1)} %reshape.9.params_ref), custom_call_target="tpu_custom_call" | custom-call | flops 10000000000 | bytes 40000000 | tf_op jit(solution)/shard_map/channel_stats/pallas_call | solution.py:123
  16.1 3.7 %all-to-all-done.act_ref = bf16[16,1,80]{2,1,0:T(2,128)(2,1)S(1)} async-done(((bf16[16,1,80]{2,1,0:T(2,128)(2,1)}), bf16[16,1,80]{2,1,0:T(2,128)(2,1)S(1)}, u32[]{:S(2)}, u32[]{:S(2)}) %all-to-all-start) | async-done | bytes 2592 | tf_op jit(solution)/shard_map/all_to_all | solution.py:333
  19.9 0.8 emb_terms.1.after_ref.refs_1_
  20.6 4.1 %all-to-all-start.1 = ((f32[16,1,640]{2,1,0:T(1,128)}), f32[16,1,640]{2,1,0:T(1,128)}, u32[]{:S(2)}, u32[]{:S(2)}) async-start(f32[16,1,640]{2,1,0:T(1,128)} %emb_terms.1.after_ref.refs_1_), calls=%async_computation.1 | async-start | bytes 81920 | tf_op jit(solution)/shard_map/all_to_all | solution.py:342
  25.5 1.3 %copy-done = bf16[1,640,1024]{2,1,0:T(8,128)(2,1)S(1)} copy-done((bf16[1,640,1024]{2,1,0:T(8,128)(2,1)S(1)}, bf16[1,640,1024]{2,1,0:T(8,128)(2,1)}, u32[]{:S(2)}) %copy-start) | copy-done | bytes 1310744
  27.2 1.8 %collective-permute-start.7 = (bf16[3,240,640]{2,1,0:T(8,128)(2,1)S(1)}, bf16[3,240,640]{2,1,0:T(8,128)(2,1)}, u32[]{:S(2)}, u32[]{:S(2)}) collective-permute-start(bf16[3,240,640]{2,1,0:T(8,128)(2,1)S(1)} %gate.7.refs_4_), channel_id=1, source_target_pairs={{0,8},{8,16},{16,24},{24,28},{28,20},{20,12},{12,4},{4,0},{2,6},{1... | collective-permute-start | bytes 2764808 | tf_op jit(solution)/shard_map/ppermute | solution.py:330
  29.0 2.5 %all-to-all-done.1.terms_ref = f32[16,1,640]{2,1,0:T(1,128)} async-done(((f32[16,1,640]{2,1,0:T(1,128)}), f32[16,1,640]{2,1,0:T(1,128)}, u32[]{:S(2)}, u32[]{:S(2)}) %all-to-all-start.1) | async-done | bytes 40992 | tf_op jit(solution)/shard_map/all_to_all | solution.py:342
  31.5 1.2 %collective-permute-done.2.refs_3_.refs_1_ = bf16[8,80,1024]{2,1,0:T(8,128)(2,1)} collective-permute-done((bf16[8,80,1024]{2,1,0:T(8,128)(2,1)}, bf16[8,80,1024]{2,1,0:T(8,128)(2,1)}, u32[]{:S(2)}, u32[]{:S(2)}) %collective-permute-start.2) | collective-permute-done | bytes 1310752 | tf_op jit(solution)/shard_map/ppermute | solution.py:307
  32.7 0.7 copy-done.7
  33.4 2.6 %affine.1 = f32[8,2,80]{2,1,0:T(2,128)S(1)} custom-call(f32[16,1,640]{2,1,0:T(1,128)} %all-to-all-done.1.terms_ref, f32[6,640]{1,0:T(8,128)S(1)} %copy-done.7, f32[640,1024]{1,0:T(8,128)S(1)} %start_total.1.refs_0_, s32[16]{0:T(128)S(1)} %fusion.refs_1_.place_ref, bf16[3,240,640]{2,1,0:T(8,128)(2,1)} %collective-permute-done.1.refs_2_, ...), custom_call_target="tpu_custom_call" | custom-call | flops 10000000000 | bytes 40000000 | tf_op jit(solution)/shard_map/affine/pallas_call | solution.py:185
  36.0 1.8 %collective-permute-start.3 = (f32[8,2,80]{2,1,0:T(2,128)S(1)}, f32[8,2,80]{2,1,0:T(2,128)S(1)}, u32[]{:S(2)}, u32[]{:S(2)}) collective-permute-start(f32[8,2,80]{2,1,0:T(2,128)S(1)} %affine.1), channel_id=1, source_target_pairs={{0,1},{1,0},{2,3},{3,2},{4,5},{5,4},{6,7},{7,6},{8,9},{9,8},{10,11... | collective-permute-start | bytes 15368 | tf_op jit(solution)/shard_map/ppermute | solution.py:307
  38.3 1.6 %collective-permute-start.9 = (bf16[3,240,640]{2,1,0:T(8,128)(2,1)}, bf16[3,240,640]{2,1,0:T(8,128)(2,1)S(1)}, u32[]{:S(2)}, u32[]{:S(2)}) collective-permute-start(bf16[3,240,640]{2,1,0:T(8,128)(2,1)} %collective-permute-done.1.refs_2_), channel_id=1, source_target_pairs={{0,8},{8,16},{16,24},{24,28},{28,20},{20,12},{12,4},{4,0},{2,6},{1... | collective-permute-start | bytes 2764808 | tf_op jit(solution)/shard_map/ppermute | solution.py:330
  39.9 3.2 %norm_units.1.refs_1_ = bf16[16,80,1024]{2,1,0:T(8,128)(2,1)S(1)} custom-call(s32[16]{0:T(128)S(1)} %fusion.refs_1_.place_ref, f32[16,2,80]{2,1,0:T(2,128)S(1)} %pad_maximum_fusion.ab_ref, bf16[8,80,1024]{2,1,0:T(8,128)(2,1)S(1)} %bitcast.21, bf16[8,80,1024]{2,1,0:T(8,128)(2,1)} %collective-permute-done.2.refs_3_.refs_1_), custom_call_target="tpu_custom_call" | custom-call | tf_op jit(solution)/shard_map/norm_units/pallas_call | solution.py:211
  43.1 1.7 %collective-permute-start.11 = (bf16[3,240,640]{2,1,0:T(8,128)(2,1)}, bf16[3,240,640]{2,1,0:T(8,128)(2,1)S(1)}, u32[]{:S(2)}, u32[]{:S(2)}) collective-permute-start(bf16[3,240,640]{2,1,0:T(8,128)(2,1)} %gate.8.refs_4_), channel_id=1, source_target_pairs={{0,8},{8,16},{16,24},{24,28},{28,20},{20,12},{12,4},{4,0},{2,6},{1... | collective-permute-start | bytes 2764808 | tf_op jit(solution)/shard_map/ppermute | solution.py:330
  44.8 6.5 %conv_units.7 = (f32[640,1024]{1,0:T(8,128)S(1)}, f32[8,128]{1,0:T(8,128)S(1)}) custom-call(f32[640,1024]{1,0:T(8,128)S(1)} %start_total.1.refs_0_, bf16[16,80,1024]{2,1,0:T(8,128)(2,1)S(1)} %norm_units.1.refs_1_, bf16[3,240,640]{2,1,0:T(8,128)(2,1)S(1)} %bitcast.24, bf16[3,240,640]{2,1,0:T(8,128)(2,1)} %gate.6.refs_3_, ...), custom_call_target="tpu_custom_call", output_to_operand_aliasing={{0}: (0, {})} | custom-call | tf_op jit(solution)/shard_map/conv_units/pallas_call | solution.py:280
  51.9 1.6 %collective-permute-start.13 = (bf16[3,240,640]{2,1,0:T(8,128)(2,1)S(1)}, bf16[3,240,640]{2,1,0:T(8,128)(2,1)S(1)}, u32[]{:S(2)}, u32[]{:S(2)}) collective-permute-start(bf16[3,240,640]{2,1,0:T(8,128)(2,1)S(1)} %gate.9.refs_3_), channel_id=1, source_target_pairs={{0,8},{8,16},{16,24},{24,28},{28,20},{20,12},{12,4},{4,0},{2,6},{1... | collective-permute-start | bytes 2764808 | tf_op jit(solution)/shard_map/ppermute | solution.py:330
  53.5 5.7 %conv_units.8 = (f32[640,1024]{1,0:T(8,128)S(1)}, f32[8,128]{1,0:T(8,128)S(1)}) custom-call(f32[640,1024]{1,0:T(8,128)S(1)} %get-tuple-element.15.refs_0_, bf16[16,80,1024]{2,1,0:T(8,128)(2,1)S(1)} %norm_units.1.refs_1_, bf16[3,240,640]{2,1,0:T(8,128)(2,1)} %collective-permute-done.1.refs_2_, ...), custom_call_target="tpu_custom_call", output_to_operand_aliasing={{0}: (0, {})} | custom-call | tf_op jit(solution)/shard_map/conv_units/pallas_call | solution.py:280
  59.3 2.5 %collective-permute-done.11.refs_0_ = bf16[3,240,640]{2,1,0:T(8,128)(2,1)S(1)} collective-permute-done((bf16[3,240,640]{2,1,0:T(8,128)(2,1)}, bf16[3,240,640]{2,1,0:T(8,128)(2,1)S(1)}, u32[]{:S(2)}, u32[]{:S(2)}) %collective-permute-start.11) | collective-permute-done | bytes 921632 | tf_op jit(solution)/shard_map/ppermute | solution.py:330
  61.8 1.6 %collective-permute-start.15 = (bf16[3,240,640]{2,1,0:T(8,128)(2,1)S(1)}, bf16[3,240,640]{2,1,0:T(8,128)(2,1)S(1)}, u32[]{:S(2)}, u32[]{:S(2)}) collective-permute-start(bf16[3,240,640]{2,1,0:T(8,128)(2,1)S(1)} %gate.10.refs_3_), channel_id=1, source_target_pairs={{0,8},{8,16},{16,24},{24,28},{28,20},{20,12},{12,4},{4,0},{2,6},{1... | collective-permute-start | bytes 2764808 | tf_op jit(solution)/shard_map/ppermute | solution.py:330
  63.4 3.4 %conv_units.9 = (f32[640,1024]{1,0:T(8,128)S(1)}, f32[8,128]{1,0:T(8,128)}) custom-call(f32[640,1024]{1,0:T(8,128)S(1)} %get-tuple-element.16.refs_0_, bf16[16,80,1024]{2,1,0:T(8,128)(2,1)S(1)} %norm_units.1.refs_1_, bf16[3,240,640]{2,1,0:T(8,128)(2,1)S(1)} %collective-permute-done.8.refs_2_, ...), custom_call_target="tpu_custom_call", output_to_operand_aliasing={{0}: (0, {})} | custom-call | tf_op jit(solution)/shard_map/conv_units/pallas_call | solution.py:280
  66.7 4.9 %collective-permute-done.13.refs_3_ = bf16[3,240,640]{2,1,0:T(8,128)(2,1)S(1)} collective-permute-done((bf16[3,240,640]{2,1,0:T(8,128)(2,1)S(1)}, bf16[3,240,640]{2,1,0:T(8,128)(2,1)S(1)}, u32[]{:S(2)}, u32[]{:S(2)}) %collective-permute-start.13) | collective-permute-done | bytes 921632 | tf_op jit(solution)/shard_map/ppermute | solution.py:330
  71.7 3.4 %conv_units.10 = (f32[640,1024]{1,0:T(8,128)S(1)}, f32[8,128]{1,0:T(8,128)}) custom-call(f32[640,1024]{1,0:T(8,128)S(1)} %get-tuple-element.18.refs_0_, bf16[16,80,1024]{2,1,0:T(8,128)(2,1)S(1)} %norm_units.1.refs_1_, bf16[3,240,640]{2,1,0:T(8,128)(2,1)S(1)} %collective-permute-done.10.refs_2_, ...), custom_call_target="tpu_custom_call", output_to_operand_aliasing={{0}: (0, {})} | custom-call | tf_op jit(solution)/shard_map/conv_units/pallas_call | solution.py:280
  75.1 3.2 %conv_units.11 = (f32[640,1024]{1,0:T(8,128)S(1)}, f32[8,128]{1,0:T(8,128)S(1)}) custom-call(f32[640,1024]{1,0:T(8,128)S(1)} %get-tuple-element.20.refs_0_, bf16[16,80,1024]{2,1,0:T(8,128)(2,1)S(1)} %norm_units.1.refs_1_, bf16[3,240,640]{2,1,0:T(8,128)(2,1)S(1)} %collective-permute-done.12.refs_2_, ...), custom_call_target="tpu_custom_call", output_to_operand_aliasing={{0}: (0, {})} | custom-call | tf_op jit(solution)/shard_map/conv_units/pallas_call | solution.py:280
  78.3 3.2 %collective-permute-done.15.refs_0_ = bf16[3,240,640]{2,1,0:T(8,128)(2,1)S(1)} collective-permute-done((bf16[3,240,640]{2,1,0:T(8,128)(2,1)S(1)}, bf16[3,240,640]{2,1,0:T(8,128)(2,1)S(1)}, u32[]{:S(2)}, u32[]{:S(2)}) %collective-permute-start.15) | collective-permute-done | bytes 921632 | tf_op jit(solution)/shard_map/ppermute | solution.py:330
  81.6 3.3 %conv_units.12 = (f32[640,1024]{1,0:T(8,128)S(1)}, f32[8,128]{1,0:T(8,128)}) custom-call(f32[640,1024]{1,0:T(8,128)S(1)} %get-tuple-element.21.refs_0_, bf16[16,80,1024]{2,1,0:T(8,128)(2,1)S(1)} %norm_units.1.refs_1_, bf16[3,240,640]{2,1,0:T(8,128)(2,1)S(1)} %collective-permute-done.14.refs_2_, ...), custom_call_target="tpu_custom_call", output_to_operand_aliasing={{0}: (0, {})} | custom-call | tf_op jit(solution)/shard_map/conv_units/pallas_call | solution.py:280
  84.9 2.9 %conv_units.13 = (bf16[640,1024]{1,0:T(8,128)(2,1)}, f32[8,128]{1,0:T(8,128)}) custom-call(f32[640,1024]{1,0:T(8,128)S(1)} %get-tuple-element.23.refs_0_, bf16[16,80,1024]{2,1,0:T(8,128)(2,1)S(1)} %norm_units.1.refs_1_, bf16[3,240,640]{2,1,0:T(8,128)(2,1)S(1)} %collective-permute-done.16.refs_2_), custom_call_target="tpu_custom_call" | custom-call | tf_op jit(solution)/shard_map/conv_units/pallas_call | solution.py:280
  (46 shorter events, 4.2 us)
Async XLA Ops:
  0.0 11.6 %collective-permute-start = (bf16[3,240,640]{2,1,0:T(8,128)(2,1)}, bf16[3,240,640]{2,1,0:T(8,128)(2,1)}, u32[]{:S(2)}, u32[]{:S(2)}) collective-permute-start(bf16[3,240,640]{2,1,0:T(8,128)(2,1)} %bitcast.22), channel_id=1, source_target_pairs={{0,2},{2,0},{4,6},{6,4},{8,10},{10,8},{12,14},{14,12},{16,18},{18,... | collective-permute-start | bytes 2764808 | tf_op jit(solution)/shard_map/ppermute | solution.py:319
  0.5 32.3 %collective-permute-start.2 = (bf16[8,80,1024]{2,1,0:T(8,128)(2,1)}, bf16[8,80,1024]{2,1,0:T(8,128)(2,1)}, u32[]{:S(2)}, u32[]{:S(2)}) collective-permute-start(bf16[8,80,1024]{2,1,0:T(8,128)(2,1)} %bitcast.19), channel_id=1, source_target_pairs={{0,1},{1,0},{2,3},{3,2},{4,5},{5,4},{6,7},{7,6},{8,9},{9,8},{10,11... | collective-permute-start | bytes 3932168 | tf_op jit(solution)/shard_map/ppermute | solution.py:307
  2.9 24.2 %collective-permute-start.4 = (bf16[3,240,640]{2,1,0:T(8,128)(2,1)}, bf16[3,240,640]{2,1,0:T(8,128)(2,1)S(1)}, u32[]{:S(2)}, u32[]{:S(2)}) collective-permute-start(bf16[3,240,640]{2,1,0:T(8,128)(2,1)} %bitcast.23), channel_id=1, source_target_pairs={{0,8},{8,16},{16,24},{24,28},{28,20},{20,12},{12,4},{4,0},{2,6},{1... | collective-permute-start | bytes 2764808 | tf_op jit(solution)/shard_map/ppermute | solution.py:320
  4.5 0.7 copy-start.5
  5.9 13.9 %all-to-all-start = ((bf16[16,1,80]{2,1,0:T(2,128)(2,1)}), bf16[16,1,80]{2,1,0:T(2,128)(2,1)S(1)}, u32[]{:S(2)}, u32[]{:S(2)}) async-start(bf16[16,1,80]{2,1,0:T(2,128)(2,1)} %act_rows.1.refs_1_), calls=%async_computation | async-start | bytes 16384 | tf_op jit(solution)/shard_map/all_to_all | solution.py:333
  11.6 21.1 %collective-permute-start.1 = (bf16[3,240,640]{2,1,0:T(8,128)(2,1)}, bf16[3,240,640]{2,1,0:T(8,128)(2,1)}, u32[]{:S(2)}, u32[]{:S(2)}) collective-permute-start(bf16[3,240,640]{2,1,0:T(8,128)(2,1)} %gate.6.refs_3_), channel_id=1, source_target_pairs={{0,8},{8,16},{16,24},{24,28},{28,20},{20,12},{12,4},{4,0},{2,6},{1... | collective-permute-start | bytes 2764808 | tf_op jit(solution)/shard_map/ppermute | solution.py:330
  13.6 1.3 %copy-start.1 = (bf16[1,640,1024]{2,1,0:T(8,128)(2,1)S(1)}, bf16[1,640,1024]{2,1,0:T(8,128)(2,1)}, u32[]{:S(2)}) copy-start(bf16[1,640,1024]{2,1,0:T(8,128)(2,1)} %param.10) | copy-start | bytes 3932164
  14.9 4.9 %copy-start.4 = (bf16[80,640]{1,0:T(8,128)(2,1)S(1)}, bf16[80,640]{1,0:T(8,128)(2,1)}, u32[]{:S(2)}) copy-start(bf16[80,640]{1,0:T(8,128)(2,1)} %w_ref.1) | copy-start | bytes 307204
  16.1 9.4 %copy-start.6 = (f32[6,640]{1,0:T(8,128)}, f32[6,640]{1,0:T(8,128)S(1)}, u32[]{:S(2)}) copy-start(f32[6,640]{1,0:T(8,128)S(1)} %channel_stats.1.table_ref) | copy-start | bytes 46084
  20.6 10.9 %all-to-all-start.1 = ((f32[16,1,640]{2,1,0:T(1,128)}), f32[16,1,640]{2,1,0:T(1,128)}, u32[]{:S(2)}, u32[]{:S(2)}) async-start(f32[16,1,640]{2,1,0:T(1,128)} %emb_terms.1.after_ref.refs_1_), calls=%async_computation.1 | async-start | bytes 81920 | tf_op jit(solution)/shard_map/all_to_all | solution.py:342
  25.5 1.3 %copy-start = (bf16[1,640,1024]{2,1,0:T(8,128)(2,1)S(1)}, bf16[1,640,1024]{2,1,0:T(8,128)(2,1)}, u32[]{:S(2)}) copy-start(bf16[1,640,1024]{2,1,0:T(8,128)(2,1)} %param.11) | copy-start | bytes 3932164
  27.2 15.9 %collective-permute-start.7 = (bf16[3,240,640]{2,1,0:T(8,128)(2,1)S(1)}, bf16[3,240,640]{2,1,0:T(8,128)(2,1)}, u32[]{:S(2)}, u32[]{:S(2)}) collective-permute-start(bf16[3,240,640]{2,1,0:T(8,128)(2,1)S(1)} %gate.7.refs_4_), channel_id=1, source_target_pairs={{0,8},{8,16},{16,24},{24,28},{28,20},{20,12},{12,4},{4,0},{2,6},{1... | collective-permute-start | bytes 2764808 | tf_op jit(solution)/shard_map/ppermute | solution.py:330
  31.5 8.4 %copy-start.2 = (bf16[1,640,1024]{2,1,0:T(8,128)(2,1)S(1)}, bf16[1,640,1024]{2,1,0:T(8,128)(2,1)}, u32[]{:S(2)}) copy-start(bf16[1,640,1024]{2,1,0:T(8,128)(2,1)} %param.10) | copy-start | bytes 3932164
  32.7 0.7 copy-start.7
  36.0 3.8 %collective-permute-start.3 = (f32[8,2,80]{2,1,0:T(2,128)S(1)}, f32[8,2,80]{2,1,0:T(2,128)S(1)}, u32[]{:S(2)}, u32[]{:S(2)}) collective-permute-start(f32[8,2,80]{2,1,0:T(2,128)S(1)} %affine.1), channel_id=1, source_target_pairs={{0,1},{1,0},{2,3},{3,2},{4,5},{5,4},{6,7},{7,6},{8,9},{9,8},{10,11... | collective-permute-start | bytes 15368 | tf_op jit(solution)/shard_map/ppermute | solution.py:307
  37.8 7.0 %collective-permute-start.5 = (bf16[3,240,640]{2,1,0:T(8,128)(2,1)S(1)}, bf16[3,240,640]{2,1,0:T(8,128)(2,1)S(1)}, u32[]{:S(2)}, u32[]{:S(2)}) collective-permute-start(bf16[3,240,640]{2,1,0:T(8,128)(2,1)S(1)} %gate.7.refs_4_), channel_id=1, source_target_pairs={{0,2},{2,0},{4,6},{6,4},{8,10},{10,8},{12,14},{14,12},{16,18},{18,... | collective-permute-start | bytes 2764808 | tf_op jit(solution)/shard_map/ppermute | solution.py:357
  37.8 15.7 %collective-permute-start.6 = (bf16[3,240,640]{2,1,0:T(8,128)(2,1)}, bf16[3,240,640]{2,1,0:T(8,128)(2,1)S(1)}, u32[]{:S(2)}, u32[]{:S(2)}) collective-permute-start(bf16[3,240,640]{2,1,0:T(8,128)(2,1)} %collective-permute-done.1.refs_2_), channel_id=1, source_target_pairs={{0,2},{2,0},{4,6},{6,4},{8,10},{10,8},{12,14},{14,12},{16,18},{18,... | collective-permute-start | bytes 2764808 | tf_op jit(solution)/shard_map/ppermute | solution.py:357
  38.3 13.6 %collective-permute-start.9 = (bf16[3,240,640]{2,1,0:T(8,128)(2,1)}, bf16[3,240,640]{2,1,0:T(8,128)(2,1)S(1)}, u32[]{:S(2)}, u32[]{:S(2)}) collective-permute-start(bf16[3,240,640]{2,1,0:T(8,128)(2,1)} %collective-permute-done.1.refs_2_), channel_id=1, source_target_pairs={{0,8},{8,16},{16,24},{24,28},{28,20},{20,12},{12,4},{4,0},{2,6},{1... | collective-permute-start | bytes 2764808 | tf_op jit(solution)/shard_map/ppermute | solution.py:330
  43.1 1.7 %copy-start.3 = (bf16[9,80,640]{2,1,0:T(8,128)(2,1)S(1)}, bf16[9,80,640]{2,1,0:T(8,128)(2,1)}, u32[]{:S(2)}) copy-start(bf16[9,80,640]{2,1,0:T(8,128)(2,1)} %param.17) | copy-start | bytes 2764804
  43.1 18.7 %collective-permute-start.11 = (bf16[3,240,640]{2,1,0:T(8,128)(2,1)}, bf16[3,240,640]{2,1,0:T(8,128)(2,1)S(1)}, u32[]{:S(2)}, u32[]{:S(2)}) collective-permute-start(bf16[3,240,640]{2,1,0:T(8,128)(2,1)} %gate.8.refs_4_), channel_id=1, source_target_pairs={{0,8},{8,16},{16,24},{24,28},{28,20},{20,12},{12,4},{4,0},{2,6},{1... | collective-permute-start | bytes 2764808 | tf_op jit(solution)/shard_map/ppermute | solution.py:330
  44.8 18.6 %collective-permute-start.8 = (bf16[3,240,640]{2,1,0:T(8,128)(2,1)}, bf16[3,240,640]{2,1,0:T(8,128)(2,1)S(1)}, u32[]{:S(2)}, u32[]{:S(2)}) collective-permute-start(bf16[3,240,640]{2,1,0:T(8,128)(2,1)} %gate.8.refs_4_), channel_id=1, source_target_pairs={{0,2},{2,0},{4,6},{6,4},{8,10},{10,8},{12,14},{14,12},{16,18},{18,... | collective-permute-start | bytes 2764808 | tf_op jit(solution)/shard_map/ppermute | solution.py:357
  51.9 19.8 %collective-permute-start.10 = (bf16[3,240,640]{2,1,0:T(8,128)(2,1)S(1)}, bf16[3,240,640]{2,1,0:T(8,128)(2,1)S(1)}, u32[]{:S(2)}, u32[]{:S(2)}) collective-permute-start(bf16[3,240,640]{2,1,0:T(8,128)(2,1)S(1)} %gate.9.refs_3_), channel_id=1, source_target_pairs={{0,2},{2,0},{4,6},{6,4},{8,10},{10,8},{12,14},{14,12},{16,18},{18,... | collective-permute-start | bytes 2764808 | tf_op jit(solution)/shard_map/ppermute | solution.py:357
  51.9 19.7 %collective-permute-start.13 = (bf16[3,240,640]{2,1,0:T(8,128)(2,1)S(1)}, bf16[3,240,640]{2,1,0:T(8,128)(2,1)S(1)}, u32[]{:S(2)}, u32[]{:S(2)}) collective-permute-start(bf16[3,240,640]{2,1,0:T(8,128)(2,1)S(1)} %gate.9.refs_3_), channel_id=1, source_target_pairs={{0,8},{8,16},{16,24},{24,28},{28,20},{20,12},{12,4},{4,0},{2,6},{1... | collective-permute-start | bytes 2764808 | tf_op jit(solution)/shard_map/ppermute | solution.py:330
  61.8 13.2 %collective-permute-start.12 = (bf16[3,240,640]{2,1,0:T(8,128)(2,1)S(1)}, bf16[3,240,640]{2,1,0:T(8,128)(2,1)S(1)}, u32[]{:S(2)}, u32[]{:S(2)}) collective-permute-start(bf16[3,240,640]{2,1,0:T(8,128)(2,1)S(1)} %gate.10.refs_3_), channel_id=1, source_target_pairs={{0,2},{2,0},{4,6},{6,4},{8,10},{10,8},{12,14},{14,12},{16,18},{18,... | collective-permute-start | bytes 2764808 | tf_op jit(solution)/shard_map/ppermute | solution.py:357
  61.8 19.7 %collective-permute-start.15 = (bf16[3,240,640]{2,1,0:T(8,128)(2,1)S(1)}, bf16[3,240,640]{2,1,0:T(8,128)(2,1)S(1)}, u32[]{:S(2)}, u32[]{:S(2)}) collective-permute-start(bf16[3,240,640]{2,1,0:T(8,128)(2,1)S(1)} %gate.10.refs_3_), channel_id=1, source_target_pairs={{0,8},{8,16},{16,24},{24,28},{28,20},{20,12},{12,4},{4,0},{2,6},{1... | collective-permute-start | bytes 2764808 | tf_op jit(solution)/shard_map/ppermute | solution.py:330
  71.7 9.9 %collective-permute-start.14 = (bf16[3,240,640]{2,1,0:T(8,128)(2,1)S(1)}, bf16[3,240,640]{2,1,0:T(8,128)(2,1)S(1)}, u32[]{:S(2)}, u32[]{:S(2)}) collective-permute-start(bf16[3,240,640]{2,1,0:T(8,128)(2,1)S(1)} %collective-permute-done.13.refs_3_), channel_id=1, source_target_pairs={{0,2},{2,0},{4,6},{6,4},{8,10},{10,8},{12,14},{14,12},{16,18},{18,... | collective-permute-start | bytes 2764808 | tf_op jit(solution)/shard_map/ppermute | solution.py:357
  81.6 3.4 %collective-permute-start.16 = (bf16[3,240,640]{2,1,0:T(8,128)(2,1)S(1)}, bf16[3,240,640]{2,1,0:T(8,128)(2,1)S(1)}, u32[]{:S(2)}, u32[]{:S(2)}) collective-permute-start(bf16[3,240,640]{2,1,0:T(8,128)(2,1)S(1)} %gate.11.refs_3_), channel_id=1, source_target_pairs={{0,2},{2,0},{4,6},{6,4},{8,10},{10,8},{12,14},{14,12},{16,18},{18,... | collective-permute-start | bytes 2764808 | tf_op jit(solution)/shard_map/ppermute | solution.py:357

commit v4 on v3

--- a/solution.py
+++ b/solution.py
@@ -69,7 +69,8 @@
     )(piece, *others)
 
 
-def act_kernel(emb_ref, out_ref):
+def act_kernel(emb_ref, *refs):
+    out_ref = refs[-1]
     v = emb_ref[...].astype(jnp.float32)
     act = (v / (1.0 + jnp.exp(-v))).astype(jnp.bfloat16)
     rows = out_ref.shape[2]
@@ -77,15 +78,15 @@
         out_ref[d] = act[:, d * rows : (d + 1) * rows]
 
 
-def act_call(emb, count):
+def act_call(emb, count, *after):
     return pl.pallas_call(
         act_kernel,
         out_shape=jax.ShapeDtypeStruct((count, 1, emb.shape[1] // count), jnp.bfloat16),
-        in_specs=[WHOLE],
+        in_specs=[WHOLE] + [ANY] * len(after),
         out_specs=WHOLE,
         compiler_params=pltpu.CompilerParams(vmem_limit_bytes=VMEM_BYTES),
         name="act_rows",
-    )(emb)
+    )(emb, *after)
 
 
 def emb_kernel(act_ref, w_ref, out_ref):
@@ -131,25 +132,6 @@
     )(h, params)
 
 
-def start_kernel(skip_ref, bias_ref, after_ref, out_ref):
-    del after_ref
-    outs = skip_ref.shape[0]
-    bias = jnp.broadcast_to(bias_ref[...], (128, outs)).T[:, 0:1]
-    out_ref[...] = skip_ref[...].astype(jnp.float32) + bias
-
-
-def start_call(skip, bias, after):
-    return pl.pallas_call(
-        start_kernel,
-        out_shape=jax.ShapeDtypeStruct(skip.shape, jnp.float32),
-        in_specs=[WHOLE, WHOLE, ANY],
-        out_specs=WHOLE,
-        compiler_params=pltpu.CompilerParams(vmem_limit_bytes=VMEM_BYTES),
-        cost_estimate=weight(0),
-        name="start_total",
-    )(skip, bias, after)
-
-
 def affine_kernel(size, terms_ref, table_ref, *refs):
     out_ref = refs[-1]
     rows = out_ref.shape[2]
@@ -188,35 +170,9 @@
         in_specs=[WHOLE, WHOLE] + [ANY] * len(after),
         out_specs=WHOLE,
         compiler_params=pltpu.CompilerParams(vmem_limit_bytes=VMEM_BYTES),
-        cost_estimate=weight(10),
+        cost_estimate=weight(5),
         name="affine",
     )(terms, table, *after)
-
-
-def norm_kernel(place_ref, ab_ref, *refs):
-    h_refs, out_ref = refs[:-1], refs[-1]
-    blocks = h_refs[0].shape[0]
-    for u in range(out_ref.shape[0]):
-        place = place_ref[u]
-        ab = ab_ref[place].T
-        h = h_refs[0][place % blocks]
-        for turn in range(1, len(h_refs)):
-            h = jnp.where(place // blocks == turn, h_refs[turn][place % blocks], h)
-        v = h.astype(jnp.float32) * ab[:, 0:1] + ab[:, 1:2]
-        half = 0.5 * v
-        out_ref[u] = (half + half * jnp.tanh(half)).astype(jnp.bfloat16)
-
-
-def norm_call(places, affine, slices):
-    return pl.pallas_call(
-        norm_kernel,
-        out_shape=jax.ShapeDtypeStruct(places.shape + slices[0].shape[1:], jnp.bfloat16),
-        in_specs=[pl.BlockSpec(memory_space=pltpu.SMEM)] + [WHOLE] * (1 + len(slices)),
-        out_specs=WHOLE,
-        compiler_params=pltpu.CompilerParams(vmem_limit_bytes=VMEM_BYTES),
-        cost_estimate=weight(0),
-        name="norm_units",
-    )(places, affine, *slices)
 
 
 def shifted(values, amount):
@@ -226,14 +182,46 @@
     return jnp.concatenate([edge, values[:, :amount]], axis=1)
 
 
-def conv_kernel(ids, last, *refs):
+def norm_kernel(units, chan, blocks_ref, ab_ref, *refs):
+    h_refs, out_ref = refs[:-1], refs[-1]
+    blocks = h_refs[0].shape[0]
+    me, side = lax.axis_index("dp"), lax.axis_index("chan")
+    for u in range(units):
+        block = blocks_ref[me * units + u]
+        turn, place = lax.rem(side - block // blocks + chan, chan), lax.rem(block, blocks)
+        ab = ab_ref[turn * blocks + place].T
+        h = h_refs[0][place]
+        for other in range(1, chan):
+            h = jnp.where(turn == other, h_refs[other][place], h)
+        v = h.astype(jnp.float32) * ab[:, 0:1] + ab[:, 1:2]
+        half = 0.5 * v
+        out_ref[u] = (half + half * jnp.tanh(half)).astype(jnp.bfloat16)
+
+
+def norm_call(blocks, affine, slices):
+    units, chan = blocks.shape[0], len(slices)
+    return pl.pallas_call(
+        functools.partial(norm_kernel, units, chan),
+        out_shape=jax.ShapeDtypeStruct((units,) + slices[0].shape[1:], jnp.bfloat16),
+        in_specs=[pl.BlockSpec(memory_space=pltpu.SMEM)] + [WHOLE] * (1 + chan),
+        out_specs=WHOLE,
+        compiler_params=pltpu.CompilerParams(vmem_limit_bytes=VMEM_BYTES),
+        cost_estimate=weight(0),
+        name="norm_units",
+    )(jnp.asarray(blocks.reshape(-1)), affine, *slices)
+
+
+def conv_kernel(ids, first, extra, last, *refs):
+    refs = list(refs)
     count = len(ids)
-    total_ref, normed_ref = refs[:2]
-    weight_refs = refs[2 : 2 + count]
-    out_ref, token_ref, even, odd, rounded, sem = refs[2 + count :]
+    total_ref = None if first else refs.pop(0)
+    normed_ref = refs.pop(0)
+    weight_refs = [refs.pop(0) for _ in range(count)]
+    skip_ref, table_ref = (refs.pop(0), refs.pop(0)) if extra else (None, None)
+    out_ref, token_ref, even, odd, rounded, sem = refs
     stacks = (even, odd)
     rows = normed_ref.shape[1]
-    outs = total_ref.shape[0]
+    outs = out_ref.shape[0]
     column = lax.broadcasted_iota(jnp.int32, (1, CELLS), 1) % WIDTH
     inside = [(column > 0).astype(jnp.bfloat16), None, (column < WIDTH - 1).astype(jnp.bfloat16)]
     token_ref[...] = jnp.zeros_like(token_ref)
@@ -257,8 +245,13 @@
         for u in range(count):
             if u + 1 < count:
                 build(u + 1)
-            source = total_ref if u == 0 else out_ref
-            out_ref[...] = source[...] + product(u, slice(0, outs))
+            part = product(u, slice(0, outs))
+            if u == 0 and extra:
+                bias = jnp.broadcast_to(table_ref[3:4, :], (128, outs)).T[:, 0:1]
+                part = part + (skip_ref[...].astype(jnp.float32) + bias)
+            if not (u == 0 and first):
+                part = part + (total_ref if u == 0 else out_ref)[...]
+            out_ref[...] = part
         return
     tile = 128 if outs % 128 == 0 else outs
     copies = []
@@ -272,18 +265,19 @@
         copy.wait()
 
 
-def conv_call(ids, total, normed, weights, last=False):
-    count = len(ids)
+def conv_call(ids, total, normed, weights, extra=(), last=False):
+    count, first = len(ids), total is None
     _, rows, _ = normed.shape
     outs = weights[0].shape[2]
     tiles = outs // 128 if outs % 128 == 0 else 1
-    return pl.pallas_call(
-        functools.partial(conv_kernel, tuple(ids), last),
+    operands = ([] if first else [total]) + [normed] + list(weights) + list(extra)
+    return pl.pallas_call(
+        functools.partial(conv_kernel, tuple(ids), first, bool(extra), last),
         out_shape=[
             jax.ShapeDtypeStruct((outs, CELLS), jnp.bfloat16 if last else jnp.float32),
             jax.ShapeDtypeStruct((8, 128), jnp.float32),
         ],
-        in_specs=[WHOLE] * (2 + count),
+        in_specs=[WHOLE] * len(operands),
         out_specs=[ANY if last else WHOLE, WHOLE],
         scratch_shapes=[
             pltpu.VMEM((9 * rows, CELLS), jnp.bfloat16),
@@ -291,10 +285,10 @@
             pltpu.VMEM((outs, CELLS) if last else (16, 128), jnp.bfloat16),
             pltpu.SemaphoreType.DMA((tiles,)),
         ],
-        input_output_aliases={} if last else {0: 0},
+        input_output_aliases={} if first or last else {0: 0},
         compiler_params=pltpu.CompilerParams(vmem_limit_bytes=VMEM_BYTES),
         name="conv_units",
-    )(total, normed, *weights)
+    )(*operands)
 
 
 def make_body(dp, chan):
@@ -311,8 +305,6 @@
         panel = h_in.shape[1]
         rows, outs = w_conv.shape[1], w_conv.shape[2]
         blocks = panel // rows
-        me = lax.axis_index("dp")
-        side = lax.axis_index("chan")
 
         own = w_conv.reshape(3, 3 * rows, outs)
         final = len(ring.hops) + 1
@@ -321,31 +313,27 @@
 
         slices = around(h_in.reshape(blocks, rows, CELLS))
 
-        block = lax.dynamic_slice(jnp.asarray(ring.blocks), (me, 0), (1, dp))[0]
-        places = ((side - block // blocks) % chan) * blocks + block % blocks
-
         def hop(i, *after):
             if after:
                 pieces[i - 2] = gate(pieces[i - 2], *after)
             pieces[i] = lax.ppermute(pieces[i - 2], "dp", ring.pairs)
 
-        act = act_call(emb, dp)
+        act = act_call(emb, dp, pieces[1])
         act_rows = lax.all_to_all(act, "dp", 0, 0, tiled=True)
         params = jnp.concatenate([b_emb, gn_gain, gn_bias, b_conv]).reshape(4, panel)
         table = stats_call(h_in[0], params)
         if final >= 3:
             hop(3, act)
         terms = emb_call(act_rows, w_emb)
-        total = start_call(skip[0], table[3:4], terms)
         if final >= 4:
             hop(4, terms)
         terms = lax.all_to_all(terms, "dp", 0, 0, tiled=True)
-        affine = affine_call(C // GROUPS, rows, terms, table, total, places, pieces[min(3, final)], *slices[1:])
+        affine = affine_call(C // GROUPS, rows, terms, table, pieces[min(3, final)])
         affine = jnp.concatenate(around(affine), axis=0)
         if final >= 5:
             hop(5)
 
-        normed = norm_call(places, affine, slices)
+        normed = norm_call(ring.blocks, affine, slices)
 
         units = [(0, own), (1, pieces[1])]
         tokens = []
@@ -356,19 +344,20 @@
         def swap(i):
             units.append((2 * i - 1, lax.ppermute(pieces[i], "dp", ring.core_pairs)))
 
-        def convolve(total, count, last=False):
+        def convolve(total, count, extra=(), last=False):
             here = [units.pop(0) for _ in range(min(count, len(units)))]
-            total, token = conv_call([u for u, _ in here], total, normed, [w for _, w in here], last)
+            total, token = conv_call([u for u, _ in here], total, normed, [w for _, w in here], extra, last)
             tokens.append(token)
             return total
 
+        total = None
         for i in range(2, min(final, 3) + 1):
             arrived(i)
             swap(i)
         if final >= 4:
             total = convolve(total, 4)
         for i in range(6, final + 1):
-            hop(i, tokens[-2] if len(tokens) > 1 else normed)
+            hop(i, ([normed, normed] + tokens)[i - 6])
             arrived(i - 2)
             total = convolve(total, 4)
             swap(i - 2)
@@ -376,16 +365,19 @@
             arrived(final - 1)
         while len(units) > 4:
             total = convolve(total, 4)
+        extra = (skip[0], table)
         if final >= 4:
-            total = convolve(total, len(units))
+            total = convolve(total, len(units), extra)
+            extra = ()
             if final >= 5:
                 swap(final - 1)
             pieces[final] = gate(pieces[final], tokens[-1])
             arrived(final)
             swap(final)
         while len(units) > 1:
-            total = convolve(total, min(4, len(units) - 1))
-        total = convolve(total, 1, last=True)
+            total = convolve(total, min(4, len(units) - 1), extra)
+            extra = ()
+        total = convolve(total, 1, extra, last=True)
         return total[None]
 
     return body

time: 88.7 us -> 83.4 us (0.940)
  Pallas kernels: 37.2 us -> 34 us
  waiting for transfers between devices: 18.8 us -> 21.6 us
  starting transfers between devices: 26.1 us -> 23.9 us
  local copies, waits for them, and re-layouts: 4.09 us -> 2.23 us
    pallas_call x9 -> x8, Pallas kernels: 32 us -> 29.6 us  [the longest x7 26.4 us: conv_call(): pl.pallas_call(functools.partial(conv_kernel, tuple(ids), first, bool(ext...]
    ppermute x6, starting transfers between devices: 10.2 us -> 8 us  [hop(): pieces[i] = lax.ppermute(pieces[i - 2], 'dp', ring.pairs)]
    unnamed x16 -> x14, local copies, waits for them, and re-layouts: 4.06 us -> 2.22 us
    ppermute x6, waiting for transfers between devices: 11.4 us -> 13.1 us  [hop(): pieces[i] = lax.ppermute(pieces[i - 2], 'dp', ring.pairs)]
    ppermute x2, starting transfers between devices: 4.25 us -> 3 us  [around(): values.append(lax.ppermute(values[-1], 'chan', chan_pairs))]
    ppermute x1, starting transfers between devices: 1.58 us -> 2.62 us  [body(): pieces[2] = lax.ppermute(own, 'dp', ring.pairs)]
  transfers between devices with their start and end apart: 19 -> 19, of which waited for: 7 -> 6; matrix products, arithmetic and copies ran while one was open for 2% -> 1% of each run, Pallas kernels for 39% -> 37%
where the time goes in v4:
time: 83.4 us; the launch traced here: 82.9 us
  Pallas kernels  34 us (41%)
  starting transfers between devices  23.9 us (29%)
  waiting for transfers between devices  21.6 us (26%)
  local copies, waits for them, and re-layouts  2.23 us (3%)
    pallas_call x7, Pallas kernels, conv_call(): pl.pallas_call(functools.partial(conv_kernel, tuple(ids), first, bool(ext...  26.4 us
    ppermute x6, waiting for transfers between devices, hop(): pieces[i] = lax.ppermute(pieces[i - 2], 'dp', ring.pairs)  13.1 us
    ppermute x6, starting transfers between devices, hop(): pieces[i] = lax.ppermute(pieces[i - 2], 'dp', ring.pairs)  8 us
    all_to_all x1, starting transfers between devices, body(): act_rows = lax.all_to_all(act, 'dp', 0, 0, tiled=True)  5.51 us
    all_to_all x1, waiting for transfers between devices, body(): act_rows = lax.all_to_all(act, 'dp', 0, 0, tiled=True)  4.19 us
    all_to_all x1, starting transfers between devices, body(): terms = lax.all_to_all(terms, 'dp', 0, 0, tiled=True)  3.5 us
    pallas_call x1, Pallas kernels, norm_call(): pl.pallas_call(functools.partial(norm_kernel, units, chan), out_shape=jax...  3.2 us
    ppermute x2, starting transfers between devices, around(): values.append(lax.ppermute(values[-1], 'chan', chan_pairs))  3 us
  transfers between devices with their start and end apart: 19, of which 6 were waited for; matrix products, arithmetic and copies ran while one was open for 1% of the time, Pallas kernels for 37%

profile of v4, /device:TPU:0, one launch (start us, length us, event | category | flops | bytes accessed | tf_op | source)
XLA Modules:
  0.0 82.9 jit_solution(11313622495530633400)
XLA Ops:
  0.0 0.5 collective-permute-start
  0.5 2.6 %collective-permute-start.4 = (bf16[3,240,640]{2,1,0:T(8,128)(2,1)}, bf16[3,240,640]{2,1,0:T(8,128)(2,1)S(1)}, u32[]{:S(2)}, u32[]{:S(2)}) collective-permute-start(bf16[3,240,640]{2,1,0:T(8,128)(2,1)} %bitcast.10), channel_id=1, source_target_pairs={{0,8},{8,16},{16,24},{24,28},{28,20},{20,12},{12,4},{4,0},{2,6},{1... | collective-permute-start | bytes 2764808 | tf_op jit(solution)/shard_map/ppermute | solution.py:312
  3.1 1.5 %collective-permute-start.3 = (bf16[8,80,1024]{2,1,0:T(8,128)(2,1)}, bf16[8,80,1024]{2,1,0:T(8,128)(2,1)}, u32[]{:S(2)}, u32[]{:S(2)}) collective-permute-start(bf16[8,80,1024]{2,1,0:T(8,128)(2,1)} %bitcast.6), channel_id=1, source_target_pairs={{0,1},{1,0},{2,3},{3,2},{4,5},{5,4},{6,7},{7,6},{8,9},{9,8},{10,11... | collective-permute-start | bytes 3932168 | tf_op jit(solution)/shard_map/ppermute | solution.py:301
  4.6 0.7 copy-done.5
  5.3 0.7 act_rows.1.refs_1_
  6.0 5.5 %all-to-all-start = ((bf16[16,1,80]{2,1,0:T(2,128)(2,1)}), bf16[16,1,80]{2,1,0:T(2,128)(2,1)S(1)}, u32[]{:S(2)}, u32[]{:S(2)}) async-start(bf16[16,1,80]{2,1,0:T(2,128)(2,1)} %act_rows.1.refs_1_), calls=%async_computation | async-start | bytes 16384 | tf_op jit(solution)/shard_map/all_to_all | solution.py:322
  11.5 0.7 pad_maximum_fusion.1
  12.2 2.0 %collective-permute-start.1 = (bf16[3,240,640]{2,1,0:T(8,128)(2,1)S(1)}, bf16[3,240,640]{2,1,0:T(8,128)(2,1)}, u32[]{:S(2)}, u32[]{:S(2)}) collective-permute-start(bf16[3,240,640]{2,1,0:T(8,128)(2,1)S(1)} %gate.6.refs_2_), channel_id=1, source_target_pairs={{0,8},{8,16},{16,24},{24,28},{28,20},{20,12},{12,4},{4,0},{2,6},{1... | collective-permute-start | bytes 2764808 | tf_op jit(solution)/shard_map/ppermute | solution.py:319
  14.2 4.2 %all-to-all-done.act_ref = bf16[16,1,80]{2,1,0:T(2,128)(2,1)S(1)} async-done(((bf16[16,1,80]{2,1,0:T(2,128)(2,1)}), bf16[16,1,80]{2,1,0:T(2,128)(2,1)S(1)}, u32[]{:S(2)}, u32[]{:S(2)}) %all-to-all-start) | async-done | bytes 2592 | tf_op jit(solution)/shard_map/all_to_all | solution.py:322
  18.4 0.8 emb_terms.1.refs_1_
  19.2 3.5 %all-to-all-start.1 = ((f32[16,1,640]{2,1,0:T(1,128)}), f32[16,1,640]{2,1,0:T(1,128)S(1)}, u32[]{:S(2)}, u32[]{:S(2)}) async-start(f32[16,1,640]{2,1,0:T(1,128)} %emb_terms.1.refs_1_), calls=%async_computation.1 | async-start | bytes 81920 | tf_op jit(solution)/shard_map/all_to_all | solution.py:330
  22.7 1.9 %collective-permute-start.7 = (bf16[3,240,640]{2,1,0:T(8,128)(2,1)S(1)}, bf16[3,240,640]{2,1,0:T(8,128)(2,1)S(1)}, u32[]{:S(2)}, u32[]{:S(2)}) collective-permute-start(bf16[3,240,640]{2,1,0:T(8,128)(2,1)S(1)} %gate.7.refs_3_), channel_id=1, source_target_pairs={{0,8},{8,16},{16,24},{24,28},{28,20},{20,12},{12,4},{4,0},{2,6},{1... | collective-permute-start | bytes 2764808 | tf_op jit(solution)/shard_map/ppermute | solution.py:319
  24.6 1.3 %copy-done.1 = bf16[1,640,1024]{2,1,0:T(8,128)(2,1)S(1)} copy-done((bf16[1,640,1024]{2,1,0:T(8,128)(2,1)S(1)}, bf16[1,640,1024]{2,1,0:T(8,128)(2,1)}, u32[]{:S(2)}) %copy-start.1) | copy-done | bytes 1310744
  25.9 1.2 %channel_stats.1.table_ref.refs_5_ = f32[6,640]{1,0:T(8,128)S(1)} custom-call(bf16[640,1024]{1,0:T(8,128)(2,1)S(1)} %bitcast.7, f32[4,640]{1,0:T(4,128)S(1)} %reshape.10.params_ref), custom_call_target="tpu_custom_call" | custom-call | flops 10000000000 | bytes 40000000 | tf_op jit(solution)/shard_map/channel_stats/pallas_call | solution.py:124
  27.1 2.5 %all-to-all-done.1.terms_ref = f32[16,1,640]{2,1,0:T(1,128)S(1)} async-done(((f32[16,1,640]{2,1,0:T(1,128)}), f32[16,1,640]{2,1,0:T(1,128)S(1)}, u32[]{:S(2)}, u32[]{:S(2)}) %all-to-all-start.1) | async-done | bytes 40992 | tf_op jit(solution)/shard_map/all_to_all | solution.py:330
  29.6 1.8 %affine.1 = f32[8,2,80]{2,1,0:T(2,128)S(1)} custom-call(f32[16,1,640]{2,1,0:T(1,128)S(1)} %all-to-all-done.1.terms_ref, f32[6,640]{1,0:T(8,128)S(1)} %channel_stats.1.table_ref.refs_5_, bf16[3,240,640]{2,1,0:T(8,128)(2,1)} %collective-permute-done.1.refs_0_.refs_2_), custom_call_target="tpu_custom_call" | custom-call | flops 5000000000 | bytes 20000000 | tf_op jit(solution)/shard_map/affine/pallas_call | solution.py:167
  31.4 1.5 %collective-permute-start.2 = (f32[8,2,80]{2,1,0:T(2,128)S(1)}, f32[8,2,80]{2,1,0:T(2,128)S(1)}, u32[]{:S(2)}, u32[]{:S(2)}) collective-permute-start(f32[8,2,80]{2,1,0:T(2,128)S(1)} %affine.1), channel_id=1, source_target_pairs={{0,1},{1,0},{2,3},{3,2},{4,5},{5,4},{6,7},{7,6},{8,9},{9,8},{10,11... | collective-permute-start | bytes 15368 | tf_op jit(solution)/shard_map/ppermute | solution.py:301
  33.3 1.8 %collective-permute-done.2 = f32[8,2,80]{2,1,0:T(2,128)S(1)} collective-permute-done((f32[8,2,80]{2,1,0:T(2,128)S(1)}, f32[8,2,80]{2,1,0:T(2,128)S(1)}, u32[]{:S(2)}, u32[]{:S(2)}) %collective-permute-start.2) | collective-permute-done | bytes 5152 | tf_op jit(solution)/shard_map/ppermute | solution.py:301
  35.1 3.2 %norm_units.1.refs_0_.refs_1_ = bf16[16,80,1024]{2,1,0:T(8,128)(2,1)S(1)} custom-call(s32[256]{0:T(256)S(1)} %copy-done.6, f32[16,2,80]{2,1,0:T(2,128)S(1)} %pad_maximum_fusion.ab_ref, bf16[8,80,1024]{2,1,0:T(8,128)(2,1)S(1)} %bitcast.8, bf16[8,80,1024]{2,1,0:T(8,128)(2,1)} %collective-permute-done.3.refs_1_), custom_call_target="tpu_custom_call" | custom-call | tf_op jit(solution)/shard_map/norm_units/pallas_call | solution.py:203
  38.8 0.5 collective-permute-start.8
  39.5 4.7 %conv_units.7 = (f32[640,1024]{1,0:T(8,128)S(1)}, f32[8,128]{1,0:T(8,128)S(1)}) custom-call(bf16[16,80,1024]{2,1,0:T(8,128)(2,1)S(1)} %norm_units.1.refs_0_.refs_1_, bf16[3,240,640]{2,1,0:T(8,128)(2,1)S(1)} %bitcast.11, bf16[3,240,640]{2,1,0:T(8,128)(2,1)S(1)} %gate.6.refs_2_, bf16[3,240,640]{2,1,0:T(8,128)(2,1)S(1)} %gate.7.refs_3_, ...), custom_call_target="tpu_custom_call" | custom-call | tf_op jit(solution)/shard_map/conv_units/pallas_call | solution.py:274
  44.1 2.4 %collective-permute-done.9.refs_0_ = bf16[3,240,640]{2,1,0:T(8,128)(2,1)S(1)} collective-permute-done((bf16[3,240,640]{2,1,0:T(8,128)(2,1)}, bf16[3,240,640]{2,1,0:T(8,128)(2,1)S(1)}, u32[]{:S(2)}, u32[]{:S(2)}) %collective-permute-start.9) | collective-permute-done | bytes 921632 | tf_op jit(solution)/shard_map/ppermute | solution.py:319
  46.5 1.5 %collective-permute-start.13 = (bf16[3,240,640]{2,1,0:T(8,128)(2,1)S(1)}, bf16[3,240,640]{2,1,0:T(8,128)(2,1)S(1)}, u32[]{:S(2)}, u32[]{:S(2)}) collective-permute-start(bf16[3,240,640]{2,1,0:T(8,128)(2,1)S(1)} %gate.9.refs_3_), channel_id=1, source_target_pairs={{0,8},{8,16},{16,24},{24,28},{28,20},{20,12},{12,4},{4,0},{2,6},{1... | collective-permute-start | bytes 2764808 | tf_op jit(solution)/shard_map/ppermute | solution.py:319
  48.1 8.3 %collective-permute-done.11.refs_0_ = bf16[3,240,640]{2,1,0:T(8,128)(2,1)S(1)} collective-permute-done((bf16[3,240,640]{2,1,0:T(8,128)(2,1)S(1)}, bf16[3,240,640]{2,1,0:T(8,128)(2,1)S(1)}, u32[]{:S(2)}, u32[]{:S(2)}) %collective-permute-start.11) | collective-permute-done | bytes 921632 | tf_op jit(solution)/shard_map/ppermute | solution.py:319
  56.4 1.8 %collective-permute-start.15 = (bf16[3,240,640]{2,1,0:T(8,128)(2,1)S(1)}, bf16[3,240,640]{2,1,0:T(8,128)(2,1)S(1)}, u32[]{:S(2)}, u32[]{:S(2)}) collective-permute-start(bf16[3,240,640]{2,1,0:T(8,128)(2,1)S(1)} %gate.10.refs_3_), channel_id=1, source_target_pairs={{0,8},{8,16},{16,24},{24,28},{28,20},{20,12},{12,4},{4,0},{2,6},{1... | collective-permute-start | bytes 2764808 | tf_op jit(solution)/shard_map/ppermute | solution.py:319
  58.2 5.2 %conv_units.8 = (f32[640,1024]{1,0:T(8,128)S(1)}, f32[8,128]{1,0:T(8,128)}) custom-call(f32[640,1024]{1,0:T(8,128)S(1)} %get-tuple-element.14.refs_0_, bf16[16,80,1024]{2,1,0:T(8,128)(2,1)S(1)} %norm_units.1.refs_0_.refs_1_, bf16[3,240,640]{2,1,0:T(8,128)(2,1)} %collective-permute-done.1.refs_0_.refs_2_, ...), custom_call_target="tpu_custom_call", output_to_operand_aliasing={{0}: (0, {})} | custom-call | tf_op jit(solution)/shard_map/conv_units/pallas_call | solution.py:274
  63.4 3.4 %conv_units.9 = (f32[640,1024]{1,0:T(8,128)S(1)}, f32[8,128]{1,0:T(8,128)}) custom-call(f32[640,1024]{1,0:T(8,128)S(1)} %get-tuple-element.15.refs_0_, bf16[16,80,1024]{2,1,0:T(8,128)(2,1)S(1)} %norm_units.1.refs_0_.refs_1_, bf16[3,240,640]{2,1,0:T(8,128)(2,1)S(1)} %collective-permute-done.8.refs_2_, ...), custom_call_target="tpu_custom_call", output_to_operand_aliasing={{0}: (0, {})} | custom-call | tf_op jit(solution)/shard_map/conv_units/pallas_call | solution.py:274
  67.1 3.4 %conv_units.10 = (f32[640,1024]{1,0:T(8,128)S(1)}, f32[8,128]{1,0:T(8,128)}) custom-call(f32[640,1024]{1,0:T(8,128)S(1)} %get-tuple-element.16.refs_0_, bf16[16,80,1024]{2,1,0:T(8,128)(2,1)S(1)} %norm_units.1.refs_0_.refs_1_, bf16[3,240,640]{2,1,0:T(8,128)(2,1)S(1)} %collective-permute-done.10.refs_2_, ...), custom_call_target="tpu_custom_call", output_to_operand_aliasing={{0}: (0, {})} | custom-call | tf_op jit(solution)/shard_map/conv_units/pallas_call | solution.py:274
  70.5 3.2 %conv_units.11 = (f32[640,1024]{1,0:T(8,128)S(1)}, f32[8,128]{1,0:T(8,128)S(1)}) custom-call(f32[640,1024]{1,0:T(8,128)S(1)} %get-tuple-element.18.refs_0_, bf16[16,80,1024]{2,1,0:T(8,128)(2,1)S(1)} %norm_units.1.refs_0_.refs_1_, bf16[3,240,640]{2,1,0:T(8,128)(2,1)S(1)} %collective-permute-done.12.refs_2_, ...), custom_call_target="tpu_custom_call", output_to_operand_aliasing={{0}: (0, {})} | custom-call | tf_op jit(solution)/shard_map/conv_units/pallas_call | solution.py:274
  73.7 2.4 %collective-permute-done.15.refs_0_ = bf16[3,240,640]{2,1,0:T(8,128)(2,1)S(1)} collective-permute-done((bf16[3,240,640]{2,1,0:T(8,128)(2,1)S(1)}, bf16[3,240,640]{2,1,0:T(8,128)(2,1)S(1)}, u32[]{:S(2)}, u32[]{:S(2)}) %collective-permute-start.15) | collective-permute-done | bytes 921632 | tf_op jit(solution)/shard_map/ppermute | solution.py:319
  76.1 3.6 %conv_units.12 = (f32[640,1024]{1,0:T(8,128)S(1)}, f32[8,128]{1,0:T(8,128)}) custom-call(f32[640,1024]{1,0:T(8,128)S(1)} %get-tuple-element.19.refs_0_, bf16[16,80,1024]{2,1,0:T(8,128)(2,1)S(1)} %norm_units.1.refs_0_.refs_1_, bf16[3,240,640]{2,1,0:T(8,128)(2,1)S(1)} %collective-permute-done.14.refs_2_, ...), custom_call_target="tpu_custom_call", output_to_operand_aliasing={{0}: (0, {})} | custom-call | tf_op jit(solution)/shard_map/conv_units/pallas_call | solution.py:274
  79.8 3.0 %conv_units.13 = (bf16[640,1024]{1,0:T(8,128)(2,1)}, f32[8,128]{1,0:T(8,128)}) custom-call(f32[640,1024]{1,0:T(8,128)S(1)} %get-tuple-element.21.refs_0_, bf16[16,80,1024]{2,1,0:T(8,128)(2,1)S(1)} %norm_units.1.refs_0_.refs_1_, bf16[3,240,640]{2,1,0:T(8,128)(2,1)S(1)} %collective-permute-done.16.refs_2_), custom_call_target="tpu_custom_call" | custom-call | tf_op jit(solution)/shard_map/conv_units/pallas_call | solution.py:274
  (41 shorter events, 1.5 us)
Async XLA Ops:
  0.0 18.4 %copy-start.4 = (bf16[80,640]{1,0:T(8,128)(2,1)S(1)}, bf16[80,640]{1,0:T(8,128)(2,1)}, u32[]{:S(2)}) copy-start(bf16[80,640]{1,0:T(8,128)(2,1)} %w_ref.1) | copy-start | bytes 307204
  0.0 4.6 %collective-permute-start = (bf16[3,240,640]{2,1,0:T(8,128)(2,1)}, bf16[3,240,640]{2,1,0:T(8,128)(2,1)S(1)}, u32[]{:S(2)}, u32[]{:S(2)}) collective-permute-start(bf16[3,240,640]{2,1,0:T(8,128)(2,1)} %bitcast.9), channel_id=1, source_target_pairs={{0,2},{2,0},{4,6},{6,4},{8,10},{10,8},{12,14},{14,12},{16,18},{18,... | collective-permute-start | bytes 2764808 | tf_op jit(solution)/shard_map/ppermute | solution.py:311
  0.5 22.2 %collective-permute-start.4 = (bf16[3,240,640]{2,1,0:T(8,128)(2,1)}, bf16[3,240,640]{2,1,0:T(8,128)(2,1)S(1)}, u32[]{:S(2)}, u32[]{:S(2)}) collective-permute-start(bf16[3,240,640]{2,1,0:T(8,128)(2,1)} %bitcast.10), channel_id=1, source_target_pairs={{0,8},{8,16},{16,24},{24,28},{28,20},{20,12},{12,4},{4,0},{2,6},{1... | collective-permute-start | bytes 2764808 | tf_op jit(solution)/shard_map/ppermute | solution.py:312
  3.1 32.0 %collective-permute-start.3 = (bf16[8,80,1024]{2,1,0:T(8,128)(2,1)}, bf16[8,80,1024]{2,1,0:T(8,128)(2,1)}, u32[]{:S(2)}, u32[]{:S(2)}) collective-permute-start(bf16[8,80,1024]{2,1,0:T(8,128)(2,1)} %bitcast.6), channel_id=1, source_target_pairs={{0,1},{1,0},{2,3},{3,2},{4,5},{5,4},{6,7},{7,6},{8,9},{9,8},{10,11... | collective-permute-start | bytes 3932168 | tf_op jit(solution)/shard_map/ppermute | solution.py:301
  4.6 0.7 copy-start.5
  6.0 12.4 %all-to-all-start = ((bf16[16,1,80]{2,1,0:T(2,128)(2,1)}), bf16[16,1,80]{2,1,0:T(2,128)(2,1)S(1)}, u32[]{:S(2)}, u32[]{:S(2)}) async-start(bf16[16,1,80]{2,1,0:T(2,128)(2,1)} %act_rows.1.refs_1_), calls=%async_computation | async-start | bytes 16384 | tf_op jit(solution)/shard_map/all_to_all | solution.py:322
  12.2 17.3 %collective-permute-start.1 = (bf16[3,240,640]{2,1,0:T(8,128)(2,1)S(1)}, bf16[3,240,640]{2,1,0:T(8,128)(2,1)}, u32[]{:S(2)}, u32[]{:S(2)}) collective-permute-start(bf16[3,240,640]{2,1,0:T(8,128)(2,1)S(1)} %gate.6.refs_2_), channel_id=1, source_target_pairs={{0,8},{8,16},{16,24},{24,28},{28,20},{20,12},{12,4},{4,0},{2,6},{1... | collective-permute-start | bytes 2764808 | tf_op jit(solution)/shard_map/ppermute | solution.py:319
  19.2 10.4 %all-to-all-start.1 = ((f32[16,1,640]{2,1,0:T(1,128)}), f32[16,1,640]{2,1,0:T(1,128)S(1)}, u32[]{:S(2)}, u32[]{:S(2)}) async-start(f32[16,1,640]{2,1,0:T(1,128)} %emb_terms.1.refs_1_), calls=%async_computation.1 | async-start | bytes 81920 | tf_op jit(solution)/shard_map/all_to_all | solution.py:330
  22.7 15.6 %collective-permute-start.7 = (bf16[3,240,640]{2,1,0:T(8,128)(2,1)S(1)}, bf16[3,240,640]{2,1,0:T(8,128)(2,1)S(1)}, u32[]{:S(2)}, u32[]{:S(2)}) collective-permute-start(bf16[3,240,640]{2,1,0:T(8,128)(2,1)S(1)} %gate.7.refs_3_), channel_id=1, source_target_pairs={{0,8},{8,16},{16,24},{24,28},{28,20},{20,12},{12,4},{4,0},{2,6},{1... | collective-permute-start | bytes 2764808 | tf_op jit(solution)/shard_map/ppermute | solution.py:319
  24.6 1.3 %copy-start.1 = (bf16[1,640,1024]{2,1,0:T(8,128)(2,1)S(1)}, bf16[1,640,1024]{2,1,0:T(8,128)(2,1)}, u32[]{:S(2)}) copy-start(bf16[1,640,1024]{2,1,0:T(8,128)(2,1)} %param.10) | copy-start | bytes 3932164
  27.1 8.0 %copy-start.6 = (s32[256]{0:T(256)S(1)}, s32[256]{0:T(256)}, u32[]{:S(2)}) copy-start(s32[256]{0:T(256)} %constant.2.clone.blocks_ref) | copy-start | bytes 3076
  29.6 5.5 %copy-start.2 = (bf16[1,640,1024]{2,1,0:T(8,128)(2,1)S(1)}, bf16[1,640,1024]{2,1,0:T(8,128)(2,1)}, u32[]{:S(2)}) copy-start(bf16[1,640,1024]{2,1,0:T(8,128)(2,1)} %param.10) | copy-start | bytes 3932164
  31.4 3.7 %collective-permute-start.2 = (f32[8,2,80]{2,1,0:T(2,128)S(1)}, f32[8,2,80]{2,1,0:T(2,128)S(1)}, u32[]{:S(2)}, u32[]{:S(2)}) collective-permute-start(f32[8,2,80]{2,1,0:T(2,128)S(1)} %affine.1), channel_id=1, source_target_pairs={{0,1},{1,0},{2,3},{3,2},{4,5},{5,4},{6,7},{7,6},{8,9},{9,8},{10,11... | collective-permute-start | bytes 15368 | tf_op jit(solution)/shard_map/ppermute | solution.py:301
  32.9 6.4 %collective-permute-start.5 = (bf16[3,240,640]{2,1,0:T(8,128)(2,1)S(1)}, bf16[3,240,640]{2,1,0:T(8,128)(2,1)S(1)}, u32[]{:S(2)}, u32[]{:S(2)}) collective-permute-start(bf16[3,240,640]{2,1,0:T(8,128)(2,1)S(1)} %gate.7.refs_3_), channel_id=1, source_target_pairs={{0,2},{2,0},{4,6},{6,4},{8,10},{10,8},{12,14},{14,12},{16,18},{18,... | collective-permute-start | bytes 2764808 | tf_op jit(solution)/shard_map/ppermute | solution.py:345
  32.9 13.6 %collective-permute-start.9 = (bf16[3,240,640]{2,1,0:T(8,128)(2,1)}, bf16[3,240,640]{2,1,0:T(8,128)(2,1)S(1)}, u32[]{:S(2)}, u32[]{:S(2)}) collective-permute-start(bf16[3,240,640]{2,1,0:T(8,128)(2,1)} %collective-permute-done.1.refs_0_.refs_2_), channel_id=1, source_target_pairs={{0,8},{8,16},{16,24},{24,28},{28,20},{20,12},{12,4},{4,0},{2,6},{1... | collective-permute-start | bytes 2764808 | tf_op jit(solution)/shard_map/ppermute | solution.py:319
  38.3 1.2 %copy-start.3 = (bf16[9,80,640]{2,1,0:T(8,128)(2,1)S(1)}, bf16[9,80,640]{2,1,0:T(8,128)(2,1)}, u32[]{:S(2)}) copy-start(bf16[9,80,640]{2,1,0:T(8,128)(2,1)} %param.17) | copy-start | bytes 2764804
  38.3 18.1 %collective-permute-start.11 = (bf16[3,240,640]{2,1,0:T(8,128)(2,1)S(1)}, bf16[3,240,640]{2,1,0:T(8,128)(2,1)S(1)}, u32[]{:S(2)}, u32[]{:S(2)}) collective-permute-start(bf16[3,240,640]{2,1,0:T(8,128)(2,1)S(1)} %gate.8.refs_4_), channel_id=1, source_target_pairs={{0,8},{8,16},{16,24},{24,28},{28,20},{20,12},{12,4},{4,0},{2,6},{1... | collective-permute-start | bytes 2764808 | tf_op jit(solution)/shard_map/ppermute | solution.py:319
  38.7 17.7 %collective-permute-start.6 = (bf16[3,240,640]{2,1,0:T(8,128)(2,1)}, bf16[3,240,640]{2,1,0:T(8,128)(2,1)S(1)}, u32[]{:S(2)}, u32[]{:S(2)}) collective-permute-start(bf16[3,240,640]{2,1,0:T(8,128)(2,1)} %collective-permute-done.1.refs_0_.refs_2_), channel_id=1, source_target_pairs={{0,2},{2,0},{4,6},{6,4},{8,10},{10,8},{12,14},{14,12},{16,18},{18,... | collective-permute-start | bytes 2764808 | tf_op jit(solution)/shard_map/ppermute | solution.py:345
  38.8 24.6 %collective-permute-start.8 = (bf16[3,240,640]{2,1,0:T(8,128)(2,1)S(1)}, bf16[3,240,640]{2,1,0:T(8,128)(2,1)S(1)}, u32[]{:S(2)}, u32[]{:S(2)}) collective-permute-start(bf16[3,240,640]{2,1,0:T(8,128)(2,1)S(1)} %gate.8.refs_4_), channel_id=1, source_target_pairs={{0,2},{2,0},{4,6},{6,4},{8,10},{10,8},{12,14},{14,12},{16,18},{18,... | collective-permute-start | bytes 2764808 | tf_op jit(solution)/shard_map/ppermute | solution.py:345
  46.5 20.2 %collective-permute-start.13 = (bf16[3,240,640]{2,1,0:T(8,128)(2,1)S(1)}, bf16[3,240,640]{2,1,0:T(8,128)(2,1)S(1)}, u32[]{:S(2)}, u32[]{:S(2)}) collective-permute-start(bf16[3,240,640]{2,1,0:T(8,128)(2,1)S(1)} %gate.9.refs_3_), channel_id=1, source_target_pairs={{0,8},{8,16},{16,24},{24,28},{28,20},{20,12},{12,4},{4,0},{2,6},{1... | collective-permute-start | bytes 2764808 | tf_op jit(solution)/shard_map/ppermute | solution.py:319
  48.1 19.0 %collective-permute-start.10 = (bf16[3,240,640]{2,1,0:T(8,128)(2,1)S(1)}, bf16[3,240,640]{2,1,0:T(8,128)(2,1)S(1)}, u32[]{:S(2)}, u32[]{:S(2)}) collective-permute-start(bf16[3,240,640]{2,1,0:T(8,128)(2,1)S(1)} %gate.9.refs_3_), channel_id=1, source_target_pairs={{0,2},{2,0},{4,6},{6,4},{8,10},{10,8},{12,14},{14,12},{16,18},{18,... | collective-permute-start | bytes 2764808 | tf_op jit(solution)/shard_map/ppermute | solution.py:345
  56.4 14.1 %collective-permute-start.12 = (bf16[3,240,640]{2,1,0:T(8,128)(2,1)S(1)}, bf16[3,240,640]{2,1,0:T(8,128)(2,1)S(1)}, u32[]{:S(2)}, u32[]{:S(2)}) collective-permute-start(bf16[3,240,640]{2,1,0:T(8,128)(2,1)S(1)} %gate.10.refs_3_), channel_id=1, source_target_pairs={{0,2},{2,0},{4,6},{6,4},{8,10},{10,8},{12,14},{14,12},{16,18},{18,... | collective-permute-start | bytes 2764808 | tf_op jit(solution)/shard_map/ppermute | solution.py:345
  56.4 19.7 %collective-permute-start.15 = (bf16[3,240,640]{2,1,0:T(8,128)(2,1)S(1)}, bf16[3,240,640]{2,1,0:T(8,128)(2,1)S(1)}, u32[]{:S(2)}, u32[]{:S(2)}) collective-permute-start(bf16[3,240,640]{2,1,0:T(8,128)(2,1)S(1)} %gate.10.refs_3_), channel_id=1, source_target_pairs={{0,8},{8,16},{16,24},{24,28},{28,20},{20,12},{12,4},{4,0},{2,6},{1... | collective-permute-start | bytes 2764808 | tf_op jit(solution)/shard_map/ppermute | solution.py:319
  66.8 9.4 %collective-permute-start.14 = (bf16[3,240,640]{2,1,0:T(8,128)(2,1)S(1)}, bf16[3,240,640]{2,1,0:T(8,128)(2,1)S(1)}, u32[]{:S(2)}, u32[]{:S(2)}) collective-permute-start(bf16[3,240,640]{2,1,0:T(8,128)(2,1)S(1)} %collective-permute-done.13.refs_3_), channel_id=1, source_target_pairs={{0,2},{2,0},{4,6},{6,4},{8,10},{10,8},{12,14},{14,12},{16,18},{18,... | collective-permute-start | bytes 2764808 | tf_op jit(solution)/shard_map/ppermute | solution.py:345
  67.1 3.4 %copy-start = (bf16[1,640,1024]{2,1,0:T(8,128)(2,1)S(1)}, bf16[1,640,1024]{2,1,0:T(8,128)(2,1)}, u32[]{:S(2)}) copy-start(bf16[1,640,1024]{2,1,0:T(8,128)(2,1)} %param.11) | copy-start | bytes 3932164
  76.1 3.6 %collective-permute-start.16 = (bf16[3,240,640]{2,1,0:T(8,128)(2,1)S(1)}, bf16[3,240,640]{2,1,0:T(8,128)(2,1)S(1)}, u32[]{:S(2)}, u32[]{:S(2)}) collective-permute-start(bf16[3,240,640]{2,1,0:T(8,128)(2,1)S(1)} %gate.11.refs_3_), channel_id=1, source_target_pairs={{0,2},{2,0},{4,6},{6,4},{8,10},{10,8},{12,14},{14,12},{16,18},{18,... | collective-permute-start | bytes 2764808 | tf_op jit(solution)/shard_map/ppermute | solution.py:345

commit v5 on v4

--- a/solution.py
+++ b/solution.py
@@ -170,7 +170,7 @@
         in_specs=[WHOLE, WHOLE] + [ANY] * len(after),
         out_specs=WHOLE,
         compiler_params=pltpu.CompilerParams(vmem_limit_bytes=VMEM_BYTES),
-        cost_estimate=weight(5),
+        cost_estimate=weight(7),
         name="affine",
     )(terms, table, *after)
 
@@ -211,9 +211,9 @@
     )(jnp.asarray(blocks.reshape(-1)), affine, *slices)
 
 
-def conv_kernel(ids, first, extra, last, *refs):
+def conv_kernel(parts, first, extra, last, *refs):
     refs = list(refs)
-    count = len(ids)
+    count = len(parts)
     total_ref = None if first else refs.pop(0)
     normed_ref = refs.pop(0)
     weight_refs = [refs.pop(0) for _ in range(count)]
@@ -227,17 +227,19 @@
     token_ref[...] = jnp.zeros_like(token_ref)
 
     def build(u):
-        normed = normed_ref[ids[u]]
+        unit, taps = parts[u]
+        normed = normed_ref[unit]
         for dx in range(3):
             moved = normed if dx == 1 else shifted(normed, dx - 1) * inside[dx]
-            for dy in range(3):
-                row = (3 * dy + dx) * rows
+            for dy in taps:
+                row = (3 * (dy - taps[0]) + dx) * rows
                 stacks[u % 2][row : row + rows, :] = moved if dy == 1 else shifted(moved, WIDTH * (dy - 1))
 
     def product(u, here):
-        weights = weight_refs[u][:, :, here].reshape(9 * rows, here.stop - here.start)
+        depth = 3 * len(parts[u][1]) * rows
+        weights = weight_refs[u][:, :, here].reshape(depth, here.stop - here.start)
         return lax.dot_general(
-            weights, stacks[u % 2][...], (((0,), (0,)), ((), ())), preferred_element_type=jnp.float32
+            weights, stacks[u % 2][:depth, :], (((0,), (0,)), ((), ())), preferred_element_type=jnp.float32
         )
 
     build(0)
@@ -265,14 +267,14 @@
         copy.wait()
 
 
-def conv_call(ids, total, normed, weights, extra=(), last=False):
-    count, first = len(ids), total is None
+def conv_call(parts, total, normed, weights, extra=(), last=False):
+    first = total is None
     _, rows, _ = normed.shape
     outs = weights[0].shape[2]
     tiles = outs // 128 if outs % 128 == 0 else 1
     operands = ([] if first else [total]) + [normed] + list(weights) + list(extra)
     return pl.pallas_call(
-        functools.partial(conv_kernel, tuple(ids), first, bool(extra), last),
+        functools.partial(conv_kernel, tuple(parts), first, bool(extra), last),
         out_shape=[
             jax.ShapeDtypeStruct((outs, CELLS), jnp.bfloat16 if last else jnp.float32),
             jax.ShapeDtypeStruct((8, 128), jnp.float32),
@@ -335,18 +337,22 @@
 
         normed = norm_call(ring.blocks, affine, slices)
 
-        units = [(0, own), (1, pieces[1])]
+        taps = tuple(range(3))
+        units = [((0, taps), own), ((1, taps), pieces[1])]
         tokens = []
 
+        def swapped(piece):
+            return lax.ppermute(piece, "dp", ring.core_pairs)
+
         def arrived(i):
-            units.append((2 * i - 2, pieces[i]))
+            units.append(((2 * i - 2, taps), pieces[i]))
 
         def swap(i):
-            units.append((2 * i - 1, lax.ppermute(pieces[i], "dp", ring.core_pairs)))
+            units.append(((2 * i - 1, taps), swapped(pieces[i])))
 
         def convolve(total, count, extra=(), last=False):
             here = [units.pop(0) for _ in range(min(count, len(units)))]
-            total, token = conv_call([u for u, _ in here], total, normed, [w for _, w in here], extra, last)
+            total, token = conv_call([p for p, _ in here], total, normed, [w for _, w in here], extra, last)
             tokens.append(token)
             return total
 
@@ -357,23 +363,39 @@
         if final >= 4:
             total = convolve(total, 4)
         for i in range(6, final + 1):
-            hop(i, ([normed, normed] + tokens)[i - 6])
+            after = ([normed] + tokens)[i - 6]
+            if i < final:
+                hop(i, after)
+            else:
+                pieces[i - 2] = gate(pieces[i - 2], after)
+                tail = [
+                    (rows_of_taps, lax.ppermute(pieces[i - 2][rows_of_taps[0] : rows_of_taps[-1] + 1], "dp", ring.pairs))
+                    for rows_of_taps in (taps[:2], taps[2:])
+                ]
             arrived(i - 2)
             total = convolve(total, 4)
             swap(i - 2)
-        if final >= 5:
+        if final >= 6:
+            pieces[final - 1] = gate(pieces[final - 1], tokens[-1])
             arrived(final - 1)
+        else:
+            tail = []
+            for i in range(4, final + 1):
+                arrived(i)
+                swap(i)
         while len(units) > 4:
             total = convolve(total, 4)
         extra = (skip[0], table)
-        if final >= 4:
+        if tail:
             total = convolve(total, len(units), extra)
             extra = ()
-            if final >= 5:
-                swap(final - 1)
-            pieces[final] = gate(pieces[final], tokens[-1])
-            arrived(final)
-            swap(final)
+            swap(final - 1)
+        for rows_of_taps, piece in tail:
+            piece = gate(piece, tokens[-1])
+            units.append(((2 * final - 2, rows_of_taps), piece))
+            moving = ((2 * final - 1, rows_of_taps), swapped(piece))
+            total = convolve(total, len(units))
+            units.append(moving)
         while len(units) > 1:
             total = convolve(total, min(4, len(units) - 1), extra)
             extra = ()

time: 83.4 us -> 81.3 us (0.975)
  waiting for transfers between devices: 21.6 us -> 14.8 us
  starting transfers between devices: 23.9 us -> 27.4 us
  Pallas kernels: 34 us -> 36.2 us
  local copies, waits for them, and re-layouts: 2.23 us -> 1.32 us
    ppermute x6 -> x5, waiting for transfers between devices: 13.1 us -> 5.25 us  [hop(): pieces[i] = lax.ppermute(pieces[i - 2], 'dp', ring.pairs)]
    ppermute x7 -> x10, starting transfers between devices: 0.85 us -> 4.22 us  [the longest x2 3.62 us: body(): lax.ppermute(pieces[i - 2][rows_of_taps[0]:rows_of_taps[-1] + 1], 'dp', r...]
    pallas_call x7 -> x8, Pallas kernels: 26.4 us -> 28.5 us  [conv_call(): pl.pallas_call(functools.partial(conv_kernel, tuple(parts), first, bool(e...]
    ppermute x7 -> x10, waiting for transfers between devices: 0.02 us -> 1.69 us  [the longest x2 1.67 us: body(): lax.ppermute(pieces[i - 2][rows_of_taps[0]:rows_of_taps[-1] + 1], 'dp', r...]
    all_to_all x1, waiting for transfers between devices: 2.48 us -> 1.46 us  [body(): terms = lax.all_to_all(terms, 'dp', 0, 0, tiled=True)]
    unnamed x14, local copies, waits for them, and re-layouts: 2.22 us -> 1.22 us
    ppermute x6 -> x5, starting transfers between devices: 8 us -> 8.13 us  [hop(): pieces[i] = lax.ppermute(pieces[i - 2], 'dp', ring.pairs)]
  transfers between devices with their start and end apart: 19 -> 21, of which waited for: 6 -> 8; matrix products, arithmetic and copies ran while one was open for 1% -> 1% of each run, Pallas kernels for 37% -> 42%
where the time goes in v5:
time: 81.3 us; the launch traced here: 80.9 us
  Pallas kernels  36.2 us (45%)
  starting transfers between devices  27.4 us (34%)
  waiting for transfers between devices  14.8 us (18%)
  local copies, waits for them, and re-layouts  1.32 us (2%)
    pallas_call x8, Pallas kernels, conv_call(): pl.pallas_call(functools.partial(conv_kernel, tuple(parts), first, bool(e...  28.5 us
    ppermute x5, starting transfers between devices, hop(): pieces[i] = lax.ppermute(pieces[i - 2], 'dp', ring.pairs)  8.13 us
    all_to_all x1, starting transfers between devices, body(): act_rows = lax.all_to_all(act, 'dp', 0, 0, tiled=True)  5.49 us
    ppermute x5, waiting for transfers between devices, hop(): pieces[i] = lax.ppermute(pieces[i - 2], 'dp', ring.pairs)  5.25 us
    all_to_all x1, waiting for transfers between devices, body(): act_rows = lax.all_to_all(act, 'dp', 0, 0, tiled=True)  4.2 us
    ppermute x2, starting transfers between devices, body(): lax.ppermute(pieces[i - 2][rows_of_taps[0]:rows_of_taps[-1] + 1], 'dp', r...  3.62 us
    all_to_all x1, starting transfers between devices, body(): terms = lax.all_to_all(terms, 'dp', 0, 0, tiled=True)  3.5 us
    pallas_call x1, Pallas kernels, norm_call(): pl.pallas_call(functools.partial(norm_kernel, units, chan), out_shape=jax...  3.2 us
  transfers between devices with their start and end apart: 21, of which 8 were waited for; matrix products, arithmetic and copies ran while one was open for 1% of the time, Pallas kernels for 42%

profile of v5, /device:TPU:0, one launch (start us, length us, event | category | flops | bytes accessed | tf_op | source)
XLA Modules:
  0.0 80.9 jit_solution(10725316683209525704)
XLA Ops:
  0.5 2.6 %collective-permute-start.4 = (bf16[3,240,640]{2,1,0:T(8,128)(2,1)}, bf16[3,240,640]{2,1,0:T(8,128)(2,1)S(1)}, u32[]{:S(2)}, u32[]{:S(2)}) collective-permute-start(bf16[3,240,640]{2,1,0:T(8,128)(2,1)} %bitcast.10), channel_id=1, source_target_pairs={{0,8},{8,16},{16,24},{24,28},{28,20},{20,12},{12,4},{4,0},{2,6},{1... | collective-permute-start | bytes 2764808 | tf_op jit(solution)/shard_map/ppermute | solution.py:314
  3.1 1.5 %collective-permute-start.3 = (bf16[8,80,1024]{2,1,0:T(8,128)(2,1)}, bf16[8,80,1024]{2,1,0:T(8,128)(2,1)}, u32[]{:S(2)}, u32[]{:S(2)}) collective-permute-start(bf16[8,80,1024]{2,1,0:T(8,128)(2,1)} %bitcast.6), channel_id=1, source_target_pairs={{0,1},{1,0},{2,3},{3,2},{4,5},{5,4},{6,7},{7,6},{8,9},{9,8},{10,11... | collective-permute-start | bytes 3932168 | tf_op jit(solution)/shard_map/ppermute | solution.py:303
  5.3 0.7 act_rows.1.refs_1_
  6.0 5.5 %all-to-all-start = ((bf16[16,1,80]{2,1,0:T(2,128)(2,1)}), bf16[16,1,80]{2,1,0:T(2,128)(2,1)S(1)}, u32[]{:S(2)}, u32[]{:S(2)}) async-start(bf16[16,1,80]{2,1,0:T(2,128)(2,1)} %act_rows.1.refs_1_), calls=%async_computation | async-start | bytes 16384 | tf_op jit(solution)/shard_map/all_to_all | solution.py:324
  11.5 0.7 pad_maximum_fusion.1
  12.2 2.0 %collective-permute-start.1 = (bf16[3,240,640]{2,1,0:T(8,128)(2,1)S(1)}, bf16[3,240,640]{2,1,0:T(8,128)(2,1)}, u32[]{:S(2)}, u32[]{:S(2)}) collective-permute-start(bf16[3,240,640]{2,1,0:T(8,128)(2,1)S(1)} %gate.8.refs_2_), channel_id=1, source_target_pairs={{0,8},{8,16},{16,24},{24,28},{28,20},{20,12},{12,4},{4,0},{2,6},{1... | collective-permute-start | bytes 2764808 | tf_op jit(solution)/shard_map/ppermute | solution.py:321
  14.2 4.2 %all-to-all-done.act_ref = bf16[16,1,80]{2,1,0:T(2,128)(2,1)S(1)} async-done(((bf16[16,1,80]{2,1,0:T(2,128)(2,1)}), bf16[16,1,80]{2,1,0:T(2,128)(2,1)S(1)}, u32[]{:S(2)}, u32[]{:S(2)}) %all-to-all-start) | async-done | bytes 2592 | tf_op jit(solution)/shard_map/all_to_all | solution.py:324
  18.4 0.8 emb_terms.1.refs_1_
  19.2 3.5 %all-to-all-start.1 = ((f32[16,1,640]{2,1,0:T(1,128)}), f32[16,1,640]{2,1,0:T(1,128)S(1)}, u32[]{:S(2)}, u32[]{:S(2)}) async-start(f32[16,1,640]{2,1,0:T(1,128)} %emb_terms.1.refs_1_), calls=%async_computation.1 | async-start | bytes 81920 | tf_op jit(solution)/shard_map/all_to_all | solution.py:332
  22.7 1.9 %collective-permute-start.7 = (bf16[3,240,640]{2,1,0:T(8,128)(2,1)S(1)}, bf16[3,240,640]{2,1,0:T(8,128)(2,1)}, u32[]{:S(2)}, u32[]{:S(2)}) collective-permute-start(bf16[3,240,640]{2,1,0:T(8,128)(2,1)S(1)} %gate.9.refs_3_), channel_id=1, source_target_pairs={{0,8},{8,16},{16,24},{24,28},{28,20},{20,12},{12,4},{4,0},{2,6},{1... | collective-permute-start | bytes 2764808 | tf_op jit(solution)/shard_map/ppermute | solution.py:321
  24.6 1.2 %channel_stats.1.table_ref.refs_5_ = f32[6,640]{1,0:T(8,128)S(1)} custom-call(bf16[640,1024]{1,0:T(8,128)(2,1)S(1)} %bitcast.7, f32[4,640]{1,0:T(4,128)S(1)} %reshape.10.params_ref), custom_call_target="tpu_custom_call" | custom-call | flops 10000000000 | bytes 40000000 | tf_op jit(solution)/shard_map/channel_stats/pallas_call | solution.py:124
  25.9 2.2 %collective-permute-start.9 = (bf16[3,240,640]{2,1,0:T(8,128)(2,1)}, bf16[3,240,640]{2,1,0:T(8,128)(2,1)S(1)}, u32[]{:S(2)}, u32[]{:S(2)}) collective-permute-start(bf16[3,240,640]{2,1,0:T(8,128)(2,1)} %collective-permute-done.1.refs_0_.refs_2_), channel_id=1, source_target_pairs={{0,8},{8,16},{16,24},{24,28},{28,20},{20,12},{12,4},{4,0},{2,6},{1... | collective-permute-start | bytes 2764808 | tf_op jit(solution)/shard_map/ppermute | solution.py:321
  28.1 1.5 %all-to-all-done.1.terms_ref = f32[16,1,640]{2,1,0:T(1,128)S(1)} async-done(((f32[16,1,640]{2,1,0:T(1,128)}), f32[16,1,640]{2,1,0:T(1,128)S(1)}, u32[]{:S(2)}, u32[]{:S(2)}) %all-to-all-start.1) | async-done | bytes 40992 | tf_op jit(solution)/shard_map/all_to_all | solution.py:332
  29.6 1.8 %affine.1 = f32[8,2,80]{2,1,0:T(2,128)S(1)} custom-call(f32[16,1,640]{2,1,0:T(1,128)S(1)} %all-to-all-done.1.terms_ref, f32[6,640]{1,0:T(8,128)S(1)} %channel_stats.1.table_ref.refs_5_, bf16[3,240,640]{2,1,0:T(8,128)(2,1)} %collective-permute-done.1.refs_0_.refs_2_), custom_call_target="tpu_custom_call" | custom-call | flops 7000000000 | bytes 28000000 | tf_op jit(solution)/shard_map/affine/pallas_call | solution.py:167
  31.4 1.5 %collective-permute-start.2 = (f32[8,2,80]{2,1,0:T(2,128)S(1)}, f32[8,2,80]{2,1,0:T(2,128)S(1)}, u32[]{:S(2)}, u32[]{:S(2)}) collective-permute-start(f32[8,2,80]{2,1,0:T(2,128)S(1)} %affine.1), channel_id=1, source_target_pairs={{0,1},{1,0},{2,3},{3,2},{4,5},{5,4},{6,7},{7,6},{8,9},{9,8},{10,11... | collective-permute-start | bytes 15368 | tf_op jit(solution)/shard_map/ppermute | solution.py:303
  32.9 2.2 %collective-permute-done.2 = f32[8,2,80]{2,1,0:T(2,128)S(1)} collective-permute-done((f32[8,2,80]{2,1,0:T(2,128)S(1)}, f32[8,2,80]{2,1,0:T(2,128)S(1)}, u32[]{:S(2)}, u32[]{:S(2)}) %collective-permute-start.2) | collective-permute-done | bytes 5152 | tf_op jit(solution)/shard_map/ppermute | solution.py:303
  35.1 3.2 %norm_units.1.refs_0_.refs_1_ = bf16[16,80,1024]{2,1,0:T(8,128)(2,1)S(1)} custom-call(s32[256]{0:T(256)S(1)} %copy-done.6, f32[16,2,80]{2,1,0:T(2,128)S(1)} %pad_maximum_fusion.ab_ref, bf16[8,80,1024]{2,1,0:T(8,128)(2,1)S(1)} %bitcast.8, bf16[8,80,1024]{2,1,0:T(8,128)(2,1)} %collective-permute-done.3.refs_1_), custom_call_target="tpu_custom_call" | custom-call | tf_op jit(solution)/shard_map/norm_units/pallas_call | solution.py:203
  39.5 5.9 %conv_units.8 = (f32[640,1024]{1,0:T(8,128)S(1)}, f32[8,128]{1,0:T(8,128)S(1)}) custom-call(bf16[16,80,1024]{2,1,0:T(8,128)(2,1)S(1)} %norm_units.1.refs_0_.refs_1_, bf16[3,240,640]{2,1,0:T(8,128)(2,1)S(1)} %bitcast.11, bf16[3,240,640]{2,1,0:T(8,128)(2,1)S(1)} %gate.8.refs_2_, bf16[3,240,640]{2,1,0:T(8,128)(2,1)S(1)} %gate.9.refs_3_, ...), custom_call_target="tpu_custom_call" | custom-call | tf_op jit(solution)/shard_map/conv_units/pallas_call | solution.py:276
  45.3 1.1 %collective-permute-done.9.refs_0_ = bf16[3,240,640]{2,1,0:T(8,128)(2,1)S(1)} collective-permute-done((bf16[3,240,640]{2,1,0:T(8,128)(2,1)}, bf16[3,240,640]{2,1,0:T(8,128)(2,1)S(1)}, u32[]{:S(2)}, u32[]{:S(2)}) %collective-permute-start.9) | collective-permute-done | bytes 921632 | tf_op jit(solution)/shard_map/ppermute | solution.py:321
  46.4 1.6 %collective-permute-start.13 = (bf16[3,240,640]{2,1,0:T(8,128)(2,1)S(1)}, bf16[3,240,640]{2,1,0:T(8,128)(2,1)S(1)}, u32[]{:S(2)}, u32[]{:S(2)}) collective-permute-start(bf16[3,240,640]{2,1,0:T(8,128)(2,1)S(1)} %gate.11.refs_3_), channel_id=1, source_target_pairs={{0,8},{8,16},{16,24},{24,28},{28,20},{20,12},{12,4},{4,0},{2,6},{1... | collective-permute-start | bytes 2764808 | tf_op jit(solution)/shard_map/ppermute | solution.py:321
  48.1 5.5 %conv_units.9 = (f32[640,1024]{1,0:T(8,128)S(1)}, f32[8,128]{1,0:T(8,128)S(1)}) custom-call(f32[640,1024]{1,0:T(8,128)S(1)} %get-tuple-element.18.refs_0_, bf16[16,80,1024]{2,1,0:T(8,128)(2,1)S(1)} %norm_units.1.refs_0_.refs_1_, bf16[3,240,640]{2,1,0:T(8,128)(2,1)} %collective-permute-done.1.refs_0_.refs_2_, ...), custom_call_target="tpu_custom_call", output_to_operand_aliasing={{0}: (0, {})} | custom-call | tf_op jit(solution)/shard_map/conv_units/pallas_call | solution.py:276
  53.6 2.7 %collective-permute-done.11.refs_0_ = bf16[3,240,640]{2,1,0:T(8,128)(2,1)S(1)} collective-permute-done((bf16[3,240,640]{2,1,0:T(8,128)(2,1)}, bf16[3,240,640]{2,1,0:T(8,128)(2,1)S(1)}, u32[]{:S(2)}, u32[]{:S(2)}) %collective-permute-start.11) | collective-permute-done | bytes 921632 | tf_op jit(solution)/shard_map/ppermute | solution.py:321
  56.4 1.7 %collective-permute-start.15 = (bf16[2,240,640]{2,1,0:T(8,128)(2,1)S(1)}, bf16[2,240,640]{2,1,0:T(8,128)(2,1)S(1)}, u32[]{:S(2)}, u32[]{:S(2)}) collective-permute-start(bf16[2,240,640]{2,1,0:T(8,128)(2,1)S(1)} %slice.8), channel_id=1, source_target_pairs={{0,8},{8,16},{16,24},{24,28},{28,20},{20,12},{12,4},{4,0},{2,6},{1... | collective-permute-start | bytes 1843208 | tf_op jit(solution)/shard_map/ppermute | solution.py:372
  58.1 3.3 %conv_units.10 = (f32[640,1024]{1,0:T(8,128)S(1)}, f32[8,128]{1,0:T(8,128)}) custom-call(f32[640,1024]{1,0:T(8,128)S(1)} %get-tuple-element.19.refs_0_, bf16[16,80,1024]{2,1,0:T(8,128)(2,1)S(1)} %norm_units.1.refs_0_.refs_1_, bf16[3,240,640]{2,1,0:T(8,128)(2,1)S(1)} %collective-permute-done.8.refs_2_, ...), custom_call_target="tpu_custom_call", output_to_operand_aliasing={{0}: (0, {})} | custom-call | tf_op jit(solution)/shard_map/conv_units/pallas_call | solution.py:276
  61.4 3.3 %conv_units.11 = (f32[640,1024]{1,0:T(8,128)S(1)}, f32[8,128]{1,0:T(8,128)S(1)}) custom-call(f32[640,1024]{1,0:T(8,128)S(1)} %get-tuple-element.21.refs_0_, bf16[16,80,1024]{2,1,0:T(8,128)(2,1)S(1)} %norm_units.1.refs_0_.refs_1_, bf16[3,240,640]{2,1,0:T(8,128)(2,1)S(1)} %collective-permute-done.10.refs_2_, ...), custom_call_target="tpu_custom_call", output_to_operand_aliasing={{0}: (0, {})} | custom-call | tf_op jit(solution)/shard_map/conv_units/pallas_call | solution.py:276
  64.8 1.4 %collective-permute-done.13.refs_0_ = bf16[3,240,640]{2,1,0:T(8,128)(2,1)S(1)} collective-permute-done((bf16[3,240,640]{2,1,0:T(8,128)(2,1)S(1)}, bf16[3,240,640]{2,1,0:T(8,128)(2,1)S(1)}, u32[]{:S(2)}, u32[]{:S(2)}) %collective-permute-start.13) | collective-permute-done | bytes 921632 | tf_op jit(solution)/shard_map/ppermute | solution.py:321
  66.2 1.9 %collective-permute-start.17 = (bf16[1,240,640]{2,1,0:T(8,128)(2,1)S(1)}, bf16[1,240,640]{2,1,0:T(8,128)(2,1)S(1)}, u32[]{:S(2)}, u32[]{:S(2)}) collective-permute-start(bf16[1,240,640]{2,1,0:T(8,128)(2,1)S(1)} %slice.9), channel_id=1, source_target_pairs={{0,8},{8,16},{16,24},{24,28},{28,20},{20,12},{12,4},{4,0},{2,6},{1... | collective-permute-start | bytes 921608 | tf_op jit(solution)/shard_map/ppermute | solution.py:372
  68.1 3.2 %conv_units.12 = (f32[640,1024]{1,0:T(8,128)S(1)}, f32[8,128]{1,0:T(8,128)S(1)}) custom-call(f32[640,1024]{1,0:T(8,128)S(1)} %get-tuple-element.23.refs_0_, bf16[16,80,1024]{2,1,0:T(8,128)(2,1)S(1)} %norm_units.1.refs_0_.refs_1_, bf16[3,240,640]{2,1,0:T(8,128)(2,1)S(1)} %collective-permute-done.12.refs_2_, ...), custom_call_target="tpu_custom_call", output_to_operand_aliasing={{0}: (0, {})} | custom-call | tf_op jit(solution)/shard_map/conv_units/pallas_call | solution.py:276
  71.3 1.4 %collective-permute-done.15.refs_0_ = bf16[2,240,640]{2,1,0:T(8,128)(2,1)S(1)} collective-permute-done((bf16[2,240,640]{2,1,0:T(8,128)(2,1)S(1)}, bf16[2,240,640]{2,1,0:T(8,128)(2,1)S(1)}, u32[]{:S(2)}, u32[]{:S(2)}) %collective-permute-start.15) | collective-permute-done | bytes 614432 | tf_op jit(solution)/shard_map/ppermute | solution.py:372
  72.8 3.0 %conv_units.13 = (f32[640,1024]{1,0:T(8,128)S(1)}, f32[8,128]{1,0:T(8,128)S(1)}) custom-call(f32[640,1024]{1,0:T(8,128)S(1)} %get-tuple-element.25.refs_0_, bf16[16,80,1024]{2,1,0:T(8,128)(2,1)S(1)} %norm_units.1.refs_0_.refs_1_, bf16[3,240,640]{2,1,0:T(8,128)(2,1)S(1)} %collective-permute-done.14.refs_2_, ...), custom_call_target="tpu_custom_call", output_to_operand_aliasing={{0}: (0, {})} | custom-call | tf_op jit(solution)/shard_map/conv_units/pallas_call | solution.py:276
  76.4 2.1 %conv_units.14 = (f32[640,1024]{1,0:T(8,128)S(1)}, f32[8,128]{1,0:T(8,128)}) custom-call(f32[640,1024]{1,0:T(8,128)S(1)} %get-tuple-element.27.refs_0_, bf16[16,80,1024]{2,1,0:T(8,128)(2,1)S(1)} %norm_units.1.refs_0_.refs_1_, bf16[2,240,640]{2,1,0:T(8,128)(2,1)S(1)} %collective-permute-done.16.refs_2_, ...), custom_call_target="tpu_custom_call", output_to_operand_aliasing={{0}: (0, {})} | custom-call | tf_op jit(solution)/shard_map/conv_units/pallas_call | solution.py:276
  78.5 2.2 %conv_units.15 = (bf16[640,1024]{1,0:T(8,128)(2,1)}, f32[8,128]{1,0:T(8,128)}) custom-call(f32[640,1024]{1,0:T(8,128)S(1)} %get-tuple-element.29.refs_0_, bf16[16,80,1024]{2,1,0:T(8,128)(2,1)S(1)} %norm_units.1.refs_0_.refs_1_, bf16[1,240,640]{2,1,0:T(8,128)(2,1)S(1)} %collective-permute-done.18.refs_2_), custom_call_target="tpu_custom_call" | custom-call | tf_op jit(solution)/shard_map/conv_units/pallas_call | solution.py:276
  (50 shorter events, 3.2 us)
Async XLA Ops:
  0.0 24.6 %copy-start.1 = (bf16[1,640,1024]{2,1,0:T(8,128)(2,1)S(1)}, bf16[1,640,1024]{2,1,0:T(8,128)(2,1)}, u32[]{:S(2)}) copy-start(bf16[1,640,1024]{2,1,0:T(8,128)(2,1)} %param.10) | copy-start | bytes 3932164
  0.0 18.4 %copy-start.4 = (bf16[80,640]{1,0:T(8,128)(2,1)S(1)}, bf16[80,640]{1,0:T(8,128)(2,1)}, u32[]{:S(2)}) copy-start(bf16[80,640]{1,0:T(8,128)(2,1)} %w_ref.1) | copy-start | bytes 307204
  0.0 4.6 %collective-permute-start = (bf16[3,240,640]{2,1,0:T(8,128)(2,1)}, bf16[3,240,640]{2,1,0:T(8,128)(2,1)S(1)}, u32[]{:S(2)}, u32[]{:S(2)}) collective-permute-start(bf16[3,240,640]{2,1,0:T(8,128)(2,1)} %bitcast.9), channel_id=1, source_target_pairs={{0,2},{2,0},{4,6},{6,4},{8,10},{10,8},{12,14},{14,12},{16,18},{18,... | collective-permute-start | bytes 2764808 | tf_op jit(solution)/shard_map/ppermute | solution.py:313
  0.5 22.3 %collective-permute-start.4 = (bf16[3,240,640]{2,1,0:T(8,128)(2,1)}, bf16[3,240,640]{2,1,0:T(8,128)(2,1)S(1)}, u32[]{:S(2)}, u32[]{:S(2)}) collective-permute-start(bf16[3,240,640]{2,1,0:T(8,128)(2,1)} %bitcast.10), channel_id=1, source_target_pairs={{0,8},{8,16},{16,24},{24,28},{28,20},{20,12},{12,4},{4,0},{2,6},{1... | collective-permute-start | bytes 2764808 | tf_op jit(solution)/shard_map/ppermute | solution.py:314
  3.1 32.0 %collective-permute-start.3 = (bf16[8,80,1024]{2,1,0:T(8,128)(2,1)}, bf16[8,80,1024]{2,1,0:T(8,128)(2,1)}, u32[]{:S(2)}, u32[]{:S(2)}) collective-permute-start(bf16[8,80,1024]{2,1,0:T(8,128)(2,1)} %bitcast.6), channel_id=1, source_target_pairs={{0,1},{1,0},{2,3},{3,2},{4,5},{5,4},{6,7},{7,6},{8,9},{9,8},{10,11... | collective-permute-start | bytes 3932168 | tf_op jit(solution)/shard_map/ppermute | solution.py:303
  4.6 0.7 copy-start.5
  6.0 12.4 %all-to-all-start = ((bf16[16,1,80]{2,1,0:T(2,128)(2,1)}), bf16[16,1,80]{2,1,0:T(2,128)(2,1)S(1)}, u32[]{:S(2)}, u32[]{:S(2)}) async-start(bf16[16,1,80]{2,1,0:T(2,128)(2,1)} %act_rows.1.refs_1_), calls=%async_computation | async-start | bytes 16384 | tf_op jit(solution)/shard_map/all_to_all | solution.py:324
  12.2 13.7 %collective-permute-start.1 = (bf16[3,240,640]{2,1,0:T(8,128)(2,1)S(1)}, bf16[3,240,640]{2,1,0:T(8,128)(2,1)}, u32[]{:S(2)}, u32[]{:S(2)}) collective-permute-start(bf16[3,240,640]{2,1,0:T(8,128)(2,1)S(1)} %gate.8.refs_2_), channel_id=1, source_target_pairs={{0,8},{8,16},{16,24},{24,28},{28,20},{20,12},{12,4},{4,0},{2,6},{1... | collective-permute-start | bytes 2764808 | tf_op jit(solution)/shard_map/ppermute | solution.py:321
  19.2 10.4 %all-to-all-start.1 = ((f32[16,1,640]{2,1,0:T(1,128)}), f32[16,1,640]{2,1,0:T(1,128)S(1)}, u32[]{:S(2)}, u32[]{:S(2)}) async-start(f32[16,1,640]{2,1,0:T(1,128)} %emb_terms.1.refs_1_), calls=%async_computation.1 | async-start | bytes 81920 | tf_op jit(solution)/shard_map/all_to_all | solution.py:332
  22.7 15.6 %collective-permute-start.7 = (bf16[3,240,640]{2,1,0:T(8,128)(2,1)S(1)}, bf16[3,240,640]{2,1,0:T(8,128)(2,1)}, u32[]{:S(2)}, u32[]{:S(2)}) collective-permute-start(bf16[3,240,640]{2,1,0:T(8,128)(2,1)S(1)} %gate.9.refs_3_), channel_id=1, source_target_pairs={{0,8},{8,16},{16,24},{24,28},{28,20},{20,12},{12,4},{4,0},{2,6},{1... | collective-permute-start | bytes 2764808 | tf_op jit(solution)/shard_map/ppermute | solution.py:321
  25.8 9.3 %copy-start.6 = (s32[256]{0:T(256)S(1)}, s32[256]{0:T(256)}, u32[]{:S(2)}) copy-start(s32[256]{0:T(256)} %constant.2.clone.blocks_ref) | copy-start | bytes 3076
  25.8 13.2 %collective-permute-start.5 = (bf16[3,240,640]{2,1,0:T(8,128)(2,1)S(1)}, bf16[3,240,640]{2,1,0:T(8,128)(2,1)}, u32[]{:S(2)}, u32[]{:S(2)}) collective-permute-start(bf16[3,240,640]{2,1,0:T(8,128)(2,1)S(1)} %gate.9.refs_3_), channel_id=1, source_target_pairs={{0,2},{2,0},{4,6},{6,4},{8,10},{10,8},{12,14},{14,12},{16,18},{18,... | collective-permute-start | bytes 2764808 | tf_op jit(solution)/shard_map/ppermute | solution.py:345
  25.9 20.5 %collective-permute-start.9 = (bf16[3,240,640]{2,1,0:T(8,128)(2,1)}, bf16[3,240,640]{2,1,0:T(8,128)(2,1)S(1)}, u32[]{:S(2)}, u32[]{:S(2)}) collective-permute-start(bf16[3,240,640]{2,1,0:T(8,128)(2,1)} %collective-permute-done.1.refs_0_.refs_2_), channel_id=1, source_target_pairs={{0,8},{8,16},{16,24},{24,28},{28,20},{20,12},{12,4},{4,0},{2,6},{1... | collective-permute-start | bytes 2764808 | tf_op jit(solution)/shard_map/ppermute | solution.py:321
  29.6 5.5 %copy-start.2 = (bf16[1,640,1024]{2,1,0:T(8,128)(2,1)S(1)}, bf16[1,640,1024]{2,1,0:T(8,128)(2,1)}, u32[]{:S(2)}) copy-start(bf16[1,640,1024]{2,1,0:T(8,128)(2,1)} %param.10) | copy-start | bytes 3932164
  31.4 3.7 %collective-permute-start.2 = (f32[8,2,80]{2,1,0:T(2,128)S(1)}, f32[8,2,80]{2,1,0:T(2,128)S(1)}, u32[]{:S(2)}, u32[]{:S(2)}) collective-permute-start(f32[8,2,80]{2,1,0:T(2,128)S(1)} %affine.1), channel_id=1, source_target_pairs={{0,1},{1,0},{2,3},{3,2},{4,5},{5,4},{6,7},{7,6},{8,9},{9,8},{10,11... | collective-permute-start | bytes 15368 | tf_op jit(solution)/shard_map/ppermute | solution.py:303
  35.0 13.1 %collective-permute-start.6 = (bf16[3,240,640]{2,1,0:T(8,128)(2,1)}, bf16[3,240,640]{2,1,0:T(8,128)(2,1)S(1)}, u32[]{:S(2)}, u32[]{:S(2)}) collective-permute-start(bf16[3,240,640]{2,1,0:T(8,128)(2,1)} %collective-permute-done.1.refs_0_.refs_2_), channel_id=1, source_target_pairs={{0,2},{2,0},{4,6},{6,4},{8,10},{10,8},{12,14},{14,12},{16,18},{18,... | collective-permute-start | bytes 2764808 | tf_op jit(solution)/shard_map/ppermute | solution.py:345
  38.3 1.2 %copy-start.3 = (bf16[9,80,640]{2,1,0:T(8,128)(2,1)S(1)}, bf16[9,80,640]{2,1,0:T(8,128)(2,1)}, u32[]{:S(2)}) copy-start(bf16[9,80,640]{2,1,0:T(8,128)(2,1)} %param.17) | copy-start | bytes 2764804
  38.3 18.0 %collective-permute-start.11 = (bf16[3,240,640]{2,1,0:T(8,128)(2,1)}, bf16[3,240,640]{2,1,0:T(8,128)(2,1)S(1)}, u32[]{:S(2)}, u32[]{:S(2)}) collective-permute-start(bf16[3,240,640]{2,1,0:T(8,128)(2,1)} %gate.10.refs_4_), channel_id=1, source_target_pairs={{0,8},{8,16},{16,24},{24,28},{28,20},{20,12},{12,4},{4,0},{2,6},{1... | collective-permute-start | bytes 2764808 | tf_op jit(solution)/shard_map/ppermute | solution.py:321
  38.7 19.3 %collective-permute-start.8 = (bf16[3,240,640]{2,1,0:T(8,128)(2,1)}, bf16[3,240,640]{2,1,0:T(8,128)(2,1)S(1)}, u32[]{:S(2)}, u32[]{:S(2)}) collective-permute-start(bf16[3,240,640]{2,1,0:T(8,128)(2,1)} %gate.10.refs_4_), channel_id=1, source_target_pairs={{0,2},{2,0},{4,6},{6,4},{8,10},{10,8},{12,14},{14,12},{16,18},{18,... | collective-permute-start | bytes 2764808 | tf_op jit(solution)/shard_map/ppermute | solution.py:345
  46.4 15.0 %collective-permute-start.10 = (bf16[3,240,640]{2,1,0:T(8,128)(2,1)S(1)}, bf16[3,240,640]{2,1,0:T(8,128)(2,1)S(1)}, u32[]{:S(2)}, u32[]{:S(2)}) collective-permute-start(bf16[3,240,640]{2,1,0:T(8,128)(2,1)S(1)} %gate.11.refs_3_), channel_id=1, source_target_pairs={{0,2},{2,0},{4,6},{6,4},{8,10},{10,8},{12,14},{14,12},{16,18},{18,... | collective-permute-start | bytes 2764808 | tf_op jit(solution)/shard_map/ppermute | solution.py:345
  46.4 19.7 %collective-permute-start.13 = (bf16[3,240,640]{2,1,0:T(8,128)(2,1)S(1)}, bf16[3,240,640]{2,1,0:T(8,128)(2,1)S(1)}, u32[]{:S(2)}, u32[]{:S(2)}) collective-permute-start(bf16[3,240,640]{2,1,0:T(8,128)(2,1)S(1)} %gate.11.refs_3_), channel_id=1, source_target_pairs={{0,8},{8,16},{16,24},{24,28},{28,20},{20,12},{12,4},{4,0},{2,6},{1... | collective-permute-start | bytes 2764808 | tf_op jit(solution)/shard_map/ppermute | solution.py:321
  56.3 11.8 %collective-permute-start.12 = (bf16[3,240,640]{2,1,0:T(8,128)(2,1)S(1)}, bf16[3,240,640]{2,1,0:T(8,128)(2,1)S(1)}, u32[]{:S(2)}, u32[]{:S(2)}) collective-permute-start(bf16[3,240,640]{2,1,0:T(8,128)(2,1)S(1)} %gate.12.refs_3_), channel_id=1, source_target_pairs={{0,2},{2,0},{4,6},{6,4},{8,10},{10,8},{12,14},{14,12},{16,18},{18,... | collective-permute-start | bytes 2764808 | tf_op jit(solution)/shard_map/ppermute | solution.py:345
  56.4 16.4 %collective-permute-start.15 = (bf16[2,240,640]{2,1,0:T(8,128)(2,1)S(1)}, bf16[2,240,640]{2,1,0:T(8,128)(2,1)S(1)}, u32[]{:S(2)}, u32[]{:S(2)}) collective-permute-start(bf16[2,240,640]{2,1,0:T(8,128)(2,1)S(1)} %slice.8), channel_id=1, source_target_pairs={{0,8},{8,16},{16,24},{24,28},{28,20},{20,12},{12,4},{4,0},{2,6},{1... | collective-permute-start | bytes 1843208 | tf_op jit(solution)/shard_map/ppermute | solution.py:372
  64.8 3.4 %copy-start = (bf16[1,640,1024]{2,1,0:T(8,128)(2,1)S(1)}, bf16[1,640,1024]{2,1,0:T(8,128)(2,1)}, u32[]{:S(2)}) copy-start(bf16[1,640,1024]{2,1,0:T(8,128)(2,1)} %param.11) | copy-start | bytes 3932164
  66.2 6.6 %collective-permute-start.14 = (bf16[3,240,640]{2,1,0:T(8,128)(2,1)S(1)}, bf16[3,240,640]{2,1,0:T(8,128)(2,1)S(1)}, u32[]{:S(2)}, u32[]{:S(2)}) collective-permute-start(bf16[3,240,640]{2,1,0:T(8,128)(2,1)S(1)} %gate.13.refs_3_), channel_id=1, source_target_pairs={{0,2},{2,0},{4,6},{6,4},{8,10},{10,8},{12,14},{14,12},{16,18},{18,... | collective-permute-start | bytes 2764808 | tf_op jit(solution)/shard_map/ppermute | solution.py:345
  66.2 9.8 %collective-permute-start.17 = (bf16[1,240,640]{2,1,0:T(8,128)(2,1)S(1)}, bf16[1,240,640]{2,1,0:T(8,128)(2,1)S(1)}, u32[]{:S(2)}, u32[]{:S(2)}) collective-permute-start(bf16[1,240,640]{2,1,0:T(8,128)(2,1)S(1)} %slice.9), channel_id=1, source_target_pairs={{0,8},{8,16},{16,24},{24,28},{28,20},{20,12},{12,4},{4,0},{2,6},{1... | collective-permute-start | bytes 921608 | tf_op jit(solution)/shard_map/ppermute | solution.py:372
  72.8 3.6 %collective-permute-start.16 = (bf16[2,240,640]{2,1,0:T(8,128)(2,1)S(1)}, bf16[2,240,640]{2,1,0:T(8,128)(2,1)S(1)}, u32[]{:S(2)}, u32[]{:S(2)}) collective-permute-start(bf16[2,240,640]{2,1,0:T(8,128)(2,1)S(1)} %gate.14.refs_3_), channel_id=1, source_target_pairs={{0,2},{2,0},{4,6},{6,4},{8,10},{10,8},{12,14},{14,12},{16,18},{18,... | collective-permute-start | bytes 1843208 | tf_op jit(solution)/shard_map/ppermute | solution.py:345
  76.0 2.4 %collective-permute-start.18 = (bf16[1,240,640]{2,1,0:T(8,128)(2,1)S(1)}, bf16[1,240,640]{2,1,0:T(8,128)(2,1)S(1)}, u32[]{:S(2)}, u32[]{:S(2)}) collective-permute-start(bf16[1,240,640]{2,1,0:T(8,128)(2,1)S(1)} %gate.15.refs_3_), channel_id=1, source_target_pairs={{0,2},{2,0},{4,6},{6,4},{8,10},{10,8},{12,14},{14,12},{16,18},{18,... | collective-permute-start | bytes 921608 | tf_op jit(solution)/shard_map/ppermute | solution.py:345

commit v6 on v5

--- a/solution.py
+++ b/solution.py
@@ -50,14 +50,14 @@
 
 
 def weight(times):
-    return pl.CostEstimate(flops=times * 10**9, transcendentals=0, bytes_accessed=times * 4 * 10**6)
+    return pl.CostEstimate(flops=int(times * 1e9), transcendentals=0, bytes_accessed=int(times * 4e6))
 
 
 def nothing(*refs):
     del refs
 
 
-def gate(piece, *others):
+def gate(piece, *others, times=None):
     return pl.pallas_call(
         nothing,
         out_shape=jax.ShapeDtypeStruct(piece.shape, piece.dtype),
@@ -65,6 +65,7 @@
         out_specs=ANY,
         input_output_aliases={0: 0},
         compiler_params=pltpu.CompilerParams(vmem_limit_bytes=2**20),
+        cost_estimate=None if times is None else weight(times),
         name="gate",
     )(piece, *others)
 
@@ -211,14 +212,17 @@
     )(jnp.asarray(blocks.reshape(-1)), affine, *slices)
 
 
-def conv_kernel(parts, first, extra, last, *refs):
+def conv_kernel(parts, ready, ahead, first, extra, last, *refs):
     refs = list(refs)
     count = len(parts)
     total_ref = None if first else refs.pop(0)
     normed_ref = refs.pop(0)
     weight_refs = [refs.pop(0) for _ in range(count)]
+    ready_refs = {unit: refs.pop(0) for unit in ready}
     skip_ref, table_ref = (refs.pop(0), refs.pop(0)) if extra else (None, None)
-    out_ref, token_ref, even, odd, rounded, sem = refs
+    out_ref, token_ref = refs.pop(0), refs.pop(0)
+    ahead_refs = {unit: refs.pop(0) for unit in ahead}
+    even, odd, rounded, sem = refs
     stacks = (even, odd)
     rows = normed_ref.shape[1]
     outs = out_ref.shape[0]
@@ -226,20 +230,25 @@
     inside = [(column > 0).astype(jnp.bfloat16), None, (column < WIDTH - 1).astype(jnp.bfloat16)]
     token_ref[...] = jnp.zeros_like(token_ref)
 
-    def build(u):
-        unit, taps = parts[u]
+    def fill(window, unit, taps):
         normed = normed_ref[unit]
         for dx in range(3):
             moved = normed if dx == 1 else shifted(normed, dx - 1) * inside[dx]
             for dy in taps:
                 row = (3 * (dy - taps[0]) + dx) * rows
-                stacks[u % 2][row : row + rows, :] = moved if dy == 1 else shifted(moved, WIDTH * (dy - 1))
+                window[row : row + rows, :] = moved if dy == 1 else shifted(moved, WIDTH * (dy - 1))
+
+    def build(u):
+        if parts[u][0] not in ready_refs:
+            fill(stacks[u % 2], *parts[u])
 
     def product(u, here):
-        depth = 3 * len(parts[u][1]) * rows
+        unit, taps = parts[u]
+        depth = 3 * len(taps) * rows
+        window, row = (ready_refs[unit], 3 * taps[0] * rows) if unit in ready_refs else (stacks[u % 2], 0)
         weights = weight_refs[u][:, :, here].reshape(depth, here.stop - here.start)
         return lax.dot_general(
-            weights, stacks[u % 2][:depth, :], (((0,), (0,)), ((), ())), preferred_element_type=jnp.float32
+            weights, window[row : row + depth, :], (((0,), (0,)), ((), ())), preferred_element_type=jnp.float32
         )
 
     build(0)
@@ -247,6 +256,9 @@
         for u in range(count):
             if u + 1 < count:
                 build(u + 1)
+            else:
+                for unit in ahead:
+                    fill(ahead_refs[unit], unit, tuple(range(3)))
             part = product(u, slice(0, outs))
             if u == 0 and extra:
                 bias = jnp.broadcast_to(table_ref[3:4, :], (128, outs)).T[:, 0:1]
@@ -267,20 +279,22 @@
         copy.wait()
 
 
-def conv_call(parts, total, normed, weights, extra=(), last=False):
+def conv_call(parts, total, normed, weights, extra=(), last=False, ready=None, ahead=()):
     first = total is None
+    ready = {unit: window for unit, window in (ready or {}).items() if unit in [p[0] for p in parts]}
     _, rows, _ = normed.shape
     outs = weights[0].shape[2]
     tiles = outs // 128 if outs % 128 == 0 else 1
-    operands = ([] if first else [total]) + [normed] + list(weights) + list(extra)
-    return pl.pallas_call(
-        functools.partial(conv_kernel, tuple(parts), first, bool(extra), last),
+    operands = ([] if first else [total]) + [normed] + list(weights) + list(ready.values()) + list(extra)
+    return pl.pallas_call(
+        functools.partial(conv_kernel, tuple(parts), tuple(ready), tuple(ahead), first, bool(extra), last),
         out_shape=[
             jax.ShapeDtypeStruct((outs, CELLS), jnp.bfloat16 if last else jnp.float32),
             jax.ShapeDtypeStruct((8, 128), jnp.float32),
-        ],
+        ]
+        + [jax.ShapeDtypeStruct((9 * rows, CELLS), jnp.bfloat16)] * len(ahead),
         in_specs=[WHOLE] * len(operands),
-        out_specs=[ANY if last else WHOLE, WHOLE],
+        out_specs=[ANY if last else WHOLE, WHOLE] + [WHOLE] * len(ahead),
         scratch_shapes=[
             pltpu.VMEM((9 * rows, CELLS), jnp.bfloat16),
             pltpu.VMEM((9 * rows, CELLS), jnp.bfloat16),
@@ -350,10 +364,15 @@
         def swap(i):
             units.append(((2 * i - 1, taps), swapped(pieces[i])))
 
-        def convolve(total, count, extra=(), last=False):
+        windows = {}
+
+        def convolve(total, count, extra=(), last=False, ahead=()):
             here = [units.pop(0) for _ in range(min(count, len(units)))]
-            total, token = conv_call([p for p, _ in here], total, normed, [w for _, w in here], extra, last)
+            total, token, *made = conv_call(
+                [p for p, _ in here], total, normed, [w for _, w in here], extra, last, windows, ahead
+            )
             tokens.append(token)
+            windows.update(zip(ahead, made))
             return total
 
         total = None
@@ -387,11 +406,11 @@
             total = convolve(total, 4)
         extra = (skip[0], table)
         if tail:
-            total = convolve(total, len(units), extra)
+            total = convolve(total, len(units), extra, ahead=(2 * final - 2, 2 * final - 1))
             extra = ()
             swap(final - 1)
         for rows_of_taps, piece in tail:
-            piece = gate(piece, tokens[-1])
+            piece = gate(piece, tokens[-1], times=1)
             units.append(((2 * final - 2, rows_of_taps), piece))
             moving = ((2 * final - 1, rows_of_taps), swapped(piece))
             total = convolve(total, len(units))

time: 81.3 us -> 80.7 us (level)
  no operation moved by 1% of the time
where the time goes in v6:
time: 80.7 us; the launch traced here: 80.2 us
  Pallas kernels  35.6 us (44%)
  starting transfers between devices  27.3 us (34%)
  waiting for transfers between devices  14.8 us (18%)
  local copies, waits for them, and re-layouts  1.32 us (2%)
    pallas_call x8, Pallas kernels, conv_call(): pl.pallas_call(functools.partial(conv_kernel, tuple(parts), tuple(ready),...  28 us
    ppermute x5, starting transfers between devices, hop(): pieces[i] = lax.ppermute(pieces[i - 2], 'dp', ring.pairs)  8.13 us
    all_to_all x1, starting transfers between devices, body(): act_rows = lax.all_to_all(act, 'dp', 0, 0, tiled=True)  5.49 us
    ppermute x5, waiting for transfers between devices, hop(): pieces[i] = lax.ppermute(pieces[i - 2], 'dp', ring.pairs)  5.32 us
    all_to_all x1, waiting for transfers between devices, body(): act_rows = lax.all_to_all(act, 'dp', 0, 0, tiled=True)  4.2 us
    ppermute x2, starting transfers between devices, body(): lax.ppermute(pieces[i - 2][rows_of_taps[0]:rows_of_taps[-1] + 1], 'dp', r...  3.62 us
    all_to_all x1, starting transfers between devices, body(): terms = lax.all_to_all(terms, 'dp', 0, 0, tiled=True)  3.5 us
    pallas_call x1, Pallas kernels, norm_call(): pl.pallas_call(functools.partial(norm_kernel, units, chan), out_shape=jax...  3.2 us
  transfers between devices with their start and end apart: 21, of which 8 were waited for; matrix products, arithmetic and copies ran while one was open for 1% of the time, Pallas kernels for 42%

profile of v6, /device:TPU:0, one launch (start us, length us, event | category | flops | bytes accessed | tf_op | source)
XLA Modules:
  0.0 80.2 jit_solution(4759710855685358453)
XLA Ops:
  0.5 2.6 %collective-permute-start.4 = (bf16[3,240,640]{2,1,0:T(8,128)(2,1)}, bf16[3,240,640]{2,1,0:T(8,128)(2,1)S(1)}, u32[]{:S(2)}, u32[]{:S(2)}) collective-permute-start(bf16[3,240,640]{2,1,0:T(8,128)(2,1)} %bitcast.10), channel_id=1, source_target_pairs={{0,8},{8,16},{16,24},{24,28},{28,20},{20,12},{12,4},{4,0},{2,6},{1... | collective-permute-start | bytes 2764808 | tf_op jit(solution)/shard_map/ppermute | solution.py:328
  3.1 1.5 %collective-permute-start.3 = (bf16[8,80,1024]{2,1,0:T(8,128)(2,1)}, bf16[8,80,1024]{2,1,0:T(8,128)(2,1)}, u32[]{:S(2)}, u32[]{:S(2)}) collective-permute-start(bf16[8,80,1024]{2,1,0:T(8,128)(2,1)} %bitcast.6), channel_id=1, source_target_pairs={{0,1},{1,0},{2,3},{3,2},{4,5},{5,4},{6,7},{7,6},{8,9},{9,8},{10,11... | collective-permute-start | bytes 3932168 | tf_op jit(solution)/shard_map/ppermute | solution.py:317
  5.3 0.7 act_rows.1.refs_1_
  6.0 5.5 %all-to-all-start = ((bf16[16,1,80]{2,1,0:T(2,128)(2,1)}), bf16[16,1,80]{2,1,0:T(2,128)(2,1)S(1)}, u32[]{:S(2)}, u32[]{:S(2)}) async-start(bf16[16,1,80]{2,1,0:T(2,128)(2,1)} %act_rows.1.refs_1_), calls=%async_computation | async-start | bytes 16384 | tf_op jit(solution)/shard_map/all_to_all | solution.py:338
  11.5 0.7 pad_maximum_fusion.1
  12.2 2.0 %collective-permute-start.1 = (bf16[3,240,640]{2,1,0:T(8,128)(2,1)S(1)}, bf16[3,240,640]{2,1,0:T(8,128)(2,1)}, u32[]{:S(2)}, u32[]{:S(2)}) collective-permute-start(bf16[3,240,640]{2,1,0:T(8,128)(2,1)S(1)} %gate.8.refs_2_), channel_id=1, source_target_pairs={{0,8},{8,16},{16,24},{24,28},{28,20},{20,12},{12,4},{4,0},{2,6},{1... | collective-permute-start | bytes 2764808 | tf_op jit(solution)/shard_map/ppermute | solution.py:335
  14.2 4.2 %all-to-all-done.act_ref = bf16[16,1,80]{2,1,0:T(2,128)(2,1)S(1)} async-done(((bf16[16,1,80]{2,1,0:T(2,128)(2,1)}), bf16[16,1,80]{2,1,0:T(2,128)(2,1)S(1)}, u32[]{:S(2)}, u32[]{:S(2)}) %all-to-all-start) | async-done | bytes 2592 | tf_op jit(solution)/shard_map/all_to_all | solution.py:338
  18.4 0.8 emb_terms.1.refs_1_
  19.2 3.5 %all-to-all-start.1 = ((f32[16,1,640]{2,1,0:T(1,128)}), f32[16,1,640]{2,1,0:T(1,128)S(1)}, u32[]{:S(2)}, u32[]{:S(2)}) async-start(f32[16,1,640]{2,1,0:T(1,128)} %emb_terms.1.refs_1_), calls=%async_computation.1 | async-start | bytes 81920 | tf_op jit(solution)/shard_map/all_to_all | solution.py:346
  22.7 1.9 %collective-permute-start.7 = (bf16[3,240,640]{2,1,0:T(8,128)(2,1)S(1)}, bf16[3,240,640]{2,1,0:T(8,128)(2,1)}, u32[]{:S(2)}, u32[]{:S(2)}) collective-permute-start(bf16[3,240,640]{2,1,0:T(8,128)(2,1)S(1)} %gate.9.refs_3_), channel_id=1, source_target_pairs={{0,8},{8,16},{16,24},{24,28},{28,20},{20,12},{12,4},{4,0},{2,6},{1... | collective-permute-start | bytes 2764808 | tf_op jit(solution)/shard_map/ppermute | solution.py:335
  24.6 1.2 %channel_stats.1.table_ref.refs_5_ = f32[6,640]{1,0:T(8,128)S(1)} custom-call(bf16[640,1024]{1,0:T(8,128)(2,1)S(1)} %bitcast.7, f32[4,640]{1,0:T(4,128)S(1)} %reshape.10.params_ref), custom_call_target="tpu_custom_call" | custom-call | flops 10000000000 | bytes 40000000 | tf_op jit(solution)/shard_map/channel_stats/pallas_call | solution.py:125
  25.9 2.2 %collective-permute-start.9 = (bf16[3,240,640]{2,1,0:T(8,128)(2,1)}, bf16[3,240,640]{2,1,0:T(8,128)(2,1)S(1)}, u32[]{:S(2)}, u32[]{:S(2)}) collective-permute-start(bf16[3,240,640]{2,1,0:T(8,128)(2,1)} %collective-permute-done.1.refs_0_.refs_2_), channel_id=1, source_target_pairs={{0,8},{8,16},{16,24},{24,28},{28,20},{20,12},{12,4},{4,0},{2,6},{1... | collective-permute-start | bytes 2764808 | tf_op jit(solution)/shard_map/ppermute | solution.py:335
  28.1 1.5 %all-to-all-done.1.terms_ref = f32[16,1,640]{2,1,0:T(1,128)S(1)} async-done(((f32[16,1,640]{2,1,0:T(1,128)}), f32[16,1,640]{2,1,0:T(1,128)S(1)}, u32[]{:S(2)}, u32[]{:S(2)}) %all-to-all-start.1) | async-done | bytes 40992 | tf_op jit(solution)/shard_map/all_to_all | solution.py:346
  29.6 1.8 %affine.1 = f32[8,2,80]{2,1,0:T(2,128)S(1)} custom-call(f32[16,1,640]{2,1,0:T(1,128)S(1)} %all-to-all-done.1.terms_ref, f32[6,640]{1,0:T(8,128)S(1)} %channel_stats.1.table_ref.refs_5_, bf16[3,240,640]{2,1,0:T(8,128)(2,1)} %collective-permute-done.1.refs_0_.refs_2_), custom_call_target="tpu_custom_call" | custom-call | flops 7000000000 | bytes 28000000 | tf_op jit(solution)/shard_map/affine/pallas_call | solution.py:168
  31.4 1.5 %collective-permute-start.2 = (f32[8,2,80]{2,1,0:T(2,128)S(1)}, f32[8,2,80]{2,1,0:T(2,128)S(1)}, u32[]{:S(2)}, u32[]{:S(2)}) collective-permute-start(f32[8,2,80]{2,1,0:T(2,128)S(1)} %affine.1), channel_id=1, source_target_pairs={{0,1},{1,0},{2,3},{3,2},{4,5},{5,4},{6,7},{7,6},{8,9},{9,8},{10,11... | collective-permute-start | bytes 15368 | tf_op jit(solution)/shard_map/ppermute | solution.py:317
  32.9 2.2 %collective-permute-done.2 = f32[8,2,80]{2,1,0:T(2,128)S(1)} collective-permute-done((f32[8,2,80]{2,1,0:T(2,128)S(1)}, f32[8,2,80]{2,1,0:T(2,128)S(1)}, u32[]{:S(2)}, u32[]{:S(2)}) %collective-permute-start.2) | collective-permute-done | bytes 5152 | tf_op jit(solution)/shard_map/ppermute | solution.py:317
  35.1 3.2 %norm_units.1.refs_0_.refs_1_ = bf16[16,80,1024]{2,1,0:T(8,128)(2,1)S(1)} custom-call(s32[256]{0:T(256)S(1)} %copy-done.6, f32[16,2,80]{2,1,0:T(2,128)S(1)} %pad_maximum_fusion.ab_ref, bf16[8,80,1024]{2,1,0:T(8,128)(2,1)S(1)} %bitcast.8, bf16[8,80,1024]{2,1,0:T(8,128)(2,1)} %collective-permute-done.3.refs_1_), custom_call_target="tpu_custom_call" | custom-call | tf_op jit(solution)/shard_map/norm_units/pallas_call | solution.py:204
  39.5 5.9 %conv_units.8 = (f32[640,1024]{1,0:T(8,128)S(1)}, f32[8,128]{1,0:T(8,128)S(1)}) custom-call(bf16[16,80,1024]{2,1,0:T(8,128)(2,1)S(1)} %norm_units.1.refs_0_.refs_1_, bf16[3,240,640]{2,1,0:T(8,128)(2,1)S(1)} %bitcast.11, bf16[3,240,640]{2,1,0:T(8,128)(2,1)S(1)} %gate.8.refs_2_, bf16[3,240,640]{2,1,0:T(8,128)(2,1)S(1)} %gate.9.refs_3_, ...), custom_call_target="tpu_custom_call" | custom-call | tf_op jit(solution)/shard_map/conv_units/pallas_call | solution.py:289
  45.3 1.1 %collective-permute-done.9.refs_0_ = bf16[3,240,640]{2,1,0:T(8,128)(2,1)S(1)} collective-permute-done((bf16[3,240,640]{2,1,0:T(8,128)(2,1)}, bf16[3,240,640]{2,1,0:T(8,128)(2,1)S(1)}, u32[]{:S(2)}, u32[]{:S(2)}) %collective-permute-start.9) | collective-permute-done | bytes 921632 | tf_op jit(solution)/shard_map/ppermute | solution.py:335
  46.4 1.6 %collective-permute-start.13 = (bf16[3,240,640]{2,1,0:T(8,128)(2,1)S(1)}, bf16[3,240,640]{2,1,0:T(8,128)(2,1)S(1)}, u32[]{:S(2)}, u32[]{:S(2)}) collective-permute-start(bf16[3,240,640]{2,1,0:T(8,128)(2,1)S(1)} %gate.11.refs_3_), channel_id=1, source_target_pairs={{0,8},{8,16},{16,24},{24,28},{28,20},{20,12},{12,4},{4,0},{2,6},{1... | collective-permute-start | bytes 2764808 | tf_op jit(solution)/shard_map/ppermute | solution.py:335
  48.1 5.4 %conv_units.9 = (f32[640,1024]{1,0:T(8,128)S(1)}, f32[8,128]{1,0:T(8,128)S(1)}) custom-call(f32[640,1024]{1,0:T(8,128)S(1)} %get-tuple-element.20.refs_0_, bf16[16,80,1024]{2,1,0:T(8,128)(2,1)S(1)} %norm_units.1.refs_0_.refs_1_, bf16[3,240,640]{2,1,0:T(8,128)(2,1)} %collective-permute-done.1.refs_0_.refs_2_, ...), custom_call_target="tpu_custom_call", output_to_operand_aliasing={{0}: (0, {})} | custom-call | tf_op jit(solution)/shard_map/conv_units/pallas_call | solution.py:289
  53.5 2.8 %collective-permute-done.11.refs_0_ = bf16[3,240,640]{2,1,0:T(8,128)(2,1)S(1)} collective-permute-done((bf16[3,240,640]{2,1,0:T(8,128)(2,1)}, bf16[3,240,640]{2,1,0:T(8,128)(2,1)S(1)}, u32[]{:S(2)}, u32[]{:S(2)}) %collective-permute-start.11) | collective-permute-done | bytes 921632 | tf_op jit(solution)/shard_map/ppermute | solution.py:335
  56.4 1.7 %collective-permute-start.15 = (bf16[2,240,640]{2,1,0:T(8,128)(2,1)S(1)}, bf16[2,240,640]{2,1,0:T(8,128)(2,1)S(1)}, u32[]{:S(2)}, u32[]{:S(2)}) collective-permute-start(bf16[2,240,640]{2,1,0:T(8,128)(2,1)S(1)} %slice.8), channel_id=1, source_target_pairs={{0,8},{8,16},{16,24},{24,28},{28,20},{20,12},{12,4},{4,0},{2,6},{1... | collective-permute-start | bytes 1843208 | tf_op jit(solution)/shard_map/ppermute | solution.py:391
  58.1 3.3 %conv_units.10 = (f32[640,1024]{1,0:T(8,128)S(1)}, f32[8,128]{1,0:T(8,128)}) custom-call(f32[640,1024]{1,0:T(8,128)S(1)} %get-tuple-element.21.refs_0_, bf16[16,80,1024]{2,1,0:T(8,128)(2,1)S(1)} %norm_units.1.refs_0_.refs_1_, bf16[3,240,640]{2,1,0:T(8,128)(2,1)S(1)} %collective-permute-done.8.refs_2_, ...), custom_call_target="tpu_custom_call", output_to_operand_aliasing={{0}: (0, {})} | custom-call | tf_op jit(solution)/shard_map/conv_units/pallas_call | solution.py:289
  61.4 3.3 %conv_units.11 = (f32[640,1024]{1,0:T(8,128)S(1)}, f32[8,128]{1,0:T(8,128)S(1)}) custom-call(f32[640,1024]{1,0:T(8,128)S(1)} %get-tuple-element.23.refs_0_, bf16[16,80,1024]{2,1,0:T(8,128)(2,1)S(1)} %norm_units.1.refs_0_.refs_1_, bf16[3,240,640]{2,1,0:T(8,128)(2,1)S(1)} %collective-permute-done.10.refs_2_, ...), custom_call_target="tpu_custom_call", output_to_operand_aliasing={{0}: (0, {})} | custom-call | tf_op jit(solution)/shard_map/conv_units/pallas_call | solution.py:289
  64.8 1.4 %collective-permute-done.13.refs_0_ = bf16[3,240,640]{2,1,0:T(8,128)(2,1)S(1)} collective-permute-done((bf16[3,240,640]{2,1,0:T(8,128)(2,1)S(1)}, bf16[3,240,640]{2,1,0:T(8,128)(2,1)S(1)}, u32[]{:S(2)}, u32[]{:S(2)}) %collective-permute-start.13) | collective-permute-done | bytes 921632 | tf_op jit(solution)/shard_map/ppermute | solution.py:335
  66.2 1.9 %collective-permute-start.17 = (bf16[1,240,640]{2,1,0:T(8,128)(2,1)S(1)}, bf16[1,240,640]{2,1,0:T(8,128)(2,1)S(1)}, u32[]{:S(2)}, u32[]{:S(2)}) collective-permute-start(bf16[1,240,640]{2,1,0:T(8,128)(2,1)S(1)} %slice.9), channel_id=1, source_target_pairs={{0,8},{8,16},{16,24},{24,28},{28,20},{20,12},{12,4},{4,0},{2,6},{1... | collective-permute-start | bytes 921608 | tf_op jit(solution)/shard_map/ppermute | solution.py:391
  68.1 3.4 %conv_units.12 = (f32[640,1024]{1,0:T(8,128)S(1)}, f32[8,128]{1,0:T(8,128)S(1)}, bf16[720,1024]{1,0:T(8,128)(2,1)S(1)}, bf16[720,1024]{1,0:T(8,128)(2,1)S(1)}) custom-call(f32[640,1024]{1,0:T(8,128)S(1)} %get-tuple-element.25.refs_0_, bf16[16,80,1024]{2,1,0:T(8,128)(2,1)S(1)} %norm_units.1.refs_0_.refs_1_, ...), custom_call_target="tpu_custom_call", output_to_operand_aliasing={{0}: (0, {})} | custom-call | tf_op jit(solution)/shard_map/conv_units/pallas_call | solution.py:289
  71.5 1.3 %collective-permute-done.15.refs_0_ = bf16[2,240,640]{2,1,0:T(8,128)(2,1)S(1)} collective-permute-done((bf16[2,240,640]{2,1,0:T(8,128)(2,1)S(1)}, bf16[2,240,640]{2,1,0:T(8,128)(2,1)S(1)}, u32[]{:S(2)}, u32[]{:S(2)}) %collective-permute-start.15) | collective-permute-done | bytes 614432 | tf_op jit(solution)/shard_map/ppermute | solution.py:391
  72.8 2.9 %conv_units.13 = (f32[640,1024]{1,0:T(8,128)S(1)}, f32[8,128]{1,0:T(8,128)S(1)}) custom-call(f32[640,1024]{1,0:T(8,128)S(1)} %get-tuple-element.27.refs_0_, bf16[16,80,1024]{2,1,0:T(8,128)(2,1)S(1)} %norm_units.1.refs_0_.refs_1_, bf16[3,240,640]{2,1,0:T(8,128)(2,1)S(1)} %collective-permute-done.14.refs_2_, ...), custom_call_target="tpu_custom_call", output_to_operand_aliasing={{0}: (0, {})} | custom-call | tf_op jit(solution)/shard_map/conv_units/pallas_call | solution.py:289
  76.2 1.9 %conv_units.14 = (f32[640,1024]{1,0:T(8,128)S(1)}, f32[8,128]{1,0:T(8,128)}) custom-call(f32[640,1024]{1,0:T(8,128)S(1)} %get-tuple-element.30.refs_0_, bf16[16,80,1024]{2,1,0:T(8,128)(2,1)S(1)} %norm_units.1.refs_0_.refs_1_, bf16[2,240,640]{2,1,0:T(8,128)(2,1)S(1)} %collective-permute-done.16.refs_2_, ...), custom_call_target="tpu_custom_call", output_to_operand_aliasing={{0}: (0, {})} | custom-call | tf_op jit(solution)/shard_map/conv_units/pallas_call | solution.py:289
  78.1 1.9 %conv_units.15 = (bf16[640,1024]{1,0:T(8,128)(2,1)}, f32[8,128]{1,0:T(8,128)}) custom-call(f32[640,1024]{1,0:T(8,128)S(1)} %get-tuple-element.33.refs_0_, bf16[16,80,1024]{2,1,0:T(8,128)(2,1)S(1)} %norm_units.1.refs_0_.refs_1_, bf16[1,240,640]{2,1,0:T(8,128)(2,1)S(1)} %collective-permute-done.18.refs_2_, bf16[720,1024]{1,0:T(8,128)(2,1)S(1)} %get-tuple-element.32.refs_5_.refs_3_), custom_call_target="tpu_custom_call" | custom-call | tf_op jit(solution)/shard_map/conv_units/pallas_call | solution.py:289
  (50 shorter events, 3.2 us)
Async XLA Ops:
  0.0 24.6 %copy-start.1 = (bf16[1,640,1024]{2,1,0:T(8,128)(2,1)S(1)}, bf16[1,640,1024]{2,1,0:T(8,128)(2,1)}, u32[]{:S(2)}) copy-start(bf16[1,640,1024]{2,1,0:T(8,128)(2,1)} %param.10) | copy-start | bytes 3932164
  0.0 18.4 %copy-start.4 = (bf16[80,640]{1,0:T(8,128)(2,1)S(1)}, bf16[80,640]{1,0:T(8,128)(2,1)}, u32[]{:S(2)}) copy-start(bf16[80,640]{1,0:T(8,128)(2,1)} %w_ref.1) | copy-start | bytes 307204
  0.0 4.6 %collective-permute-start = (bf16[3,240,640]{2,1,0:T(8,128)(2,1)}, bf16[3,240,640]{2,1,0:T(8,128)(2,1)S(1)}, u32[]{:S(2)}, u32[]{:S(2)}) collective-permute-start(bf16[3,240,640]{2,1,0:T(8,128)(2,1)} %bitcast.9), channel_id=1, source_target_pairs={{0,2},{2,0},{4,6},{6,4},{8,10},{10,8},{12,14},{14,12},{16,18},{18,... | collective-permute-start | bytes 2764808 | tf_op jit(solution)/shard_map/ppermute | solution.py:327
  0.5 22.3 %collective-permute-start.4 = (bf16[3,240,640]{2,1,0:T(8,128)(2,1)}, bf16[3,240,640]{2,1,0:T(8,128)(2,1)S(1)}, u32[]{:S(2)}, u32[]{:S(2)}) collective-permute-start(bf16[3,240,640]{2,1,0:T(8,128)(2,1)} %bitcast.10), channel_id=1, source_target_pairs={{0,8},{8,16},{16,24},{24,28},{28,20},{20,12},{12,4},{4,0},{2,6},{1... | collective-permute-start | bytes 2764808 | tf_op jit(solution)/shard_map/ppermute | solution.py:328
  3.1 32.0 %collective-permute-start.3 = (bf16[8,80,1024]{2,1,0:T(8,128)(2,1)}, bf16[8,80,1024]{2,1,0:T(8,128)(2,1)}, u32[]{:S(2)}, u32[]{:S(2)}) collective-permute-start(bf16[8,80,1024]{2,1,0:T(8,128)(2,1)} %bitcast.6), channel_id=1, source_target_pairs={{0,1},{1,0},{2,3},{3,2},{4,5},{5,4},{6,7},{7,6},{8,9},{9,8},{10,11... | collective-permute-start | bytes 3932168 | tf_op jit(solution)/shard_map/ppermute | solution.py:317
  4.6 0.7 copy-start.5
  6.0 12.4 %all-to-all-start = ((bf16[16,1,80]{2,1,0:T(2,128)(2,1)}), bf16[16,1,80]{2,1,0:T(2,128)(2,1)S(1)}, u32[]{:S(2)}, u32[]{:S(2)}) async-start(bf16[16,1,80]{2,1,0:T(2,128)(2,1)} %act_rows.1.refs_1_), calls=%async_computation | async-start | bytes 16384 | tf_op jit(solution)/shard_map/all_to_all | solution.py:338
  12.2 13.7 %collective-permute-start.1 = (bf16[3,240,640]{2,1,0:T(8,128)(2,1)S(1)}, bf16[3,240,640]{2,1,0:T(8,128)(2,1)}, u32[]{:S(2)}, u32[]{:S(2)}) collective-permute-start(bf16[3,240,640]{2,1,0:T(8,128)(2,1)S(1)} %gate.8.refs_2_), channel_id=1, source_target_pairs={{0,8},{8,16},{16,24},{24,28},{28,20},{20,12},{12,4},{4,0},{2,6},{1... | collective-permute-start | bytes 2764808 | tf_op jit(solution)/shard_map/ppermute | solution.py:335
  19.2 10.4 %all-to-all-start.1 = ((f32[16,1,640]{2,1,0:T(1,128)}), f32[16,1,640]{2,1,0:T(1,128)S(1)}, u32[]{:S(2)}, u32[]{:S(2)}) async-start(f32[16,1,640]{2,1,0:T(1,128)} %emb_terms.1.refs_1_), calls=%async_computation.1 | async-start | bytes 81920 | tf_op jit(solution)/shard_map/all_to_all | solution.py:346
  22.7 15.6 %collective-permute-start.7 = (bf16[3,240,640]{2,1,0:T(8,128)(2,1)S(1)}, bf16[3,240,640]{2,1,0:T(8,128)(2,1)}, u32[]{:S(2)}, u32[]{:S(2)}) collective-permute-start(bf16[3,240,640]{2,1,0:T(8,128)(2,1)S(1)} %gate.9.refs_3_), channel_id=1, source_target_pairs={{0,8},{8,16},{16,24},{24,28},{28,20},{20,12},{12,4},{4,0},{2,6},{1... | collective-permute-start | bytes 2764808 | tf_op jit(solution)/shard_map/ppermute | solution.py:335
  25.8 9.3 %copy-start.6 = (s32[256]{0:T(256)S(1)}, s32[256]{0:T(256)}, u32[]{:S(2)}) copy-start(s32[256]{0:T(256)} %constant.2.clone.blocks_ref) | copy-start | bytes 3076
  25.8 13.2 %collective-permute-start.5 = (bf16[3,240,640]{2,1,0:T(8,128)(2,1)S(1)}, bf16[3,240,640]{2,1,0:T(8,128)(2,1)}, u32[]{:S(2)}, u32[]{:S(2)}) collective-permute-start(bf16[3,240,640]{2,1,0:T(8,128)(2,1)S(1)} %gate.9.refs_3_), channel_id=1, source_target_pairs={{0,2},{2,0},{4,6},{6,4},{8,10},{10,8},{12,14},{14,12},{16,18},{18,... | collective-permute-start | bytes 2764808 | tf_op jit(solution)/shard_map/ppermute | solution.py:359
  25.9 20.5 %collective-permute-start.9 = (bf16[3,240,640]{2,1,0:T(8,128)(2,1)}, bf16[3,240,640]{2,1,0:T(8,128)(2,1)S(1)}, u32[]{:S(2)}, u32[]{:S(2)}) collective-permute-start(bf16[3,240,640]{2,1,0:T(8,128)(2,1)} %collective-permute-done.1.refs_0_.refs_2_), channel_id=1, source_target_pairs={{0,8},{8,16},{16,24},{24,28},{28,20},{20,12},{12,4},{4,0},{2,6},{1... | collective-permute-start | bytes 2764808 | tf_op jit(solution)/shard_map/ppermute | solution.py:335
  29.6 5.5 %copy-start.2 = (bf16[1,640,1024]{2,1,0:T(8,128)(2,1)S(1)}, bf16[1,640,1024]{2,1,0:T(8,128)(2,1)}, u32[]{:S(2)}) copy-start(bf16[1,640,1024]{2,1,0:T(8,128)(2,1)} %param.10) | copy-start | bytes 3932164
  31.4 3.7 %collective-permute-start.2 = (f32[8,2,80]{2,1,0:T(2,128)S(1)}, f32[8,2,80]{2,1,0:T(2,128)S(1)}, u32[]{:S(2)}, u32[]{:S(2)}) collective-permute-start(f32[8,2,80]{2,1,0:T(2,128)S(1)} %affine.1), channel_id=1, source_target_pairs={{0,1},{1,0},{2,3},{3,2},{4,5},{5,4},{6,7},{7,6},{8,9},{9,8},{10,11... | collective-permute-start | bytes 15368 | tf_op jit(solution)/shard_map/ppermute | solution.py:317
  35.0 13.1 %collective-permute-start.6 = (bf16[3,240,640]{2,1,0:T(8,128)(2,1)}, bf16[3,240,640]{2,1,0:T(8,128)(2,1)S(1)}, u32[]{:S(2)}, u32[]{:S(2)}) collective-permute-start(bf16[3,240,640]{2,1,0:T(8,128)(2,1)} %collective-permute-done.1.refs_0_.refs_2_), channel_id=1, source_target_pairs={{0,2},{2,0},{4,6},{6,4},{8,10},{10,8},{12,14},{14,12},{16,18},{18,... | collective-permute-start | bytes 2764808 | tf_op jit(solution)/shard_map/ppermute | solution.py:359
  38.3 1.2 %copy-start.3 = (bf16[9,80,640]{2,1,0:T(8,128)(2,1)S(1)}, bf16[9,80,640]{2,1,0:T(8,128)(2,1)}, u32[]{:S(2)}) copy-start(bf16[9,80,640]{2,1,0:T(8,128)(2,1)} %param.17) | copy-start | bytes 2764804
  38.3 18.0 %collective-permute-start.11 = (bf16[3,240,640]{2,1,0:T(8,128)(2,1)}, bf16[3,240,640]{2,1,0:T(8,128)(2,1)S(1)}, u32[]{:S(2)}, u32[]{:S(2)}) collective-permute-start(bf16[3,240,640]{2,1,0:T(8,128)(2,1)} %gate.10.refs_4_), channel_id=1, source_target_pairs={{0,8},{8,16},{16,24},{24,28},{28,20},{20,12},{12,4},{4,0},{2,6},{1... | collective-permute-start | bytes 2764808 | tf_op jit(solution)/shard_map/ppermute | solution.py:335
  38.7 19.3 %collective-permute-start.8 = (bf16[3,240,640]{2,1,0:T(8,128)(2,1)}, bf16[3,240,640]{2,1,0:T(8,128)(2,1)S(1)}, u32[]{:S(2)}, u32[]{:S(2)}) collective-permute-start(bf16[3,240,640]{2,1,0:T(8,128)(2,1)} %gate.10.refs_4_), channel_id=1, source_target_pairs={{0,2},{2,0},{4,6},{6,4},{8,10},{10,8},{12,14},{14,12},{16,18},{18,... | collective-permute-start | bytes 2764808 | tf_op jit(solution)/shard_map/ppermute | solution.py:359
  46.4 15.0 %collective-permute-start.10 = (bf16[3,240,640]{2,1,0:T(8,128)(2,1)S(1)}, bf16[3,240,640]{2,1,0:T(8,128)(2,1)S(1)}, u32[]{:S(2)}, u32[]{:S(2)}) collective-permute-start(bf16[3,240,640]{2,1,0:T(8,128)(2,1)S(1)} %gate.11.refs_3_), channel_id=1, source_target_pairs={{0,2},{2,0},{4,6},{6,4},{8,10},{10,8},{12,14},{14,12},{16,18},{18,... | collective-permute-start | bytes 2764808 | tf_op jit(solution)/shard_map/ppermute | solution.py:359
  46.4 19.7 %collective-permute-start.13 = (bf16[3,240,640]{2,1,0:T(8,128)(2,1)S(1)}, bf16[3,240,640]{2,1,0:T(8,128)(2,1)S(1)}, u32[]{:S(2)}, u32[]{:S(2)}) collective-permute-start(bf16[3,240,640]{2,1,0:T(8,128)(2,1)S(1)} %gate.11.refs_3_), channel_id=1, source_target_pairs={{0,8},{8,16},{16,24},{24,28},{28,20},{20,12},{12,4},{4,0},{2,6},{1... | collective-permute-start | bytes 2764808 | tf_op jit(solution)/shard_map/ppermute | solution.py:335
  56.3 11.8 %collective-permute-start.12 = (bf16[3,240,640]{2,1,0:T(8,128)(2,1)S(1)}, bf16[3,240,640]{2,1,0:T(8,128)(2,1)S(1)}, u32[]{:S(2)}, u32[]{:S(2)}) collective-permute-start(bf16[3,240,640]{2,1,0:T(8,128)(2,1)S(1)} %gate.12.refs_3_), channel_id=1, source_target_pairs={{0,2},{2,0},{4,6},{6,4},{8,10},{10,8},{12,14},{14,12},{16,18},{18,... | collective-permute-start | bytes 2764808 | tf_op jit(solution)/shard_map/ppermute | solution.py:359
  56.4 16.4 %collective-permute-start.15 = (bf16[2,240,640]{2,1,0:T(8,128)(2,1)S(1)}, bf16[2,240,640]{2,1,0:T(8,128)(2,1)S(1)}, u32[]{:S(2)}, u32[]{:S(2)}) collective-permute-start(bf16[2,240,640]{2,1,0:T(8,128)(2,1)S(1)} %slice.8), channel_id=1, source_target_pairs={{0,8},{8,16},{16,24},{24,28},{28,20},{20,12},{12,4},{4,0},{2,6},{1... | collective-permute-start | bytes 1843208 | tf_op jit(solution)/shard_map/ppermute | solution.py:391
  64.8 3.4 %copy-start = (bf16[1,640,1024]{2,1,0:T(8,128)(2,1)S(1)}, bf16[1,640,1024]{2,1,0:T(8,128)(2,1)}, u32[]{:S(2)}) copy-start(bf16[1,640,1024]{2,1,0:T(8,128)(2,1)} %param.11) | copy-start | bytes 3932164
  66.2 6.6 %collective-permute-start.14 = (bf16[3,240,640]{2,1,0:T(8,128)(2,1)S(1)}, bf16[3,240,640]{2,1,0:T(8,128)(2,1)S(1)}, u32[]{:S(2)}, u32[]{:S(2)}) collective-permute-start(bf16[3,240,640]{2,1,0:T(8,128)(2,1)S(1)} %gate.13.refs_3_), channel_id=1, source_target_pairs={{0,2},{2,0},{4,6},{6,4},{8,10},{10,8},{12,14},{14,12},{16,18},{18,... | collective-permute-start | bytes 2764808 | tf_op jit(solution)/shard_map/ppermute | solution.py:359
  66.2 9.8 %collective-permute-start.17 = (bf16[1,240,640]{2,1,0:T(8,128)(2,1)S(1)}, bf16[1,240,640]{2,1,0:T(8,128)(2,1)S(1)}, u32[]{:S(2)}, u32[]{:S(2)}) collective-permute-start(bf16[1,240,640]{2,1,0:T(8,128)(2,1)S(1)} %slice.9), channel_id=1, source_target_pairs={{0,8},{8,16},{16,24},{24,28},{28,20},{20,12},{12,4},{4,0},{2,6},{1... | collective-permute-start | bytes 921608 | tf_op jit(solution)/shard_map/ppermute | solution.py:391
  72.8 3.5 %collective-permute-start.16 = (bf16[2,240,640]{2,1,0:T(8,128)(2,1)S(1)}, bf16[2,240,640]{2,1,0:T(8,128)(2,1)S(1)}, u32[]{:S(2)}, u32[]{:S(2)}) collective-permute-start(bf16[2,240,640]{2,1,0:T(8,128)(2,1)S(1)} %gate.14.refs_3_), channel_id=1, source_target_pairs={{0,2},{2,0},{4,6},{6,4},{8,10},{10,8},{12,14},{14,12},{16,18},{18,... | collective-permute-start | bytes 1843208 | tf_op jit(solution)/shard_map/ppermute | solution.py:359
  76.0 2.1 %collective-permute-start.18 = (bf16[1,240,640]{2,1,0:T(8,128)(2,1)S(1)}, bf16[1,240,640]{2,1,0:T(8,128)(2,1)S(1)}, u32[]{:S(2)}, u32[]{:S(2)}) collective-permute-start(bf16[1,240,640]{2,1,0:T(8,128)(2,1)S(1)} %gate.15.refs_3_), channel_id=1, source_target_pairs={{0,2},{2,0},{4,6},{6,4},{8,10},{10,8},{12,14},{14,12},{16,18},{18,... | collective-permute-start | bytes 921608 | tf_op jit(solution)/shard_map/ppermute | solution.py:359

commit v7 on v6

--- a/solution.py
+++ b/solution.py
@@ -251,7 +251,8 @@
             weights, window[row : row + depth, :], (((0,), (0,)), ((), ())), preferred_element_type=jnp.float32
         )
 
-    build(0)
+    for u in range(count if last else 1):
+        build(u)
     if not last:
         for u in range(count):
             if u + 1 < count:
@@ -271,7 +272,10 @@
     copies = []
     for start in range(0, outs, tile):
         here = slice(start, start + tile)
-        rounded[here, :] = (total_ref[here, :] + product(0, here)).astype(jnp.bfloat16)
+        value = total_ref[here, :] + product(0, here)
+        for u in range(1, count):
+            value = value + product(u, here)
+        rounded[here, :] = value.astype(jnp.bfloat16)
         part = pl.ds(start, tile)
         copies.append(pltpu.make_async_copy(rounded.at[part], out_ref.at[part], sem.at[start // tile]))
         copies[-1].start()
@@ -411,14 +415,16 @@
             swap(final - 1)
         for rows_of_taps, piece in tail:
             piece = gate(piece, tokens[-1], times=1)
-            units.append(((2 * final - 2, rows_of_taps), piece))
-            moving = ((2 * final - 1, rows_of_taps), swapped(piece))
+            if rows_of_taps == tail[0][0]:
+                units.append(((2 * final - 2, rows_of_taps), piece))
             total = convolve(total, len(units))
-            units.append(moving)
-        while len(units) > 1:
-            total = convolve(total, min(4, len(units) - 1), extra)
+            if rows_of_taps != tail[0][0]:
+                units.append(((2 * final - 2, rows_of_taps), piece))
+            units.append(((2 * final - 1, rows_of_taps), swapped(piece)))
+        while len(units) > 2:
+            total = convolve(total, min(4, len(units) - 2), extra)
             extra = ()
-        total = convolve(total, 1, extra, last=True)
+        total = convolve(total, len(units), extra, last=True)
         return total[None]
 
     return body

time: 80.7 us -> 80.6 us (level)
  no operation moved by 1% of the time
where the time goes in v7:
time: 80.6 us; the launch traced here: 80.2 us
  Pallas kernels  35.6 us (44%)
  starting transfers between devices  27.3 us (34%)
  waiting for transfers between devices  14.8 us (18%)
  local copies, waits for them, and re-layouts  1.32 us (2%)
    pallas_call x8, Pallas kernels, conv_call(): pl.pallas_call(functools.partial(conv_kernel, tuple(parts), tuple(ready),...  28 us
    ppermute x5, starting transfers between devices, hop(): pieces[i] = lax.ppermute(pieces[i - 2], 'dp', ring.pairs)  8.13 us
    all_to_all x1, starting transfers between devices, body(): act_rows = lax.all_to_all(act, 'dp', 0, 0, tiled=True)  5.49 us
    ppermute x5, waiting for transfers between devices, hop(): pieces[i] = lax.ppermute(pieces[i - 2], 'dp', ring.pairs)  5.32 us
    all_to_all x1, waiting for transfers between devices, body(): act_rows = lax.all_to_all(act, 'dp', 0, 0, tiled=True)  4.2 us
    ppermute x2, starting transfers between devices, body(): lax.ppermute(pieces[i - 2][rows_of_taps[0]:rows_of_taps[-1] + 1], 'dp', r...  3.62 us
    all_to_all x1, starting transfers between devices, body(): terms = lax.all_to_all(terms, 'dp', 0, 0, tiled=True)  3.5 us
    pallas_call x1, Pallas kernels, norm_call(): pl.pallas_call(functools.partial(norm_kernel, units, chan), out_shape=jax...  3.2 us
  transfers between devices with their start and end apart: 21, of which 8 were waited for; matrix products, arithmetic and copies ran while one was open for 1% of the time, Pallas kernels for 42%

profile of v7, /device:TPU:0, one launch (start us, length us, event | category | flops | bytes accessed | tf_op | source)
XLA Modules:
  0.0 80.2 jit_solution(8121273013801524952)
XLA Ops:
  0.5 2.6 %collective-permute-start.4 = (bf16[3,240,640]{2,1,0:T(8,128)(2,1)}, bf16[3,240,640]{2,1,0:T(8,128)(2,1)S(1)}, u32[]{:S(2)}, u32[]{:S(2)}) collective-permute-start(bf16[3,240,640]{2,1,0:T(8,128)(2,1)} %bitcast.10), channel_id=1, source_target_pairs={{0,8},{8,16},{16,24},{24,28},{28,20},{20,12},{12,4},{4,0},{2,6},{1... | collective-permute-start | bytes 2764808 | tf_op jit(solution)/shard_map/ppermute | solution.py:332
  3.1 1.5 %collective-permute-start.3 = (bf16[8,80,1024]{2,1,0:T(8,128)(2,1)}, bf16[8,80,1024]{2,1,0:T(8,128)(2,1)}, u32[]{:S(2)}, u32[]{:S(2)}) collective-permute-start(bf16[8,80,1024]{2,1,0:T(8,128)(2,1)} %bitcast.6), channel_id=1, source_target_pairs={{0,1},{1,0},{2,3},{3,2},{4,5},{5,4},{6,7},{7,6},{8,9},{9,8},{10,11... | collective-permute-start | bytes 3932168 | tf_op jit(solution)/shard_map/ppermute | solution.py:321
  5.3 0.7 act_rows.1.refs_1_
  6.0 5.5 %all-to-all-start = ((bf16[16,1,80]{2,1,0:T(2,128)(2,1)}), bf16[16,1,80]{2,1,0:T(2,128)(2,1)S(1)}, u32[]{:S(2)}, u32[]{:S(2)}) async-start(bf16[16,1,80]{2,1,0:T(2,128)(2,1)} %act_rows.1.refs_1_), calls=%async_computation | async-start | bytes 16384 | tf_op jit(solution)/shard_map/all_to_all | solution.py:342
  11.5 0.7 pad_maximum_fusion.1
  12.2 2.0 %collective-permute-start.1 = (bf16[3,240,640]{2,1,0:T(8,128)(2,1)S(1)}, bf16[3,240,640]{2,1,0:T(8,128)(2,1)}, u32[]{:S(2)}, u32[]{:S(2)}) collective-permute-start(bf16[3,240,640]{2,1,0:T(8,128)(2,1)S(1)} %gate.8.refs_2_), channel_id=1, source_target_pairs={{0,8},{8,16},{16,24},{24,28},{28,20},{20,12},{12,4},{4,0},{2,6},{1... | collective-permute-start | bytes 2764808 | tf_op jit(solution)/shard_map/ppermute | solution.py:339
  14.2 4.2 %all-to-all-done.act_ref = bf16[16,1,80]{2,1,0:T(2,128)(2,1)S(1)} async-done(((bf16[16,1,80]{2,1,0:T(2,128)(2,1)}), bf16[16,1,80]{2,1,0:T(2,128)(2,1)S(1)}, u32[]{:S(2)}, u32[]{:S(2)}) %all-to-all-start) | async-done | bytes 2592 | tf_op jit(solution)/shard_map/all_to_all | solution.py:342
  18.4 0.8 emb_terms.1.refs_1_
  19.2 3.5 %all-to-all-start.1 = ((f32[16,1,640]{2,1,0:T(1,128)}), f32[16,1,640]{2,1,0:T(1,128)S(1)}, u32[]{:S(2)}, u32[]{:S(2)}) async-start(f32[16,1,640]{2,1,0:T(1,128)} %emb_terms.1.refs_1_), calls=%async_computation.1 | async-start | bytes 81920 | tf_op jit(solution)/shard_map/all_to_all | solution.py:350
  22.7 1.9 %collective-permute-start.7 = (bf16[3,240,640]{2,1,0:T(8,128)(2,1)S(1)}, bf16[3,240,640]{2,1,0:T(8,128)(2,1)}, u32[]{:S(2)}, u32[]{:S(2)}) collective-permute-start(bf16[3,240,640]{2,1,0:T(8,128)(2,1)S(1)} %gate.9.refs_3_), channel_id=1, source_target_pairs={{0,8},{8,16},{16,24},{24,28},{28,20},{20,12},{12,4},{4,0},{2,6},{1... | collective-permute-start | bytes 2764808 | tf_op jit(solution)/shard_map/ppermute | solution.py:339
  24.6 1.2 %channel_stats.1.table_ref.refs_5_ = f32[6,640]{1,0:T(8,128)S(1)} custom-call(bf16[640,1024]{1,0:T(8,128)(2,1)S(1)} %bitcast.7, f32[4,640]{1,0:T(4,128)S(1)} %reshape.10.params_ref), custom_call_target="tpu_custom_call" | custom-call | flops 10000000000 | bytes 40000000 | tf_op jit(solution)/shard_map/channel_stats/pallas_call | solution.py:125
  25.9 2.2 %collective-permute-start.9 = (bf16[3,240,640]{2,1,0:T(8,128)(2,1)}, bf16[3,240,640]{2,1,0:T(8,128)(2,1)S(1)}, u32[]{:S(2)}, u32[]{:S(2)}) collective-permute-start(bf16[3,240,640]{2,1,0:T(8,128)(2,1)} %collective-permute-done.1.refs_0_.refs_2_), channel_id=1, source_target_pairs={{0,8},{8,16},{16,24},{24,28},{28,20},{20,12},{12,4},{4,0},{2,6},{1... | collective-permute-start | bytes 2764808 | tf_op jit(solution)/shard_map/ppermute | solution.py:339
  28.1 1.5 %all-to-all-done.1.terms_ref = f32[16,1,640]{2,1,0:T(1,128)S(1)} async-done(((f32[16,1,640]{2,1,0:T(1,128)}), f32[16,1,640]{2,1,0:T(1,128)S(1)}, u32[]{:S(2)}, u32[]{:S(2)}) %all-to-all-start.1) | async-done | bytes 40992 | tf_op jit(solution)/shard_map/all_to_all | solution.py:350
  29.6 1.8 %affine.1 = f32[8,2,80]{2,1,0:T(2,128)S(1)} custom-call(f32[16,1,640]{2,1,0:T(1,128)S(1)} %all-to-all-done.1.terms_ref, f32[6,640]{1,0:T(8,128)S(1)} %channel_stats.1.table_ref.refs_5_, bf16[3,240,640]{2,1,0:T(8,128)(2,1)} %collective-permute-done.1.refs_0_.refs_2_), custom_call_target="tpu_custom_call" | custom-call | flops 7000000000 | bytes 28000000 | tf_op jit(solution)/shard_map/affine/pallas_call | solution.py:168
  31.4 1.5 %collective-permute-start.2 = (f32[8,2,80]{2,1,0:T(2,128)S(1)}, f32[8,2,80]{2,1,0:T(2,128)S(1)}, u32[]{:S(2)}, u32[]{:S(2)}) collective-permute-start(f32[8,2,80]{2,1,0:T(2,128)S(1)} %affine.1), channel_id=1, source_target_pairs={{0,1},{1,0},{2,3},{3,2},{4,5},{5,4},{6,7},{7,6},{8,9},{9,8},{10,11... | collective-permute-start | bytes 15368 | tf_op jit(solution)/shard_map/ppermute | solution.py:321
  32.9 2.2 %collective-permute-done.2 = f32[8,2,80]{2,1,0:T(2,128)S(1)} collective-permute-done((f32[8,2,80]{2,1,0:T(2,128)S(1)}, f32[8,2,80]{2,1,0:T(2,128)S(1)}, u32[]{:S(2)}, u32[]{:S(2)}) %collective-permute-start.2) | collective-permute-done | bytes 5152 | tf_op jit(solution)/shard_map/ppermute | solution.py:321
  35.1 3.2 %norm_units.1.refs_0_.refs_1_ = bf16[16,80,1024]{2,1,0:T(8,128)(2,1)S(1)} custom-call(s32[256]{0:T(256)S(1)} %copy-done.6, f32[16,2,80]{2,1,0:T(2,128)S(1)} %pad_maximum_fusion.ab_ref, bf16[8,80,1024]{2,1,0:T(8,128)(2,1)S(1)} %bitcast.8, bf16[8,80,1024]{2,1,0:T(8,128)(2,1)} %collective-permute-done.3.refs_1_), custom_call_target="tpu_custom_call" | custom-call | tf_op jit(solution)/shard_map/norm_units/pallas_call | solution.py:204
  39.5 5.9 %conv_units.8 = (f32[640,1024]{1,0:T(8,128)S(1)}, f32[8,128]{1,0:T(8,128)S(1)}) custom-call(bf16[16,80,1024]{2,1,0:T(8,128)(2,1)S(1)} %norm_units.1.refs_0_.refs_1_, bf16[3,240,640]{2,1,0:T(8,128)(2,1)S(1)} %bitcast.11, bf16[3,240,640]{2,1,0:T(8,128)(2,1)S(1)} %gate.8.refs_2_, bf16[3,240,640]{2,1,0:T(8,128)(2,1)S(1)} %gate.9.refs_3_, ...), custom_call_target="tpu_custom_call" | custom-call | tf_op jit(solution)/shard_map/conv_units/pallas_call | solution.py:293
  45.3 1.1 %collective-permute-done.9.refs_0_ = bf16[3,240,640]{2,1,0:T(8,128)(2,1)S(1)} collective-permute-done((bf16[3,240,640]{2,1,0:T(8,128)(2,1)}, bf16[3,240,640]{2,1,0:T(8,128)(2,1)S(1)}, u32[]{:S(2)}, u32[]{:S(2)}) %collective-permute-start.9) | collective-permute-done | bytes 921632 | tf_op jit(solution)/shard_map/ppermute | solution.py:339
  46.4 1.6 %collective-permute-start.13 = (bf16[3,240,640]{2,1,0:T(8,128)(2,1)S(1)}, bf16[3,240,640]{2,1,0:T(8,128)(2,1)S(1)}, u32[]{:S(2)}, u32[]{:S(2)}) collective-permute-start(bf16[3,240,640]{2,1,0:T(8,128)(2,1)S(1)} %gate.11.refs_3_), channel_id=1, source_target_pairs={{0,8},{8,16},{16,24},{24,28},{28,20},{20,12},{12,4},{4,0},{2,6},{1... | collective-permute-start | bytes 2764808 | tf_op jit(solution)/shard_map/ppermute | solution.py:339
  48.1 5.4 %conv_units.9 = (f32[640,1024]{1,0:T(8,128)S(1)}, f32[8,128]{1,0:T(8,128)S(1)}) custom-call(f32[640,1024]{1,0:T(8,128)S(1)} %get-tuple-element.20.refs_0_, bf16[16,80,1024]{2,1,0:T(8,128)(2,1)S(1)} %norm_units.1.refs_0_.refs_1_, bf16[3,240,640]{2,1,0:T(8,128)(2,1)} %collective-permute-done.1.refs_0_.refs_2_, ...), custom_call_target="tpu_custom_call", output_to_operand_aliasing={{0}: (0, {})} | custom-call | tf_op jit(solution)/shard_map/conv_units/pallas_call | solution.py:293
  53.5 2.8 %collective-permute-done.11.refs_0_ = bf16[3,240,640]{2,1,0:T(8,128)(2,1)S(1)} collective-permute-done((bf16[3,240,640]{2,1,0:T(8,128)(2,1)}, bf16[3,240,640]{2,1,0:T(8,128)(2,1)S(1)}, u32[]{:S(2)}, u32[]{:S(2)}) %collective-permute-start.11) | collective-permute-done | bytes 921632 | tf_op jit(solution)/shard_map/ppermute | solution.py:339
  56.4 1.7 %collective-permute-start.15 = (bf16[2,240,640]{2,1,0:T(8,128)(2,1)S(1)}, bf16[2,240,640]{2,1,0:T(8,128)(2,1)S(1)}, u32[]{:S(2)}, u32[]{:S(2)}) collective-permute-start(bf16[2,240,640]{2,1,0:T(8,128)(2,1)S(1)} %slice.8), channel_id=1, source_target_pairs={{0,8},{8,16},{16,24},{24,28},{28,20},{20,12},{12,4},{4,0},{2,6},{1... | collective-permute-start | bytes 1843208 | tf_op jit(solution)/shard_map/ppermute | solution.py:395
  58.1 3.3 %conv_units.10 = (f32[640,1024]{1,0:T(8,128)S(1)}, f32[8,128]{1,0:T(8,128)}) custom-call(f32[640,1024]{1,0:T(8,128)S(1)} %get-tuple-element.21.refs_0_, bf16[16,80,1024]{2,1,0:T(8,128)(2,1)S(1)} %norm_units.1.refs_0_.refs_1_, bf16[3,240,640]{2,1,0:T(8,128)(2,1)S(1)} %collective-permute-done.8.refs_2_, ...), custom_call_target="tpu_custom_call", output_to_operand_aliasing={{0}: (0, {})} | custom-call | tf_op jit(solution)/shard_map/conv_units/pallas_call | solution.py:293
  61.4 3.3 %conv_units.11 = (f32[640,1024]{1,0:T(8,128)S(1)}, f32[8,128]{1,0:T(8,128)S(1)}) custom-call(f32[640,1024]{1,0:T(8,128)S(1)} %get-tuple-element.23.refs_0_, bf16[16,80,1024]{2,1,0:T(8,128)(2,1)S(1)} %norm_units.1.refs_0_.refs_1_, bf16[3,240,640]{2,1,0:T(8,128)(2,1)S(1)} %collective-permute-done.10.refs_2_, ...), custom_call_target="tpu_custom_call", output_to_operand_aliasing={{0}: (0, {})} | custom-call | tf_op jit(solution)/shard_map/conv_units/pallas_call | solution.py:293
  64.8 1.4 %collective-permute-done.13.refs_0_ = bf16[3,240,640]{2,1,0:T(8,128)(2,1)S(1)} collective-permute-done((bf16[3,240,640]{2,1,0:T(8,128)(2,1)S(1)}, bf16[3,240,640]{2,1,0:T(8,128)(2,1)S(1)}, u32[]{:S(2)}, u32[]{:S(2)}) %collective-permute-start.13) | collective-permute-done | bytes 921632 | tf_op jit(solution)/shard_map/ppermute | solution.py:339
  66.2 1.9 %collective-permute-start.17 = (bf16[1,240,640]{2,1,0:T(8,128)(2,1)S(1)}, bf16[1,240,640]{2,1,0:T(8,128)(2,1)S(1)}, u32[]{:S(2)}, u32[]{:S(2)}) collective-permute-start(bf16[1,240,640]{2,1,0:T(8,128)(2,1)S(1)} %slice.9), channel_id=1, source_target_pairs={{0,8},{8,16},{16,24},{24,28},{28,20},{20,12},{12,4},{4,0},{2,6},{1... | collective-permute-start | bytes 921608 | tf_op jit(solution)/shard_map/ppermute | solution.py:395
  68.1 3.4 %conv_units.12 = (f32[640,1024]{1,0:T(8,128)S(1)}, f32[8,128]{1,0:T(8,128)S(1)}, bf16[720,1024]{1,0:T(8,128)(2,1)S(1)}, bf16[720,1024]{1,0:T(8,128)(2,1)S(1)}) custom-call(f32[640,1024]{1,0:T(8,128)S(1)} %get-tuple-element.25.refs_0_, bf16[16,80,1024]{2,1,0:T(8,128)(2,1)S(1)} %norm_units.1.refs_0_.refs_1_, ...), custom_call_target="tpu_custom_call", output_to_operand_aliasing={{0}: (0, {})} | custom-call | tf_op jit(solution)/shard_map/conv_units/pallas_call | solution.py:293
  71.5 1.3 %collective-permute-done.15.refs_0_ = bf16[2,240,640]{2,1,0:T(8,128)(2,1)S(1)} collective-permute-done((bf16[2,240,640]{2,1,0:T(8,128)(2,1)S(1)}, bf16[2,240,640]{2,1,0:T(8,128)(2,1)S(1)}, u32[]{:S(2)}, u32[]{:S(2)}) %collective-permute-start.15) | collective-permute-done | bytes 614432 | tf_op jit(solution)/shard_map/ppermute | solution.py:395
  72.8 2.9 %conv_units.13 = (f32[640,1024]{1,0:T(8,128)S(1)}, f32[8,128]{1,0:T(8,128)S(1)}) custom-call(f32[640,1024]{1,0:T(8,128)S(1)} %get-tuple-element.27.refs_0_, bf16[16,80,1024]{2,1,0:T(8,128)(2,1)S(1)} %norm_units.1.refs_0_.refs_1_, bf16[3,240,640]{2,1,0:T(8,128)(2,1)S(1)} %collective-permute-done.14.refs_2_, ...), custom_call_target="tpu_custom_call", output_to_operand_aliasing={{0}: (0, {})} | custom-call | tf_op jit(solution)/shard_map/conv_units/pallas_call | solution.py:293
  76.2 1.5 %conv_units.14 = (f32[640,1024]{1,0:T(8,128)S(1)}, f32[8,128]{1,0:T(8,128)}) custom-call(f32[640,1024]{1,0:T(8,128)S(1)} %get-tuple-element.30.refs_0_, bf16[16,80,1024]{2,1,0:T(8,128)(2,1)S(1)} %norm_units.1.refs_0_.refs_1_, bf16[2,240,640]{2,1,0:T(8,128)(2,1)S(1)} %collective-permute-done.16.refs_2_, ...), custom_call_target="tpu_custom_call", output_to_operand_aliasing={{0}: (0, {})} | custom-call | tf_op jit(solution)/shard_map/conv_units/pallas_call | solution.py:293
  77.8 2.3 %conv_units.15 = (bf16[640,1024]{1,0:T(8,128)(2,1)}, f32[8,128]{1,0:T(8,128)}) custom-call(f32[640,1024]{1,0:T(8,128)S(1)} %get-tuple-element.32.refs_0_, bf16[16,80,1024]{2,1,0:T(8,128)(2,1)S(1)} %norm_units.1.refs_0_.refs_1_, bf16[1,240,640]{2,1,0:T(8,128)(2,1)S(1)} %gate.15.refs_2_, bf16[1,240,640]{2,1,0:T(8,128)(2,1)S(1)} %collective-permute-done.18.refs_3_, ...), custom_call_target="tpu_custom_call" | custom-call | tf_op jit(solution)/shard_map/conv_units/pallas_call | solution.py:293
  (50 shorter events, 3.2 us)
Async XLA Ops:
  0.0 24.6 %copy-start.1 = (bf16[1,640,1024]{2,1,0:T(8,128)(2,1)S(1)}, bf16[1,640,1024]{2,1,0:T(8,128)(2,1)}, u32[]{:S(2)}) copy-start(bf16[1,640,1024]{2,1,0:T(8,128)(2,1)} %param.10) | copy-start | bytes 3932164
  0.0 18.4 %copy-start.4 = (bf16[80,640]{1,0:T(8,128)(2,1)S(1)}, bf16[80,640]{1,0:T(8,128)(2,1)}, u32[]{:S(2)}) copy-start(bf16[80,640]{1,0:T(8,128)(2,1)} %w_ref.1) | copy-start | bytes 307204
  0.0 4.6 %collective-permute-start = (bf16[3,240,640]{2,1,0:T(8,128)(2,1)}, bf16[3,240,640]{2,1,0:T(8,128)(2,1)S(1)}, u32[]{:S(2)}, u32[]{:S(2)}) collective-permute-start(bf16[3,240,640]{2,1,0:T(8,128)(2,1)} %bitcast.9), channel_id=1, source_target_pairs={{0,2},{2,0},{4,6},{6,4},{8,10},{10,8},{12,14},{14,12},{16,18},{18,... | collective-permute-start | bytes 2764808 | tf_op jit(solution)/shard_map/ppermute | solution.py:331
  0.5 22.3 %collective-permute-start.4 = (bf16[3,240,640]{2,1,0:T(8,128)(2,1)}, bf16[3,240,640]{2,1,0:T(8,128)(2,1)S(1)}, u32[]{:S(2)}, u32[]{:S(2)}) collective-permute-start(bf16[3,240,640]{2,1,0:T(8,128)(2,1)} %bitcast.10), channel_id=1, source_target_pairs={{0,8},{8,16},{16,24},{24,28},{28,20},{20,12},{12,4},{4,0},{2,6},{1... | collective-permute-start | bytes 2764808 | tf_op jit(solution)/shard_map/ppermute | solution.py:332
  3.1 32.0 %collective-permute-start.3 = (bf16[8,80,1024]{2,1,0:T(8,128)(2,1)}, bf16[8,80,1024]{2,1,0:T(8,128)(2,1)}, u32[]{:S(2)}, u32[]{:S(2)}) collective-permute-start(bf16[8,80,1024]{2,1,0:T(8,128)(2,1)} %bitcast.6), channel_id=1, source_target_pairs={{0,1},{1,0},{2,3},{3,2},{4,5},{5,4},{6,7},{7,6},{8,9},{9,8},{10,11... | collective-permute-start | bytes 3932168 | tf_op jit(solution)/shard_map/ppermute | solution.py:321
  4.6 0.7 copy-start.5
  6.0 12.4 %all-to-all-start = ((bf16[16,1,80]{2,1,0:T(2,128)(2,1)}), bf16[16,1,80]{2,1,0:T(2,128)(2,1)S(1)}, u32[]{:S(2)}, u32[]{:S(2)}) async-start(bf16[16,1,80]{2,1,0:T(2,128)(2,1)} %act_rows.1.refs_1_), calls=%async_computation | async-start | bytes 16384 | tf_op jit(solution)/shard_map/all_to_all | solution.py:342
  12.2 13.7 %collective-permute-start.1 = (bf16[3,240,640]{2,1,0:T(8,128)(2,1)S(1)}, bf16[3,240,640]{2,1,0:T(8,128)(2,1)}, u32[]{:S(2)}, u32[]{:S(2)}) collective-permute-start(bf16[3,240,640]{2,1,0:T(8,128)(2,1)S(1)} %gate.8.refs_2_), channel_id=1, source_target_pairs={{0,8},{8,16},{16,24},{24,28},{28,20},{20,12},{12,4},{4,0},{2,6},{1... | collective-permute-start | bytes 2764808 | tf_op jit(solution)/shard_map/ppermute | solution.py:339
  19.2 10.4 %all-to-all-start.1 = ((f32[16,1,640]{2,1,0:T(1,128)}), f32[16,1,640]{2,1,0:T(1,128)S(1)}, u32[]{:S(2)}, u32[]{:S(2)}) async-start(f32[16,1,640]{2,1,0:T(1,128)} %emb_terms.1.refs_1_), calls=%async_computation.1 | async-start | bytes 81920 | tf_op jit(solution)/shard_map/all_to_all | solution.py:350
  22.7 15.6 %collective-permute-start.7 = (bf16[3,240,640]{2,1,0:T(8,128)(2,1)S(1)}, bf16[3,240,640]{2,1,0:T(8,128)(2,1)}, u32[]{:S(2)}, u32[]{:S(2)}) collective-permute-start(bf16[3,240,640]{2,1,0:T(8,128)(2,1)S(1)} %gate.9.refs_3_), channel_id=1, source_target_pairs={{0,8},{8,16},{16,24},{24,28},{28,20},{20,12},{12,4},{4,0},{2,6},{1... | collective-permute-start | bytes 2764808 | tf_op jit(solution)/shard_map/ppermute | solution.py:339
  25.8 9.3 %copy-start.6 = (s32[256]{0:T(256)S(1)}, s32[256]{0:T(256)}, u32[]{:S(2)}) copy-start(s32[256]{0:T(256)} %constant.2.clone.blocks_ref) | copy-start | bytes 3076
  25.8 13.2 %collective-permute-start.5 = (bf16[3,240,640]{2,1,0:T(8,128)(2,1)S(1)}, bf16[3,240,640]{2,1,0:T(8,128)(2,1)}, u32[]{:S(2)}, u32[]{:S(2)}) collective-permute-start(bf16[3,240,640]{2,1,0:T(8,128)(2,1)S(1)} %gate.9.refs_3_), channel_id=1, source_target_pairs={{0,2},{2,0},{4,6},{6,4},{8,10},{10,8},{12,14},{14,12},{16,18},{18,... | collective-permute-start | bytes 2764808 | tf_op jit(solution)/shard_map/ppermute | solution.py:363
  25.9 20.5 %collective-permute-start.9 = (bf16[3,240,640]{2,1,0:T(8,128)(2,1)}, bf16[3,240,640]{2,1,0:T(8,128)(2,1)S(1)}, u32[]{:S(2)}, u32[]{:S(2)}) collective-permute-start(bf16[3,240,640]{2,1,0:T(8,128)(2,1)} %collective-permute-done.1.refs_0_.refs_2_), channel_id=1, source_target_pairs={{0,8},{8,16},{16,24},{24,28},{28,20},{20,12},{12,4},{4,0},{2,6},{1... | collective-permute-start | bytes 2764808 | tf_op jit(solution)/shard_map/ppermute | solution.py:339
  29.6 5.5 %copy-start.2 = (bf16[1,640,1024]{2,1,0:T(8,128)(2,1)S(1)}, bf16[1,640,1024]{2,1,0:T(8,128)(2,1)}, u32[]{:S(2)}) copy-start(bf16[1,640,1024]{2,1,0:T(8,128)(2,1)} %param.10) | copy-start | bytes 3932164
  31.4 3.7 %collective-permute-start.2 = (f32[8,2,80]{2,1,0:T(2,128)S(1)}, f32[8,2,80]{2,1,0:T(2,128)S(1)}, u32[]{:S(2)}, u32[]{:S(2)}) collective-permute-start(f32[8,2,80]{2,1,0:T(2,128)S(1)} %affine.1), channel_id=1, source_target_pairs={{0,1},{1,0},{2,3},{3,2},{4,5},{5,4},{6,7},{7,6},{8,9},{9,8},{10,11... | collective-permute-start | bytes 15368 | tf_op jit(solution)/shard_map/ppermute | solution.py:321
  35.0 13.1 %collective-permute-start.6 = (bf16[3,240,640]{2,1,0:T(8,128)(2,1)}, bf16[3,240,640]{2,1,0:T(8,128)(2,1)S(1)}, u32[]{:S(2)}, u32[]{:S(2)}) collective-permute-start(bf16[3,240,640]{2,1,0:T(8,128)(2,1)} %collective-permute-done.1.refs_0_.refs_2_), channel_id=1, source_target_pairs={{0,2},{2,0},{4,6},{6,4},{8,10},{10,8},{12,14},{14,12},{16,18},{18,... | collective-permute-start | bytes 2764808 | tf_op jit(solution)/shard_map/ppermute | solution.py:363
  38.3 1.2 %copy-start.3 = (bf16[9,80,640]{2,1,0:T(8,128)(2,1)S(1)}, bf16[9,80,640]{2,1,0:T(8,128)(2,1)}, u32[]{:S(2)}) copy-start(bf16[9,80,640]{2,1,0:T(8,128)(2,1)} %param.17) | copy-start | bytes 2764804
  38.3 18.0 %collective-permute-start.11 = (bf16[3,240,640]{2,1,0:T(8,128)(2,1)}, bf16[3,240,640]{2,1,0:T(8,128)(2,1)S(1)}, u32[]{:S(2)}, u32[]{:S(2)}) collective-permute-start(bf16[3,240,640]{2,1,0:T(8,128)(2,1)} %gate.10.refs_4_), channel_id=1, source_target_pairs={{0,8},{8,16},{16,24},{24,28},{28,20},{20,12},{12,4},{4,0},{2,6},{1... | collective-permute-start | bytes 2764808 | tf_op jit(solution)/shard_map/ppermute | solution.py:339
  38.7 19.3 %collective-permute-start.8 = (bf16[3,240,640]{2,1,0:T(8,128)(2,1)}, bf16[3,240,640]{2,1,0:T(8,128)(2,1)S(1)}, u32[]{:S(2)}, u32[]{:S(2)}) collective-permute-start(bf16[3,240,640]{2,1,0:T(8,128)(2,1)} %gate.10.refs_4_), channel_id=1, source_target_pairs={{0,2},{2,0},{4,6},{6,4},{8,10},{10,8},{12,14},{14,12},{16,18},{18,... | collective-permute-start | bytes 2764808 | tf_op jit(solution)/shard_map/ppermute | solution.py:363
  46.4 15.0 %collective-permute-start.10 = (bf16[3,240,640]{2,1,0:T(8,128)(2,1)S(1)}, bf16[3,240,640]{2,1,0:T(8,128)(2,1)S(1)}, u32[]{:S(2)}, u32[]{:S(2)}) collective-permute-start(bf16[3,240,640]{2,1,0:T(8,128)(2,1)S(1)} %gate.11.refs_3_), channel_id=1, source_target_pairs={{0,2},{2,0},{4,6},{6,4},{8,10},{10,8},{12,14},{14,12},{16,18},{18,... | collective-permute-start | bytes 2764808 | tf_op jit(solution)/shard_map/ppermute | solution.py:363
  46.4 19.7 %collective-permute-start.13 = (bf16[3,240,640]{2,1,0:T(8,128)(2,1)S(1)}, bf16[3,240,640]{2,1,0:T(8,128)(2,1)S(1)}, u32[]{:S(2)}, u32[]{:S(2)}) collective-permute-start(bf16[3,240,640]{2,1,0:T(8,128)(2,1)S(1)} %gate.11.refs_3_), channel_id=1, source_target_pairs={{0,8},{8,16},{16,24},{24,28},{28,20},{20,12},{12,4},{4,0},{2,6},{1... | collective-permute-start | bytes 2764808 | tf_op jit(solution)/shard_map/ppermute | solution.py:339
  56.3 11.8 %collective-permute-start.12 = (bf16[3,240,640]{2,1,0:T(8,128)(2,1)S(1)}, bf16[3,240,640]{2,1,0:T(8,128)(2,1)S(1)}, u32[]{:S(2)}, u32[]{:S(2)}) collective-permute-start(bf16[3,240,640]{2,1,0:T(8,128)(2,1)S(1)} %gate.12.refs_3_), channel_id=1, source_target_pairs={{0,2},{2,0},{4,6},{6,4},{8,10},{10,8},{12,14},{14,12},{16,18},{18,... | collective-permute-start | bytes 2764808 | tf_op jit(solution)/shard_map/ppermute | solution.py:363
  56.4 16.4 %collective-permute-start.15 = (bf16[2,240,640]{2,1,0:T(8,128)(2,1)S(1)}, bf16[2,240,640]{2,1,0:T(8,128)(2,1)S(1)}, u32[]{:S(2)}, u32[]{:S(2)}) collective-permute-start(bf16[2,240,640]{2,1,0:T(8,128)(2,1)S(1)} %slice.8), channel_id=1, source_target_pairs={{0,8},{8,16},{16,24},{24,28},{28,20},{20,12},{12,4},{4,0},{2,6},{1... | collective-permute-start | bytes 1843208 | tf_op jit(solution)/shard_map/ppermute | solution.py:395
  64.8 3.4 %copy-start = (bf16[1,640,1024]{2,1,0:T(8,128)(2,1)S(1)}, bf16[1,640,1024]{2,1,0:T(8,128)(2,1)}, u32[]{:S(2)}) copy-start(bf16[1,640,1024]{2,1,0:T(8,128)(2,1)} %param.11) | copy-start | bytes 3932164
  66.2 6.6 %collective-permute-start.14 = (bf16[3,240,640]{2,1,0:T(8,128)(2,1)S(1)}, bf16[3,240,640]{2,1,0:T(8,128)(2,1)S(1)}, u32[]{:S(2)}, u32[]{:S(2)}) collective-permute-start(bf16[3,240,640]{2,1,0:T(8,128)(2,1)S(1)} %gate.13.refs_3_), channel_id=1, source_target_pairs={{0,2},{2,0},{4,6},{6,4},{8,10},{10,8},{12,14},{14,12},{16,18},{18,... | collective-permute-start | bytes 2764808 | tf_op jit(solution)/shard_map/ppermute | solution.py:363
  66.2 9.8 %collective-permute-start.17 = (bf16[1,240,640]{2,1,0:T(8,128)(2,1)S(1)}, bf16[1,240,640]{2,1,0:T(8,128)(2,1)S(1)}, u32[]{:S(2)}, u32[]{:S(2)}) collective-permute-start(bf16[1,240,640]{2,1,0:T(8,128)(2,1)S(1)} %slice.9), channel_id=1, source_target_pairs={{0,8},{8,16},{16,24},{24,28},{28,20},{20,12},{12,4},{4,0},{2,6},{1... | collective-permute-start | bytes 921608 | tf_op jit(solution)/shard_map/ppermute | solution.py:395
  72.8 3.5 %collective-permute-start.16 = (bf16[2,240,640]{2,1,0:T(8,128)(2,1)S(1)}, bf16[2,240,640]{2,1,0:T(8,128)(2,1)S(1)}, u32[]{:S(2)}, u32[]{:S(2)}) collective-permute-start(bf16[2,240,640]{2,1,0:T(8,128)(2,1)S(1)} %gate.14.refs_3_), channel_id=1, source_target_pairs={{0,2},{2,0},{4,6},{6,4},{8,10},{10,8},{12,14},{14,12},{16,18},{18,... | collective-permute-start | bytes 1843208 | tf_op jit(solution)/shard_map/ppermute | solution.py:363
  76.0 1.7 %collective-permute-start.18 = (bf16[1,240,640]{2,1,0:T(8,128)(2,1)S(1)}, bf16[1,240,640]{2,1,0:T(8,128)(2,1)S(1)}, u32[]{:S(2)}, u32[]{:S(2)}) collective-permute-start(bf16[1,240,640]{2,1,0:T(8,128)(2,1)S(1)} %gate.15.refs_2_), channel_id=1, source_target_pairs={{0,2},{2,0},{4,6},{6,4},{8,10},{10,8},{12,14},{14,12},{16,18},{18,... | collective-permute-start | bytes 921608 | tf_op jit(solution)/shard_map/ppermute | solution.py:363

commit v8 on v7

--- a/solution.py
+++ b/solution.py
@@ -105,11 +105,13 @@
     )(act_rows, w_emb)
 
 
-def stats_kernel(h_ref, params_ref, out_ref):
+def stats_kernel(h_ref, *refs):
     panel = h_ref.shape[0]
     step = 80 if panel % 80 == 0 else panel
-    count = params_ref.shape[0]
-    out_ref[0:count, :] = params_ref[...]
+    params, out_ref = refs[:-1], refs[-1]
+    count = len(params)
+    for i in range(count):
+        out_ref[i : i + 1, :] = params[i][...].reshape(1, panel)
     means, variances = [], []
     for start in range(0, panel, step):
         values = h_ref[start : start + step, :].astype(jnp.float32)
@@ -121,16 +123,16 @@
         out_ref[i : i + 1, :] = jnp.broadcast_to(column, (panel, 128)).T[0:1, :]
 
 
-def stats_call(h, params):
+def stats_call(h, *params):
     return pl.pallas_call(
         stats_kernel,
-        out_shape=jax.ShapeDtypeStruct((params.shape[0] + 2, h.shape[0]), jnp.float32),
-        in_specs=[WHOLE, WHOLE],
+        out_shape=jax.ShapeDtypeStruct((len(params) + 2, h.shape[0]), jnp.float32),
+        in_specs=[WHOLE] * (1 + len(params)),
         out_specs=WHOLE,
         compiler_params=pltpu.CompilerParams(vmem_limit_bytes=VMEM_BYTES),
         cost_estimate=weight(10),
         name="channel_stats",
-    )(h, params)
+    )(h, *params)
 
 
 def affine_kernel(size, terms_ref, table_ref, *refs):
@@ -335,13 +337,12 @@
 
         def hop(i, *after):
             if after:
-                pieces[i - 2] = gate(pieces[i - 2], *after)
+                pieces[i - 2] = gate(pieces[i - 2], *after, times=3 if i == 3 else None)
             pieces[i] = lax.ppermute(pieces[i - 2], "dp", ring.pairs)
 
         act = act_call(emb, dp, pieces[1])
         act_rows = lax.all_to_all(act, "dp", 0, 0, tiled=True)
-        params = jnp.concatenate([b_emb, gn_gain, gn_bias, b_conv]).reshape(4, panel)
-        table = stats_call(h_in[0], params)
+        table = stats_call(h_in[0], b_emb, gn_gain, gn_bias, b_conv)
         if final >= 3:
             hop(3, act)
         terms = emb_call(act_rows, w_emb)

time: 80.6 us -> 80.6 us (level)
  local copies, waits for them, and re-layouts: 1.32 us -> 2.38 us
    unnamed x14 -> x22, local copies, waits for them, and re-layouts: 1.22 us -> 2.3 us
    all_to_all x1, waiting for transfers between devices: 1.46 us -> 0.65 us  [body(): terms = lax.all_to_all(terms, 'dp', 0, 0, tiled=True)]
  transfers between devices with their start and end apart: 21 -> 21, of which waited for: 8 -> 8; matrix products, arithmetic and copies ran while one was open for 1% -> 0% of each run, Pallas kernels for 42% -> 42%
where the time goes in v8:
time: 80.6 us; the launch traced here: 80.2 us
  Pallas kernels  35.6 us (44%)
  starting transfers between devices  26.6 us (33%)
  waiting for transfers between devices  15.1 us (19%)
  local copies, waits for them, and re-layouts  2.38 us (3%)
    pallas_call x8, Pallas kernels, conv_call(): pl.pallas_call(functools.partial(conv_kernel, tuple(parts), tuple(ready),...  28 us
    ppermute x5, starting transfers between devices, hop(): pieces[i] = lax.ppermute(pieces[i - 2], 'dp', ring.pairs)  7.83 us
    ppermute x5, waiting for transfers between devices, hop(): pieces[i] = lax.ppermute(pieces[i - 2], 'dp', ring.pairs)  5.66 us
    all_to_all x1, starting transfers between devices, body(): act_rows = lax.all_to_all(act, 'dp', 0, 0, tiled=True)  5.55 us
    all_to_all x1, waiting for transfers between devices, body(): act_rows = lax.all_to_all(act, 'dp', 0, 0, tiled=True)  4.83 us
    all_to_all x1, starting transfers between devices, body(): terms = lax.all_to_all(terms, 'dp', 0, 0, tiled=True)  3.5 us
    ppermute x2, starting transfers between devices, body(): lax.ppermute(pieces[i - 2][rows_of_taps[0]:rows_of_taps[-1] + 1], 'dp', r...  3.41 us
    pallas_call x1, Pallas kernels, norm_call(): pl.pallas_call(functools.partial(norm_kernel, units, chan), out_shape=jax...  3.2 us
  transfers between devices with their start and end apart: 21, of which 8 were waited for; matrix products, arithmetic and copies ran while one was open for 0% of the time, Pallas kernels for 42%

profile of v8, /device:TPU:0, one launch (start us, length us, event | category | flops | bytes accessed | tf_op | source)
XLA Modules:
  0.0 80.2 jit_solution(14551515838976590184)
XLA Ops:
  0.5 2.6 %collective-permute-start.4 = (bf16[3,240,640]{2,1,0:T(8,128)(2,1)}, bf16[3,240,640]{2,1,0:T(8,128)(2,1)S(1)}, u32[]{:S(2)}, u32[]{:S(2)}) collective-permute-start(bf16[3,240,640]{2,1,0:T(8,128)(2,1)} %bitcast.10), channel_id=1, source_target_pairs={{0,8},{8,16},{16,24},{24,28},{28,20},{20,12},{12,4},{4,0},{2,6},{1... | collective-permute-start | bytes 2764808 | tf_op jit(solution)/shard_map/ppermute | solution.py:334
  3.0 1.5 %collective-permute-start.3 = (bf16[8,80,1024]{2,1,0:T(8,128)(2,1)}, bf16[8,80,1024]{2,1,0:T(8,128)(2,1)}, u32[]{:S(2)}, u32[]{:S(2)}) collective-permute-start(bf16[8,80,1024]{2,1,0:T(8,128)(2,1)} %bitcast.6), channel_id=1, source_target_pairs={{0,1},{1,0},{2,3},{3,2},{4,5},{5,4},{6,7},{7,6},{8,9},{9,8},{10,11... | collective-permute-start | bytes 3932168 | tf_op jit(solution)/shard_map/ppermute | solution.py:323
  5.2 0.7 act_rows.1.refs_1_
  5.9 5.6 %all-to-all-start = ((bf16[16,1,80]{2,1,0:T(2,128)(2,1)}), bf16[16,1,80]{2,1,0:T(2,128)(2,1)S(1)}, u32[]{:S(2)}, u32[]{:S(2)}) async-start(bf16[16,1,80]{2,1,0:T(2,128)(2,1)} %act_rows.1.refs_1_), calls=%async_computation | async-start | bytes 16384 | tf_op jit(solution)/shard_map/all_to_all | solution.py:344
  11.5 2.0 %collective-permute-start.1 = (bf16[3,240,640]{2,1,0:T(8,128)(2,1)S(1)}, bf16[3,240,640]{2,1,0:T(8,128)(2,1)}, u32[]{:S(2)}, u32[]{:S(2)}) collective-permute-start(bf16[3,240,640]{2,1,0:T(8,128)(2,1)S(1)} %gate.8.refs_2_), channel_id=1, source_target_pairs={{0,8},{8,16},{16,24},{24,28},{28,20},{20,12},{12,4},{4,0},{2,6},{1... | collective-permute-start | bytes 2764808 | tf_op jit(solution)/shard_map/ppermute | solution.py:341
  13.5 4.8 %all-to-all-done.act_ref = bf16[16,1,80]{2,1,0:T(2,128)(2,1)S(1)} async-done(((bf16[16,1,80]{2,1,0:T(2,128)(2,1)}), bf16[16,1,80]{2,1,0:T(2,128)(2,1)S(1)}, u32[]{:S(2)}, u32[]{:S(2)}) %all-to-all-start) | async-done | bytes 2592 | tf_op jit(solution)/shard_map/all_to_all | solution.py:344
  18.4 0.8 emb_terms.1.refs_1_
  19.1 3.5 %all-to-all-start.1 = ((f32[16,1,640]{2,1,0:T(1,128)}), f32[16,1,640]{2,1,0:T(1,128)S(1)}, u32[]{:S(2)}, u32[]{:S(2)}) async-start(f32[16,1,640]{2,1,0:T(1,128)} %emb_terms.1.refs_1_), calls=%async_computation.1 | async-start | bytes 81920 | tf_op jit(solution)/shard_map/all_to_all | solution.py:351
  22.7 1.9 %collective-permute-start.7 = (bf16[3,240,640]{2,1,0:T(8,128)(2,1)S(1)}, bf16[3,240,640]{2,1,0:T(8,128)(2,1)}, u32[]{:S(2)}, u32[]{:S(2)}) collective-permute-start(bf16[3,240,640]{2,1,0:T(8,128)(2,1)S(1)} %gate.9.refs_3_), channel_id=1, source_target_pairs={{0,8},{8,16},{16,24},{24,28},{28,20},{20,12},{12,4},{4,0},{2,6},{1... | collective-permute-start | bytes 2764808 | tf_op jit(solution)/shard_map/ppermute | solution.py:341
  24.6 1.3 %copy-done.1 = bf16[1,640,1024]{2,1,0:T(8,128)(2,1)S(1)} copy-done((bf16[1,640,1024]{2,1,0:T(8,128)(2,1)S(1)}, bf16[1,640,1024]{2,1,0:T(8,128)(2,1)}, u32[]{:S(2)}) %copy-start.1) | copy-done | bytes 1310744
  25.9 1.2 %channel_stats.1.table_ref.refs_5_ = f32[6,640]{1,0:T(8,128)S(1)} custom-call(bf16[640,1024]{1,0:T(8,128)(2,1)S(1)} %bitcast.7, f32[640]{0:T(1024)S(1)} %copy-done.7, f32[640]{0:T(1024)S(1)} %copy-done.8, f32[640]{0:T(1024)S(1)} %copy-done.9, f32[640]{0:T(1024)S(1)} %copy-done.10), custom_call_target="tpu_custom_call" | custom-call | flops 10000000000 | bytes 40000000 | tf_op jit(solution)/shard_map/channel_stats/pallas_call | solution.py:127
  27.1 1.5 %collective-permute-start.9 = (bf16[3,240,640]{2,1,0:T(8,128)(2,1)}, bf16[3,240,640]{2,1,0:T(8,128)(2,1)S(1)}, u32[]{:S(2)}, u32[]{:S(2)}) collective-permute-start(bf16[3,240,640]{2,1,0:T(8,128)(2,1)} %collective-permute-done.1.refs_0_.refs_2_), channel_id=1, source_target_pairs={{0,8},{8,16},{16,24},{24,28},{28,20},{20,12},{12,4},{4,0},{2,6},{1... | collective-permute-start | bytes 2764808 | tf_op jit(solution)/shard_map/ppermute | solution.py:341
  29.3 1.8 %affine.1 = f32[8,2,80]{2,1,0:T(2,128)S(1)} custom-call(f32[16,1,640]{2,1,0:T(1,128)S(1)} %all-to-all-done.1.terms_ref, f32[6,640]{1,0:T(8,128)S(1)} %channel_stats.1.table_ref.refs_5_, bf16[3,240,640]{2,1,0:T(8,128)(2,1)} %collective-permute-done.1.refs_0_.refs_2_), custom_call_target="tpu_custom_call" | custom-call | flops 7000000000 | bytes 28000000 | tf_op jit(solution)/shard_map/affine/pallas_call | solution.py:170
  31.1 1.5 %collective-permute-start.2 = (f32[8,2,80]{2,1,0:T(2,128)S(1)}, f32[8,2,80]{2,1,0:T(2,128)S(1)}, u32[]{:S(2)}, u32[]{:S(2)}) collective-permute-start(f32[8,2,80]{2,1,0:T(2,128)S(1)} %affine.1), channel_id=1, source_target_pairs={{0,1},{1,0},{2,3},{3,2},{4,5},{5,4},{6,7},{7,6},{8,9},{9,8},{10,11... | collective-permute-start | bytes 15368 | tf_op jit(solution)/shard_map/ppermute | solution.py:323
  32.6 2.2 %collective-permute-done.2 = f32[8,2,80]{2,1,0:T(2,128)S(1)} collective-permute-done((f32[8,2,80]{2,1,0:T(2,128)S(1)}, f32[8,2,80]{2,1,0:T(2,128)S(1)}, u32[]{:S(2)}, u32[]{:S(2)}) %collective-permute-start.2) | collective-permute-done | bytes 5152 | tf_op jit(solution)/shard_map/ppermute | solution.py:323
  34.8 3.2 %norm_units.1.refs_0_.refs_1_ = bf16[16,80,1024]{2,1,0:T(8,128)(2,1)S(1)} custom-call(s32[256]{0:T(256)S(1)} %copy-done.6, f32[16,2,80]{2,1,0:T(2,128)S(1)} %pad_maximum_fusion.ab_ref, bf16[8,80,1024]{2,1,0:T(8,128)(2,1)S(1)} %bitcast.8, bf16[8,80,1024]{2,1,0:T(8,128)(2,1)} %collective-permute-done.3.refs_1_), custom_call_target="tpu_custom_call" | custom-call | tf_op jit(solution)/shard_map/norm_units/pallas_call | solution.py:206
  38.1 0.9 %collective-permute-start.11 = (bf16[3,240,640]{2,1,0:T(8,128)(2,1)}, bf16[3,240,640]{2,1,0:T(8,128)(2,1)S(1)}, u32[]{:S(2)}, u32[]{:S(2)}) collective-permute-start(bf16[3,240,640]{2,1,0:T(8,128)(2,1)} %gate.10.refs_4_), channel_id=1, source_target_pairs={{0,8},{8,16},{16,24},{24,28},{28,20},{20,12},{12,4},{4,0},{2,6},{1... | collective-permute-start | bytes 2764808 | tf_op jit(solution)/shard_map/ppermute | solution.py:341
  39.2 5.8 %conv_units.8 = (f32[640,1024]{1,0:T(8,128)S(1)}, f32[8,128]{1,0:T(8,128)S(1)}) custom-call(bf16[16,80,1024]{2,1,0:T(8,128)(2,1)S(1)} %norm_units.1.refs_0_.refs_1_, bf16[3,240,640]{2,1,0:T(8,128)(2,1)S(1)} %bitcast.11, bf16[3,240,640]{2,1,0:T(8,128)(2,1)S(1)} %gate.8.refs_2_, bf16[3,240,640]{2,1,0:T(8,128)(2,1)S(1)} %gate.9.refs_3_, ...), custom_call_target="tpu_custom_call" | custom-call | tf_op jit(solution)/shard_map/conv_units/pallas_call | solution.py:295
  45.1 1.3 %collective-permute-done.9.refs_0_ = bf16[3,240,640]{2,1,0:T(8,128)(2,1)S(1)} collective-permute-done((bf16[3,240,640]{2,1,0:T(8,128)(2,1)}, bf16[3,240,640]{2,1,0:T(8,128)(2,1)S(1)}, u32[]{:S(2)}, u32[]{:S(2)}) %collective-permute-start.9) | collective-permute-done | bytes 921632 | tf_op jit(solution)/shard_map/ppermute | solution.py:341
  46.4 1.5 %collective-permute-start.13 = (bf16[3,240,640]{2,1,0:T(8,128)(2,1)S(1)}, bf16[3,240,640]{2,1,0:T(8,128)(2,1)S(1)}, u32[]{:S(2)}, u32[]{:S(2)}) collective-permute-start(bf16[3,240,640]{2,1,0:T(8,128)(2,1)S(1)} %gate.11.refs_3_), channel_id=1, source_target_pairs={{0,8},{8,16},{16,24},{24,28},{28,20},{20,12},{12,4},{4,0},{2,6},{1... | collective-permute-start | bytes 2764808 | tf_op jit(solution)/shard_map/ppermute | solution.py:341
  47.9 5.4 %conv_units.9 = (f32[640,1024]{1,0:T(8,128)S(1)}, f32[8,128]{1,0:T(8,128)S(1)}) custom-call(f32[640,1024]{1,0:T(8,128)S(1)} %get-tuple-element.20.refs_0_, bf16[16,80,1024]{2,1,0:T(8,128)(2,1)S(1)} %norm_units.1.refs_0_.refs_1_, bf16[3,240,640]{2,1,0:T(8,128)(2,1)} %collective-permute-done.1.refs_0_.refs_2_, ...), custom_call_target="tpu_custom_call", output_to_operand_aliasing={{0}: (0, {})} | custom-call | tf_op jit(solution)/shard_map/conv_units/pallas_call | solution.py:295
  53.4 2.9 %collective-permute-done.11.refs_0_ = bf16[3,240,640]{2,1,0:T(8,128)(2,1)S(1)} collective-permute-done((bf16[3,240,640]{2,1,0:T(8,128)(2,1)}, bf16[3,240,640]{2,1,0:T(8,128)(2,1)S(1)}, u32[]{:S(2)}, u32[]{:S(2)}) %collective-permute-start.11) | collective-permute-done | bytes 921632 | tf_op jit(solution)/shard_map/ppermute | solution.py:341
  56.3 1.6 %collective-permute-start.15 = (bf16[2,240,640]{2,1,0:T(8,128)(2,1)S(1)}, bf16[2,240,640]{2,1,0:T(8,128)(2,1)S(1)}, u32[]{:S(2)}, u32[]{:S(2)}) collective-permute-start(bf16[2,240,640]{2,1,0:T(8,128)(2,1)S(1)} %slice.8), channel_id=1, source_target_pairs={{0,8},{8,16},{16,24},{24,28},{28,20},{20,12},{12,4},{4,0},{2,6},{1... | collective-permute-start | bytes 1843208 | tf_op jit(solution)/shard_map/ppermute | solution.py:396
  57.9 3.3 %conv_units.10 = (f32[640,1024]{1,0:T(8,128)S(1)}, f32[8,128]{1,0:T(8,128)}) custom-call(f32[640,1024]{1,0:T(8,128)S(1)} %get-tuple-element.21.refs_0_, bf16[16,80,1024]{2,1,0:T(8,128)(2,1)S(1)} %norm_units.1.refs_0_.refs_1_, bf16[3,240,640]{2,1,0:T(8,128)(2,1)S(1)} %collective-permute-done.8.refs_2_, ...), custom_call_target="tpu_custom_call", output_to_operand_aliasing={{0}: (0, {})} | custom-call | tf_op jit(solution)/shard_map/conv_units/pallas_call | solution.py:295
  61.2 3.3 %conv_units.11 = (f32[640,1024]{1,0:T(8,128)S(1)}, f32[8,128]{1,0:T(8,128)S(1)}) custom-call(f32[640,1024]{1,0:T(8,128)S(1)} %get-tuple-element.23.refs_0_, bf16[16,80,1024]{2,1,0:T(8,128)(2,1)S(1)} %norm_units.1.refs_0_.refs_1_, bf16[3,240,640]{2,1,0:T(8,128)(2,1)S(1)} %collective-permute-done.10.refs_2_, ...), custom_call_target="tpu_custom_call", output_to_operand_aliasing={{0}: (0, {})} | custom-call | tf_op jit(solution)/shard_map/conv_units/pallas_call | solution.py:295
  64.6 1.5 %collective-permute-done.13.refs_0_ = bf16[3,240,640]{2,1,0:T(8,128)(2,1)S(1)} collective-permute-done((bf16[3,240,640]{2,1,0:T(8,128)(2,1)S(1)}, bf16[3,240,640]{2,1,0:T(8,128)(2,1)S(1)}, u32[]{:S(2)}, u32[]{:S(2)}) %collective-permute-start.13) | collective-permute-done | bytes 921632 | tf_op jit(solution)/shard_map/ppermute | solution.py:341
  66.1 1.8 %collective-permute-start.17 = (bf16[1,240,640]{2,1,0:T(8,128)(2,1)S(1)}, bf16[1,240,640]{2,1,0:T(8,128)(2,1)S(1)}, u32[]{:S(2)}, u32[]{:S(2)}) collective-permute-start(bf16[1,240,640]{2,1,0:T(8,128)(2,1)S(1)} %slice.9), channel_id=1, source_target_pairs={{0,8},{8,16},{16,24},{24,28},{28,20},{20,12},{12,4},{4,0},{2,6},{1... | collective-permute-start | bytes 921608 | tf_op jit(solution)/shard_map/ppermute | solution.py:396
  68.0 3.4 %conv_units.12 = (f32[640,1024]{1,0:T(8,128)S(1)}, f32[8,128]{1,0:T(8,128)S(1)}, bf16[720,1024]{1,0:T(8,128)(2,1)S(1)}, bf16[720,1024]{1,0:T(8,128)(2,1)S(1)}) custom-call(f32[640,1024]{1,0:T(8,128)S(1)} %get-tuple-element.25.refs_0_, bf16[16,80,1024]{2,1,0:T(8,128)(2,1)S(1)} %norm_units.1.refs_0_.refs_1_, ...), custom_call_target="tpu_custom_call", output_to_operand_aliasing={{0}: (0, {})} | custom-call | tf_op jit(solution)/shard_map/conv_units/pallas_call | solution.py:295
  71.3 1.4 %collective-permute-done.15.refs_0_ = bf16[2,240,640]{2,1,0:T(8,128)(2,1)S(1)} collective-permute-done((bf16[2,240,640]{2,1,0:T(8,128)(2,1)S(1)}, bf16[2,240,640]{2,1,0:T(8,128)(2,1)S(1)}, u32[]{:S(2)}, u32[]{:S(2)}) %collective-permute-start.15) | collective-permute-done | bytes 614432 | tf_op jit(solution)/shard_map/ppermute | solution.py:396
  72.7 2.9 %conv_units.13 = (f32[640,1024]{1,0:T(8,128)S(1)}, f32[8,128]{1,0:T(8,128)S(1)}) custom-call(f32[640,1024]{1,0:T(8,128)S(1)} %get-tuple-element.27.refs_0_, bf16[16,80,1024]{2,1,0:T(8,128)(2,1)S(1)} %norm_units.1.refs_0_.refs_1_, bf16[3,240,640]{2,1,0:T(8,128)(2,1)S(1)} %collective-permute-done.14.refs_2_, ...), custom_call_target="tpu_custom_call", output_to_operand_aliasing={{0}: (0, {})} | custom-call | tf_op jit(solution)/shard_map/conv_units/pallas_call | solution.py:295
  76.2 1.5 %conv_units.14 = (f32[640,1024]{1,0:T(8,128)S(1)}, f32[8,128]{1,0:T(8,128)}) custom-call(f32[640,1024]{1,0:T(8,128)S(1)} %get-tuple-element.30.refs_0_, bf16[16,80,1024]{2,1,0:T(8,128)(2,1)S(1)} %norm_units.1.refs_0_.refs_1_, bf16[2,240,640]{2,1,0:T(8,128)(2,1)S(1)} %collective-permute-done.16.refs_2_, ...), custom_call_target="tpu_custom_call", output_to_operand_aliasing={{0}: (0, {})} | custom-call | tf_op jit(solution)/shard_map/conv_units/pallas_call | solution.py:295
  77.7 2.3 %conv_units.15 = (bf16[640,1024]{1,0:T(8,128)(2,1)}, f32[8,128]{1,0:T(8,128)}) custom-call(f32[640,1024]{1,0:T(8,128)S(1)} %get-tuple-element.32.refs_0_, bf16[16,80,1024]{2,1,0:T(8,128)(2,1)S(1)} %norm_units.1.refs_0_.refs_1_, bf16[1,240,640]{2,1,0:T(8,128)(2,1)S(1)} %gate.15.refs_2_, bf16[1,240,640]{2,1,0:T(8,128)(2,1)S(1)} %collective-permute-done.18.refs_3_, ...), custom_call_target="tpu_custom_call" | custom-call | tf_op jit(solution)/shard_map/conv_units/pallas_call | solution.py:295
  (56 shorter events, 2.9 us)
Async XLA Ops:
  0.0 4.5 %collective-permute-start = (bf16[3,240,640]{2,1,0:T(8,128)(2,1)}, bf16[3,240,640]{2,1,0:T(8,128)(2,1)S(1)}, u32[]{:S(2)}, u32[]{:S(2)}) collective-permute-start(bf16[3,240,640]{2,1,0:T(8,128)(2,1)} %bitcast.9), channel_id=1, source_target_pairs={{0,2},{2,0},{4,6},{6,4},{8,10},{10,8},{12,14},{14,12},{16,18},{18,... | collective-permute-start | bytes 2764808 | tf_op jit(solution)/shard_map/ppermute | solution.py:333
  0.5 22.2 %collective-permute-start.4 = (bf16[3,240,640]{2,1,0:T(8,128)(2,1)}, bf16[3,240,640]{2,1,0:T(8,128)(2,1)S(1)}, u32[]{:S(2)}, u32[]{:S(2)}) collective-permute-start(bf16[3,240,640]{2,1,0:T(8,128)(2,1)} %bitcast.10), channel_id=1, source_target_pairs={{0,8},{8,16},{16,24},{24,28},{28,20},{20,12},{12,4},{4,0},{2,6},{1... | collective-permute-start | bytes 2764808 | tf_op jit(solution)/shard_map/ppermute | solution.py:334
  3.0 31.8 %collective-permute-start.3 = (bf16[8,80,1024]{2,1,0:T(8,128)(2,1)}, bf16[8,80,1024]{2,1,0:T(8,128)(2,1)}, u32[]{:S(2)}, u32[]{:S(2)}) collective-permute-start(bf16[8,80,1024]{2,1,0:T(8,128)(2,1)} %bitcast.6), channel_id=1, source_target_pairs={{0,1},{1,0},{2,3},{3,2},{4,5},{5,4},{6,7},{7,6},{8,9},{9,8},{10,11... | collective-permute-start | bytes 3932168 | tf_op jit(solution)/shard_map/ppermute | solution.py:323
  4.5 0.7 copy-start.5
  5.9 12.4 %all-to-all-start = ((bf16[16,1,80]{2,1,0:T(2,128)(2,1)}), bf16[16,1,80]{2,1,0:T(2,128)(2,1)S(1)}, u32[]{:S(2)}, u32[]{:S(2)}) async-start(bf16[16,1,80]{2,1,0:T(2,128)(2,1)} %act_rows.1.refs_1_), calls=%async_computation | async-start | bytes 16384 | tf_op jit(solution)/shard_map/all_to_all | solution.py:344
  11.5 6.9 %copy-start.4 = (bf16[80,640]{1,0:T(8,128)(2,1)S(1)}, bf16[80,640]{1,0:T(8,128)(2,1)}, u32[]{:S(2)}) copy-start(bf16[80,640]{1,0:T(8,128)(2,1)} %w_ref.1) | copy-start | bytes 307204
  11.5 13.0 %copy-start.7 = (f32[640]{0:T(1024)S(1)}, f32[640]{0:T(1024)}, u32[]{:S(2)}) copy-start(f32[640]{0:T(1024)} %refs_0_.1) | copy-start | bytes 7684
  11.5 13.0 %copy-start.8 = (f32[640]{0:T(1024)S(1)}, f32[640]{0:T(1024)}, u32[]{:S(2)}) copy-start(f32[640]{0:T(1024)} %refs_1_.1) | copy-start | bytes 7684
  11.5 13.0 %copy-start.9 = (f32[640]{0:T(1024)S(1)}, f32[640]{0:T(1024)}, u32[]{:S(2)}) copy-start(f32[640]{0:T(1024)} %refs_2_.1) | copy-start | bytes 7684
  11.5 13.0 %copy-start.10 = (f32[640]{0:T(1024)S(1)}, f32[640]{0:T(1024)}, u32[]{:S(2)}) copy-start(f32[640]{0:T(1024)} %refs_3_.1) | copy-start | bytes 7684
  11.5 15.6 %collective-permute-start.1 = (bf16[3,240,640]{2,1,0:T(8,128)(2,1)S(1)}, bf16[3,240,640]{2,1,0:T(8,128)(2,1)}, u32[]{:S(2)}, u32[]{:S(2)}) collective-permute-start(bf16[3,240,640]{2,1,0:T(8,128)(2,1)S(1)} %gate.8.refs_2_), channel_id=1, source_target_pairs={{0,8},{8,16},{16,24},{24,28},{28,20},{20,12},{12,4},{4,0},{2,6},{1... | collective-permute-start | bytes 2764808 | tf_op jit(solution)/shard_map/ppermute | solution.py:341
  19.1 10.2 %all-to-all-start.1 = ((f32[16,1,640]{2,1,0:T(1,128)}), f32[16,1,640]{2,1,0:T(1,128)S(1)}, u32[]{:S(2)}, u32[]{:S(2)}) async-start(f32[16,1,640]{2,1,0:T(1,128)} %emb_terms.1.refs_1_), calls=%async_computation.1 | async-start | bytes 81920 | tf_op jit(solution)/shard_map/all_to_all | solution.py:351
  22.7 15.4 %collective-permute-start.7 = (bf16[3,240,640]{2,1,0:T(8,128)(2,1)S(1)}, bf16[3,240,640]{2,1,0:T(8,128)(2,1)}, u32[]{:S(2)}, u32[]{:S(2)}) collective-permute-start(bf16[3,240,640]{2,1,0:T(8,128)(2,1)S(1)} %gate.9.refs_3_), channel_id=1, source_target_pairs={{0,8},{8,16},{16,24},{24,28},{28,20},{20,12},{12,4},{4,0},{2,6},{1... | collective-permute-start | bytes 2764808 | tf_op jit(solution)/shard_map/ppermute | solution.py:341
  24.5 1.3 %copy-start.1 = (bf16[1,640,1024]{2,1,0:T(8,128)(2,1)S(1)}, bf16[1,640,1024]{2,1,0:T(8,128)(2,1)}, u32[]{:S(2)}) copy-start(bf16[1,640,1024]{2,1,0:T(8,128)(2,1)} %param.10) | copy-start | bytes 3932164
  27.0 7.8 %copy-start.6 = (s32[256]{0:T(256)S(1)}, s32[256]{0:T(256)}, u32[]{:S(2)}) copy-start(s32[256]{0:T(256)} %constant.2.clone.blocks_ref) | copy-start | bytes 3076
  27.0 11.9 %collective-permute-start.5 = (bf16[3,240,640]{2,1,0:T(8,128)(2,1)S(1)}, bf16[3,240,640]{2,1,0:T(8,128)(2,1)}, u32[]{:S(2)}, u32[]{:S(2)}) collective-permute-start(bf16[3,240,640]{2,1,0:T(8,128)(2,1)S(1)} %gate.9.refs_3_), channel_id=1, source_target_pairs={{0,2},{2,0},{4,6},{6,4},{8,10},{10,8},{12,14},{14,12},{16,18},{18,... | collective-permute-start | bytes 2764808 | tf_op jit(solution)/shard_map/ppermute | solution.py:364
  27.1 19.2 %collective-permute-start.9 = (bf16[3,240,640]{2,1,0:T(8,128)(2,1)}, bf16[3,240,640]{2,1,0:T(8,128)(2,1)S(1)}, u32[]{:S(2)}, u32[]{:S(2)}) collective-permute-start(bf16[3,240,640]{2,1,0:T(8,128)(2,1)} %collective-permute-done.1.refs_0_.refs_2_), channel_id=1, source_target_pairs={{0,8},{8,16},{16,24},{24,28},{28,20},{20,12},{12,4},{4,0},{2,6},{1... | collective-permute-start | bytes 2764808 | tf_op jit(solution)/shard_map/ppermute | solution.py:341
  29.3 5.5 %copy-start.2 = (bf16[1,640,1024]{2,1,0:T(8,128)(2,1)S(1)}, bf16[1,640,1024]{2,1,0:T(8,128)(2,1)}, u32[]{:S(2)}) copy-start(bf16[1,640,1024]{2,1,0:T(8,128)(2,1)} %param.10) | copy-start | bytes 3932164
  31.1 3.7 %collective-permute-start.2 = (f32[8,2,80]{2,1,0:T(2,128)S(1)}, f32[8,2,80]{2,1,0:T(2,128)S(1)}, u32[]{:S(2)}, u32[]{:S(2)}) collective-permute-start(f32[8,2,80]{2,1,0:T(2,128)S(1)} %affine.1), channel_id=1, source_target_pairs={{0,1},{1,0},{2,3},{3,2},{4,5},{5,4},{6,7},{7,6},{8,9},{9,8},{10,11... | collective-permute-start | bytes 15368 | tf_op jit(solution)/shard_map/ppermute | solution.py:323
  34.8 13.1 %collective-permute-start.6 = (bf16[3,240,640]{2,1,0:T(8,128)(2,1)}, bf16[3,240,640]{2,1,0:T(8,128)(2,1)S(1)}, u32[]{:S(2)}, u32[]{:S(2)}) collective-permute-start(bf16[3,240,640]{2,1,0:T(8,128)(2,1)} %collective-permute-done.1.refs_0_.refs_2_), channel_id=1, source_target_pairs={{0,2},{2,0},{4,6},{6,4},{8,10},{10,8},{12,14},{14,12},{16,18},{18,... | collective-permute-start | bytes 2764808 | tf_op jit(solution)/shard_map/ppermute | solution.py:364
  38.0 1.2 %copy-start.3 = (bf16[9,80,640]{2,1,0:T(8,128)(2,1)S(1)}, bf16[9,80,640]{2,1,0:T(8,128)(2,1)}, u32[]{:S(2)}) copy-start(bf16[9,80,640]{2,1,0:T(8,128)(2,1)} %param.17) | copy-start | bytes 2764804
  38.1 18.2 %collective-permute-start.11 = (bf16[3,240,640]{2,1,0:T(8,128)(2,1)}, bf16[3,240,640]{2,1,0:T(8,128)(2,1)S(1)}, u32[]{:S(2)}, u32[]{:S(2)}) collective-permute-start(bf16[3,240,640]{2,1,0:T(8,128)(2,1)} %gate.10.refs_4_), channel_id=1, source_target_pairs={{0,8},{8,16},{16,24},{24,28},{28,20},{20,12},{12,4},{4,0},{2,6},{1... | collective-permute-start | bytes 2764808 | tf_op jit(solution)/shard_map/ppermute | solution.py:341
  39.0 18.9 %collective-permute-start.8 = (bf16[3,240,640]{2,1,0:T(8,128)(2,1)}, bf16[3,240,640]{2,1,0:T(8,128)(2,1)S(1)}, u32[]{:S(2)}, u32[]{:S(2)}) collective-permute-start(bf16[3,240,640]{2,1,0:T(8,128)(2,1)} %gate.10.refs_4_), channel_id=1, source_target_pairs={{0,2},{2,0},{4,6},{6,4},{8,10},{10,8},{12,14},{14,12},{16,18},{18,... | collective-permute-start | bytes 2764808 | tf_op jit(solution)/shard_map/ppermute | solution.py:364
  46.4 14.9 %collective-permute-start.10 = (bf16[3,240,640]{2,1,0:T(8,128)(2,1)S(1)}, bf16[3,240,640]{2,1,0:T(8,128)(2,1)S(1)}, u32[]{:S(2)}, u32[]{:S(2)}) collective-permute-start(bf16[3,240,640]{2,1,0:T(8,128)(2,1)S(1)} %gate.11.refs_3_), channel_id=1, source_target_pairs={{0,2},{2,0},{4,6},{6,4},{8,10},{10,8},{12,14},{14,12},{16,18},{18,... | collective-permute-start | bytes 2764808 | tf_op jit(solution)/shard_map/ppermute | solution.py:364
  46.4 19.7 %collective-permute-start.13 = (bf16[3,240,640]{2,1,0:T(8,128)(2,1)S(1)}, bf16[3,240,640]{2,1,0:T(8,128)(2,1)S(1)}, u32[]{:S(2)}, u32[]{:S(2)}) collective-permute-start(bf16[3,240,640]{2,1,0:T(8,128)(2,1)S(1)} %gate.11.refs_3_), channel_id=1, source_target_pairs={{0,8},{8,16},{16,24},{24,28},{28,20},{20,12},{12,4},{4,0},{2,6},{1... | collective-permute-start | bytes 2764808 | tf_op jit(solution)/shard_map/ppermute | solution.py:341
  56.2 11.7 %collective-permute-start.12 = (bf16[3,240,640]{2,1,0:T(8,128)(2,1)S(1)}, bf16[3,240,640]{2,1,0:T(8,128)(2,1)S(1)}, u32[]{:S(2)}, u32[]{:S(2)}) collective-permute-start(bf16[3,240,640]{2,1,0:T(8,128)(2,1)S(1)} %gate.12.refs_3_), channel_id=1, source_target_pairs={{0,2},{2,0},{4,6},{6,4},{8,10},{10,8},{12,14},{14,12},{16,18},{18,... | collective-permute-start | bytes 2764808 | tf_op jit(solution)/shard_map/ppermute | solution.py:364
  56.3 16.4 %collective-permute-start.15 = (bf16[2,240,640]{2,1,0:T(8,128)(2,1)S(1)}, bf16[2,240,640]{2,1,0:T(8,128)(2,1)S(1)}, u32[]{:S(2)}, u32[]{:S(2)}) collective-permute-start(bf16[2,240,640]{2,1,0:T(8,128)(2,1)S(1)} %slice.8), channel_id=1, source_target_pairs={{0,8},{8,16},{16,24},{24,28},{28,20},{20,12},{12,4},{4,0},{2,6},{1... | collective-permute-start | bytes 1843208 | tf_op jit(solution)/shard_map/ppermute | solution.py:396
  64.6 3.4 %copy-start = (bf16[1,640,1024]{2,1,0:T(8,128)(2,1)S(1)}, bf16[1,640,1024]{2,1,0:T(8,128)(2,1)}, u32[]{:S(2)}) copy-start(bf16[1,640,1024]{2,1,0:T(8,128)(2,1)} %param.11) | copy-start | bytes 3932164
  66.1 6.6 %collective-permute-start.14 = (bf16[3,240,640]{2,1,0:T(8,128)(2,1)S(1)}, bf16[3,240,640]{2,1,0:T(8,128)(2,1)S(1)}, u32[]{:S(2)}, u32[]{:S(2)}) collective-permute-start(bf16[3,240,640]{2,1,0:T(8,128)(2,1)S(1)} %gate.13.refs_3_), channel_id=1, source_target_pairs={{0,2},{2,0},{4,6},{6,4},{8,10},{10,8},{12,14},{14,12},{16,18},{18,... | collective-permute-start | bytes 2764808 | tf_op jit(solution)/shard_map/ppermute | solution.py:364
  66.1 9.8 %collective-permute-start.17 = (bf16[1,240,640]{2,1,0:T(8,128)(2,1)S(1)}, bf16[1,240,640]{2,1,0:T(8,128)(2,1)S(1)}, u32[]{:S(2)}, u32[]{:S(2)}) collective-permute-start(bf16[1,240,640]{2,1,0:T(8,128)(2,1)S(1)} %slice.9), channel_id=1, source_target_pairs={{0,8},{8,16},{16,24},{24,28},{28,20},{20,12},{12,4},{4,0},{2,6},{1... | collective-permute-start | bytes 921608 | tf_op jit(solution)/shard_map/ppermute | solution.py:396
  72.7 3.5 %collective-permute-start.16 = (bf16[2,240,640]{2,1,0:T(8,128)(2,1)S(1)}, bf16[2,240,640]{2,1,0:T(8,128)(2,1)S(1)}, u32[]{:S(2)}, u32[]{:S(2)}) collective-permute-start(bf16[2,240,640]{2,1,0:T(8,128)(2,1)S(1)} %gate.14.refs_3_), channel_id=1, source_target_pairs={{0,2},{2,0},{4,6},{6,4},{8,10},{10,8},{12,14},{14,12},{16,18},{18,... | collective-permute-start | bytes 1843208 | tf_op jit(solution)/shard_map/ppermute | solution.py:364
  76.0 1.7 %collective-permute-start.18 = (bf16[1,240,640]{2,1,0:T(8,128)(2,1)S(1)}, bf16[1,240,640]{2,1,0:T(8,128)(2,1)S(1)}, u32[]{:S(2)}, u32[]{:S(2)}) collective-permute-start(bf16[1,240,640]{2,1,0:T(8,128)(2,1)S(1)} %gate.15.refs_2_), channel_id=1, source_target_pairs={{0,2},{2,0},{4,6},{6,4},{8,10},{10,8},{12,14},{14,12},{16,18},{18,... | collective-permute-start | bytes 921608 | tf_op jit(solution)/shard_map/ppermute | solution.py:364

commit v9 on v8

--- a/solution.py
+++ b/solution.py
@@ -13,7 +13,7 @@
 HEIGHT = 32
 WIDTH = 32
 CELLS = HEIGHT * WIDTH
-VMEM_BYTES = 28 * 2**20
+VMEM_BYTES = 24 * 2**20
 ANY = pl.BlockSpec(memory_space=pl.ANY)
 WHOLE = pl.BlockSpec(memory_space=pltpu.VMEM)
 

time: 80.6 us -> 80.6 us (level)
  no operation moved by 1% of the time
where the time goes in v9:
time: 80.6 us; the launch traced here: 80.2 us
  Pallas kernels  35.6 us (44%)
  starting transfers between devices  26.6 us (33%)
  waiting for transfers between devices  15.1 us (19%)
  local copies, waits for them, and re-layouts  2.38 us (3%)
    pallas_call x8, Pallas kernels, conv_call(): pl.pallas_call(functools.partial(conv_kernel, tuple(parts), tuple(ready),...  28 us
    ppermute x5, starting transfers between devices, hop(): pieces[i] = lax.ppermute(pieces[i - 2], 'dp', ring.pairs)  7.83 us
    ppermute x5, waiting for transfers between devices, hop(): pieces[i] = lax.ppermute(pieces[i - 2], 'dp', ring.pairs)  5.66 us
    all_to_all x1, starting transfers between devices, body(): act_rows = lax.all_to_all(act, 'dp', 0, 0, tiled=True)  5.55 us
    all_to_all x1, waiting for transfers between devices, body(): act_rows = lax.all_to_all(act, 'dp', 0, 0, tiled=True)  4.83 us
    all_to_all x1, starting transfers between devices, body(): terms = lax.all_to_all(terms, 'dp', 0, 0, tiled=True)  3.5 us
    ppermute x2, starting transfers between devices, body(): lax.ppermute(pieces[i - 2][rows_of_taps[0]:rows_of_taps[-1] + 1], 'dp', r...  3.41 us
    pallas_call x1, Pallas kernels, norm_call(): pl.pallas_call(functools.partial(norm_kernel, units, chan), out_shape=jax...  3.2 us
  transfers between devices with their start and end apart: 21, of which 8 were waited for; matrix products, arithmetic and copies ran while one was open for 0% of the time, Pallas kernels for 42%

profile of v9, /device:TPU:0, one launch (start us, length us, event | category | flops | bytes accessed | tf_op | source)
XLA Modules:
  0.0 80.2 jit_solution(17446859261268563576)
XLA Ops:
  0.5 2.6 %collective-permute-start.4 = (bf16[3,240,640]{2,1,0:T(8,128)(2,1)}, bf16[3,240,640]{2,1,0:T(8,128)(2,1)S(1)}, u32[]{:S(2)}, u32[]{:S(2)}) collective-permute-start(bf16[3,240,640]{2,1,0:T(8,128)(2,1)} %bitcast.10), channel_id=1, source_target_pairs={{0,8},{8,16},{16,24},{24,28},{28,20},{20,12},{12,4},{4,0},{2,6},{1... | collective-permute-start | bytes 2764808 | tf_op jit(solution)/shard_map/ppermute | solution.py:334
  3.0 1.5 %collective-permute-start.3 = (bf16[8,80,1024]{2,1,0:T(8,128)(2,1)}, bf16[8,80,1024]{2,1,0:T(8,128)(2,1)}, u32[]{:S(2)}, u32[]{:S(2)}) collective-permute-start(bf16[8,80,1024]{2,1,0:T(8,128)(2,1)} %bitcast.6), channel_id=1, source_target_pairs={{0,1},{1,0},{2,3},{3,2},{4,5},{5,4},{6,7},{7,6},{8,9},{9,8},{10,11... | collective-permute-start | bytes 3932168 | tf_op jit(solution)/shard_map/ppermute | solution.py:323
  5.2 0.7 act_rows.1.refs_1_
  5.9 5.6 %all-to-all-start = ((bf16[16,1,80]{2,1,0:T(2,128)(2,1)}), bf16[16,1,80]{2,1,0:T(2,128)(2,1)S(1)}, u32[]{:S(2)}, u32[]{:S(2)}) async-start(bf16[16,1,80]{2,1,0:T(2,128)(2,1)} %act_rows.1.refs_1_), calls=%async_computation | async-start | bytes 16384 | tf_op jit(solution)/shard_map/all_to_all | solution.py:344
  11.5 2.0 %collective-permute-start.1 = (bf16[3,240,640]{2,1,0:T(8,128)(2,1)S(1)}, bf16[3,240,640]{2,1,0:T(8,128)(2,1)}, u32[]{:S(2)}, u32[]{:S(2)}) collective-permute-start(bf16[3,240,640]{2,1,0:T(8,128)(2,1)S(1)} %gate.8.refs_2_), channel_id=1, source_target_pairs={{0,8},{8,16},{16,24},{24,28},{28,20},{20,12},{12,4},{4,0},{2,6},{1... | collective-permute-start | bytes 2764808 | tf_op jit(solution)/shard_map/ppermute | solution.py:341
  13.5 4.8 %all-to-all-done.act_ref = bf16[16,1,80]{2,1,0:T(2,128)(2,1)S(1)} async-done(((bf16[16,1,80]{2,1,0:T(2,128)(2,1)}), bf16[16,1,80]{2,1,0:T(2,128)(2,1)S(1)}, u32[]{:S(2)}, u32[]{:S(2)}) %all-to-all-start) | async-done | bytes 2592 | tf_op jit(solution)/shard_map/all_to_all | solution.py:344
  18.4 0.8 emb_terms.1.refs_1_
  19.1 3.5 %all-to-all-start.1 = ((f32[16,1,640]{2,1,0:T(1,128)}), f32[16,1,640]{2,1,0:T(1,128)S(1)}, u32[]{:S(2)}, u32[]{:S(2)}) async-start(f32[16,1,640]{2,1,0:T(1,128)} %emb_terms.1.refs_1_), calls=%async_computation.1 | async-start | bytes 81920 | tf_op jit(solution)/shard_map/all_to_all | solution.py:351
  22.7 1.9 %collective-permute-start.7 = (bf16[3,240,640]{2,1,0:T(8,128)(2,1)S(1)}, bf16[3,240,640]{2,1,0:T(8,128)(2,1)}, u32[]{:S(2)}, u32[]{:S(2)}) collective-permute-start(bf16[3,240,640]{2,1,0:T(8,128)(2,1)S(1)} %gate.9.refs_3_), channel_id=1, source_target_pairs={{0,8},{8,16},{16,24},{24,28},{28,20},{20,12},{12,4},{4,0},{2,6},{1... | collective-permute-start | bytes 2764808 | tf_op jit(solution)/shard_map/ppermute | solution.py:341
  24.6 1.3 %copy-done.1 = bf16[1,640,1024]{2,1,0:T(8,128)(2,1)S(1)} copy-done((bf16[1,640,1024]{2,1,0:T(8,128)(2,1)S(1)}, bf16[1,640,1024]{2,1,0:T(8,128)(2,1)}, u32[]{:S(2)}) %copy-start.1) | copy-done | bytes 1310744
  25.9 1.2 %channel_stats.1.table_ref.refs_5_ = f32[6,640]{1,0:T(8,128)S(1)} custom-call(bf16[640,1024]{1,0:T(8,128)(2,1)S(1)} %bitcast.7, f32[640]{0:T(1024)S(1)} %copy-done.7, f32[640]{0:T(1024)S(1)} %copy-done.8, f32[640]{0:T(1024)S(1)} %copy-done.9, f32[640]{0:T(1024)S(1)} %copy-done.10), custom_call_target="tpu_custom_call" | custom-call | flops 10000000000 | bytes 40000000 | tf_op jit(solution)/shard_map/channel_stats/pallas_call | solution.py:127
  27.1 1.5 %collective-permute-start.9 = (bf16[3,240,640]{2,1,0:T(8,128)(2,1)}, bf16[3,240,640]{2,1,0:T(8,128)(2,1)S(1)}, u32[]{:S(2)}, u32[]{:S(2)}) collective-permute-start(bf16[3,240,640]{2,1,0:T(8,128)(2,1)} %collective-permute-done.1.refs_0_.refs_2_), channel_id=1, source_target_pairs={{0,8},{8,16},{16,24},{24,28},{28,20},{20,12},{12,4},{4,0},{2,6},{1... | collective-permute-start | bytes 2764808 | tf_op jit(solution)/shard_map/ppermute | solution.py:341
  29.3 1.8 %affine.1 = f32[8,2,80]{2,1,0:T(2,128)S(1)} custom-call(f32[16,1,640]{2,1,0:T(1,128)S(1)} %all-to-all-done.1.terms_ref, f32[6,640]{1,0:T(8,128)S(1)} %channel_stats.1.table_ref.refs_5_, bf16[3,240,640]{2,1,0:T(8,128)(2,1)} %collective-permute-done.1.refs_0_.refs_2_), custom_call_target="tpu_custom_call" | custom-call | flops 7000000000 | bytes 28000000 | tf_op jit(solution)/shard_map/affine/pallas_call | solution.py:170
  31.1 1.5 %collective-permute-start.2 = (f32[8,2,80]{2,1,0:T(2,128)S(1)}, f32[8,2,80]{2,1,0:T(2,128)S(1)}, u32[]{:S(2)}, u32[]{:S(2)}) collective-permute-start(f32[8,2,80]{2,1,0:T(2,128)S(1)} %affine.1), channel_id=1, source_target_pairs={{0,1},{1,0},{2,3},{3,2},{4,5},{5,4},{6,7},{7,6},{8,9},{9,8},{10,11... | collective-permute-start | bytes 15368 | tf_op jit(solution)/shard_map/ppermute | solution.py:323
  32.6 2.2 %collective-permute-done.2 = f32[8,2,80]{2,1,0:T(2,128)S(1)} collective-permute-done((f32[8,2,80]{2,1,0:T(2,128)S(1)}, f32[8,2,80]{2,1,0:T(2,128)S(1)}, u32[]{:S(2)}, u32[]{:S(2)}) %collective-permute-start.2) | collective-permute-done | bytes 5152 | tf_op jit(solution)/shard_map/ppermute | solution.py:323
  34.8 3.2 %norm_units.1.refs_0_.refs_1_ = bf16[16,80,1024]{2,1,0:T(8,128)(2,1)S(1)} custom-call(s32[256]{0:T(256)S(1)} %copy-done.6, f32[16,2,80]{2,1,0:T(2,128)S(1)} %pad_maximum_fusion.ab_ref, bf16[8,80,1024]{2,1,0:T(8,128)(2,1)S(1)} %bitcast.8, bf16[8,80,1024]{2,1,0:T(8,128)(2,1)} %collective-permute-done.3.refs_1_), custom_call_target="tpu_custom_call" | custom-call | tf_op jit(solution)/shard_map/norm_units/pallas_call | solution.py:206
  38.1 0.9 %collective-permute-start.11 = (bf16[3,240,640]{2,1,0:T(8,128)(2,1)}, bf16[3,240,640]{2,1,0:T(8,128)(2,1)S(1)}, u32[]{:S(2)}, u32[]{:S(2)}) collective-permute-start(bf16[3,240,640]{2,1,0:T(8,128)(2,1)} %gate.10.refs_4_), channel_id=1, source_target_pairs={{0,8},{8,16},{16,24},{24,28},{28,20},{20,12},{12,4},{4,0},{2,6},{1... | collective-permute-start | bytes 2764808 | tf_op jit(solution)/shard_map/ppermute | solution.py:341
  39.2 5.8 %conv_units.8 = (f32[640,1024]{1,0:T(8,128)S(1)}, f32[8,128]{1,0:T(8,128)S(1)}) custom-call(bf16[16,80,1024]{2,1,0:T(8,128)(2,1)S(1)} %norm_units.1.refs_0_.refs_1_, bf16[3,240,640]{2,1,0:T(8,128)(2,1)S(1)} %bitcast.11, bf16[3,240,640]{2,1,0:T(8,128)(2,1)S(1)} %gate.8.refs_2_, bf16[3,240,640]{2,1,0:T(8,128)(2,1)S(1)} %gate.9.refs_3_, ...), custom_call_target="tpu_custom_call" | custom-call | tf_op jit(solution)/shard_map/conv_units/pallas_call | solution.py:295
  45.1 1.3 %collective-permute-done.9.refs_0_ = bf16[3,240,640]{2,1,0:T(8,128)(2,1)S(1)} collective-permute-done((bf16[3,240,640]{2,1,0:T(8,128)(2,1)}, bf16[3,240,640]{2,1,0:T(8,128)(2,1)S(1)}, u32[]{:S(2)}, u32[]{:S(2)}) %collective-permute-start.9) | collective-permute-done | bytes 921632 | tf_op jit(solution)/shard_map/ppermute | solution.py:341
  46.4 1.5 %collective-permute-start.13 = (bf16[3,240,640]{2,1,0:T(8,128)(2,1)S(1)}, bf16[3,240,640]{2,1,0:T(8,128)(2,1)S(1)}, u32[]{:S(2)}, u32[]{:S(2)}) collective-permute-start(bf16[3,240,640]{2,1,0:T(8,128)(2,1)S(1)} %gate.11.refs_3_), channel_id=1, source_target_pairs={{0,8},{8,16},{16,24},{24,28},{28,20},{20,12},{12,4},{4,0},{2,6},{1... | collective-permute-start | bytes 2764808 | tf_op jit(solution)/shard_map/ppermute | solution.py:341
  47.9 5.4 %conv_units.9 = (f32[640,1024]{1,0:T(8,128)S(1)}, f32[8,128]{1,0:T(8,128)S(1)}) custom-call(f32[640,1024]{1,0:T(8,128)S(1)} %get-tuple-element.20.refs_0_, bf16[16,80,1024]{2,1,0:T(8,128)(2,1)S(1)} %norm_units.1.refs_0_.refs_1_, bf16[3,240,640]{2,1,0:T(8,128)(2,1)} %collective-permute-done.1.refs_0_.refs_2_, ...), custom_call_target="tpu_custom_call", output_to_operand_aliasing={{0}: (0, {})} | custom-call | tf_op jit(solution)/shard_map/conv_units/pallas_call | solution.py:295
  53.4 2.9 %collective-permute-done.11.refs_0_ = bf16[3,240,640]{2,1,0:T(8,128)(2,1)S(1)} collective-permute-done((bf16[3,240,640]{2,1,0:T(8,128)(2,1)}, bf16[3,240,640]{2,1,0:T(8,128)(2,1)S(1)}, u32[]{:S(2)}, u32[]{:S(2)}) %collective-permute-start.11) | collective-permute-done | bytes 921632 | tf_op jit(solution)/shard_map/ppermute | solution.py:341
  56.3 1.6 %collective-permute-start.15 = (bf16[2,240,640]{2,1,0:T(8,128)(2,1)S(1)}, bf16[2,240,640]{2,1,0:T(8,128)(2,1)S(1)}, u32[]{:S(2)}, u32[]{:S(2)}) collective-permute-start(bf16[2,240,640]{2,1,0:T(8,128)(2,1)S(1)} %slice.8), channel_id=1, source_target_pairs={{0,8},{8,16},{16,24},{24,28},{28,20},{20,12},{12,4},{4,0},{2,6},{1... | collective-permute-start | bytes 1843208 | tf_op jit(solution)/shard_map/ppermute | solution.py:396
  57.9 3.3 %conv_units.10 = (f32[640,1024]{1,0:T(8,128)S(1)}, f32[8,128]{1,0:T(8,128)}) custom-call(f32[640,1024]{1,0:T(8,128)S(1)} %get-tuple-element.21.refs_0_, bf16[16,80,1024]{2,1,0:T(8,128)(2,1)S(1)} %norm_units.1.refs_0_.refs_1_, bf16[3,240,640]{2,1,0:T(8,128)(2,1)S(1)} %collective-permute-done.8.refs_2_, ...), custom_call_target="tpu_custom_call", output_to_operand_aliasing={{0}: (0, {})} | custom-call | tf_op jit(solution)/shard_map/conv_units/pallas_call | solution.py:295
  61.2 3.3 %conv_units.11 = (f32[640,1024]{1,0:T(8,128)S(1)}, f32[8,128]{1,0:T(8,128)S(1)}) custom-call(f32[640,1024]{1,0:T(8,128)S(1)} %get-tuple-element.23.refs_0_, bf16[16,80,1024]{2,1,0:T(8,128)(2,1)S(1)} %norm_units.1.refs_0_.refs_1_, bf16[3,240,640]{2,1,0:T(8,128)(2,1)S(1)} %collective-permute-done.10.refs_2_, ...), custom_call_target="tpu_custom_call", output_to_operand_aliasing={{0}: (0, {})} | custom-call | tf_op jit(solution)/shard_map/conv_units/pallas_call | solution.py:295
  64.6 1.5 %collective-permute-done.13.refs_0_ = bf16[3,240,640]{2,1,0:T(8,128)(2,1)S(1)} collective-permute-done((bf16[3,240,640]{2,1,0:T(8,128)(2,1)S(1)}, bf16[3,240,640]{2,1,0:T(8,128)(2,1)S(1)}, u32[]{:S(2)}, u32[]{:S(2)}) %collective-permute-start.13) | collective-permute-done | bytes 921632 | tf_op jit(solution)/shard_map/ppermute | solution.py:341
  66.1 1.8 %collective-permute-start.17 = (bf16[1,240,640]{2,1,0:T(8,128)(2,1)S(1)}, bf16[1,240,640]{2,1,0:T(8,128)(2,1)S(1)}, u32[]{:S(2)}, u32[]{:S(2)}) collective-permute-start(bf16[1,240,640]{2,1,0:T(8,128)(2,1)S(1)} %slice.9), channel_id=1, source_target_pairs={{0,8},{8,16},{16,24},{24,28},{28,20},{20,12},{12,4},{4,0},{2,6},{1... | collective-permute-start | bytes 921608 | tf_op jit(solution)/shard_map/ppermute | solution.py:396
  68.0 3.4 %conv_units.12 = (f32[640,1024]{1,0:T(8,128)S(1)}, f32[8,128]{1,0:T(8,128)S(1)}, bf16[720,1024]{1,0:T(8,128)(2,1)S(1)}, bf16[720,1024]{1,0:T(8,128)(2,1)S(1)}) custom-call(f32[640,1024]{1,0:T(8,128)S(1)} %get-tuple-element.25.refs_0_, bf16[16,80,1024]{2,1,0:T(8,128)(2,1)S(1)} %norm_units.1.refs_0_.refs_1_, ...), custom_call_target="tpu_custom_call", output_to_operand_aliasing={{0}: (0, {})} | custom-call | tf_op jit(solution)/shard_map/conv_units/pallas_call | solution.py:295
  71.3 1.4 %collective-permute-done.15.refs_0_ = bf16[2,240,640]{2,1,0:T(8,128)(2,1)S(1)} collective-permute-done((bf16[2,240,640]{2,1,0:T(8,128)(2,1)S(1)}, bf16[2,240,640]{2,1,0:T(8,128)(2,1)S(1)}, u32[]{:S(2)}, u32[]{:S(2)}) %collective-permute-start.15) | collective-permute-done | bytes 614432 | tf_op jit(solution)/shard_map/ppermute | solution.py:396
  72.7 2.9 %conv_units.13 = (f32[640,1024]{1,0:T(8,128)S(1)}, f32[8,128]{1,0:T(8,128)S(1)}) custom-call(f32[640,1024]{1,0:T(8,128)S(1)} %get-tuple-element.27.refs_0_, bf16[16,80,1024]{2,1,0:T(8,128)(2,1)S(1)} %norm_units.1.refs_0_.refs_1_, bf16[3,240,640]{2,1,0:T(8,128)(2,1)S(1)} %collective-permute-done.14.refs_2_, ...), custom_call_target="tpu_custom_call", output_to_operand_aliasing={{0}: (0, {})} | custom-call | tf_op jit(solution)/shard_map/conv_units/pallas_call | solution.py:295
  76.2 1.5 %conv_units.14 = (f32[640,1024]{1,0:T(8,128)S(1)}, f32[8,128]{1,0:T(8,128)}) custom-call(f32[640,1024]{1,0:T(8,128)S(1)} %get-tuple-element.30.refs_0_, bf16[16,80,1024]{2,1,0:T(8,128)(2,1)S(1)} %norm_units.1.refs_0_.refs_1_, bf16[2,240,640]{2,1,0:T(8,128)(2,1)S(1)} %collective-permute-done.16.refs_2_, ...), custom_call_target="tpu_custom_call", output_to_operand_aliasing={{0}: (0, {})} | custom-call | tf_op jit(solution)/shard_map/conv_units/pallas_call | solution.py:295
  77.7 2.3 %conv_units.15 = (bf16[640,1024]{1,0:T(8,128)(2,1)}, f32[8,128]{1,0:T(8,128)}) custom-call(f32[640,1024]{1,0:T(8,128)S(1)} %get-tuple-element.32.refs_0_, bf16[16,80,1024]{2,1,0:T(8,128)(2,1)S(1)} %norm_units.1.refs_0_.refs_1_, bf16[1,240,640]{2,1,0:T(8,128)(2,1)S(1)} %gate.15.refs_2_, bf16[1,240,640]{2,1,0:T(8,128)(2,1)S(1)} %collective-permute-done.18.refs_3_, ...), custom_call_target="tpu_custom_call" | custom-call | tf_op jit(solution)/shard_map/conv_units/pallas_call | solution.py:295
  (56 shorter events, 2.9 us)
Async XLA Ops:
  0.0 4.5 %collective-permute-start = (bf16[3,240,640]{2,1,0:T(8,128)(2,1)}, bf16[3,240,640]{2,1,0:T(8,128)(2,1)S(1)}, u32[]{:S(2)}, u32[]{:S(2)}) collective-permute-start(bf16[3,240,640]{2,1,0:T(8,128)(2,1)} %bitcast.9), channel_id=1, source_target_pairs={{0,2},{2,0},{4,6},{6,4},{8,10},{10,8},{12,14},{14,12},{16,18},{18,... | collective-permute-start | bytes 2764808 | tf_op jit(solution)/shard_map/ppermute | solution.py:333
  0.5 22.2 %collective-permute-start.4 = (bf16[3,240,640]{2,1,0:T(8,128)(2,1)}, bf16[3,240,640]{2,1,0:T(8,128)(2,1)S(1)}, u32[]{:S(2)}, u32[]{:S(2)}) collective-permute-start(bf16[3,240,640]{2,1,0:T(8,128)(2,1)} %bitcast.10), channel_id=1, source_target_pairs={{0,8},{8,16},{16,24},{24,28},{28,20},{20,12},{12,4},{4,0},{2,6},{1... | collective-permute-start | bytes 2764808 | tf_op jit(solution)/shard_map/ppermute | solution.py:334
  3.0 31.8 %collective-permute-start.3 = (bf16[8,80,1024]{2,1,0:T(8,128)(2,1)}, bf16[8,80,1024]{2,1,0:T(8,128)(2,1)}, u32[]{:S(2)}, u32[]{:S(2)}) collective-permute-start(bf16[8,80,1024]{2,1,0:T(8,128)(2,1)} %bitcast.6), channel_id=1, source_target_pairs={{0,1},{1,0},{2,3},{3,2},{4,5},{5,4},{6,7},{7,6},{8,9},{9,8},{10,11... | collective-permute-start | bytes 3932168 | tf_op jit(solution)/shard_map/ppermute | solution.py:323
  4.5 0.7 copy-start.5
  5.9 12.4 %all-to-all-start = ((bf16[16,1,80]{2,1,0:T(2,128)(2,1)}), bf16[16,1,80]{2,1,0:T(2,128)(2,1)S(1)}, u32[]{:S(2)}, u32[]{:S(2)}) async-start(bf16[16,1,80]{2,1,0:T(2,128)(2,1)} %act_rows.1.refs_1_), calls=%async_computation | async-start | bytes 16384 | tf_op jit(solution)/shard_map/all_to_all | solution.py:344
  11.5 6.9 %copy-start.4 = (bf16[80,640]{1,0:T(8,128)(2,1)S(1)}, bf16[80,640]{1,0:T(8,128)(2,1)}, u32[]{:S(2)}) copy-start(bf16[80,640]{1,0:T(8,128)(2,1)} %w_ref.1) | copy-start | bytes 307204
  11.5 13.0 %copy-start.7 = (f32[640]{0:T(1024)S(1)}, f32[640]{0:T(1024)}, u32[]{:S(2)}) copy-start(f32[640]{0:T(1024)} %refs_0_.1) | copy-start | bytes 7684
  11.5 13.0 %copy-start.8 = (f32[640]{0:T(1024)S(1)}, f32[640]{0:T(1024)}, u32[]{:S(2)}) copy-start(f32[640]{0:T(1024)} %refs_1_.1) | copy-start | bytes 7684
  11.5 13.0 %copy-start.9 = (f32[640]{0:T(1024)S(1)}, f32[640]{0:T(1024)}, u32[]{:S(2)}) copy-start(f32[640]{0:T(1024)} %refs_2_.1) | copy-start | bytes 7684
  11.5 13.0 %copy-start.10 = (f32[640]{0:T(1024)S(1)}, f32[640]{0:T(1024)}, u32[]{:S(2)}) copy-start(f32[640]{0:T(1024)} %refs_3_.1) | copy-start | bytes 7684
  11.5 15.6 %collective-permute-start.1 = (bf16[3,240,640]{2,1,0:T(8,128)(2,1)S(1)}, bf16[3,240,640]{2,1,0:T(8,128)(2,1)}, u32[]{:S(2)}, u32[]{:S(2)}) collective-permute-start(bf16[3,240,640]{2,1,0:T(8,128)(2,1)S(1)} %gate.8.refs_2_), channel_id=1, source_target_pairs={{0,8},{8,16},{16,24},{24,28},{28,20},{20,12},{12,4},{4,0},{2,6},{1... | collective-permute-start | bytes 2764808 | tf_op jit(solution)/shard_map/ppermute | solution.py:341
  19.1 10.2 %all-to-all-start.1 = ((f32[16,1,640]{2,1,0:T(1,128)}), f32[16,1,640]{2,1,0:T(1,128)S(1)}, u32[]{:S(2)}, u32[]{:S(2)}) async-start(f32[16,1,640]{2,1,0:T(1,128)} %emb_terms.1.refs_1_), calls=%async_computation.1 | async-start | bytes 81920 | tf_op jit(solution)/shard_map/all_to_all | solution.py:351
  22.7 15.4 %collective-permute-start.7 = (bf16[3,240,640]{2,1,0:T(8,128)(2,1)S(1)}, bf16[3,240,640]{2,1,0:T(8,128)(2,1)}, u32[]{:S(2)}, u32[]{:S(2)}) collective-permute-start(bf16[3,240,640]{2,1,0:T(8,128)(2,1)S(1)} %gate.9.refs_3_), channel_id=1, source_target_pairs={{0,8},{8,16},{16,24},{24,28},{28,20},{20,12},{12,4},{4,0},{2,6},{1... | collective-permute-start | bytes 2764808 | tf_op jit(solution)/shard_map/ppermute | solution.py:341
  24.5 1.3 %copy-start.1 = (bf16[1,640,1024]{2,1,0:T(8,128)(2,1)S(1)}, bf16[1,640,1024]{2,1,0:T(8,128)(2,1)}, u32[]{:S(2)}) copy-start(bf16[1,640,1024]{2,1,0:T(8,128)(2,1)} %param.10) | copy-start | bytes 3932164
  27.0 7.8 %copy-start.6 = (s32[256]{0:T(256)S(1)}, s32[256]{0:T(256)}, u32[]{:S(2)}) copy-start(s32[256]{0:T(256)} %constant.2.clone.blocks_ref) | copy-start | bytes 3076
  27.0 11.9 %collective-permute-start.5 = (bf16[3,240,640]{2,1,0:T(8,128)(2,1)S(1)}, bf16[3,240,640]{2,1,0:T(8,128)(2,1)}, u32[]{:S(2)}, u32[]{:S(2)}) collective-permute-start(bf16[3,240,640]{2,1,0:T(8,128)(2,1)S(1)} %gate.9.refs_3_), channel_id=1, source_target_pairs={{0,2},{2,0},{4,6},{6,4},{8,10},{10,8},{12,14},{14,12},{16,18},{18,... | collective-permute-start | bytes 2764808 | tf_op jit(solution)/shard_map/ppermute | solution.py:364
  27.1 19.2 %collective-permute-start.9 = (bf16[3,240,640]{2,1,0:T(8,128)(2,1)}, bf16[3,240,640]{2,1,0:T(8,128)(2,1)S(1)}, u32[]{:S(2)}, u32[]{:S(2)}) collective-permute-start(bf16[3,240,640]{2,1,0:T(8,128)(2,1)} %collective-permute-done.1.refs_0_.refs_2_), channel_id=1, source_target_pairs={{0,8},{8,16},{16,24},{24,28},{28,20},{20,12},{12,4},{4,0},{2,6},{1... | collective-permute-start | bytes 2764808 | tf_op jit(solution)/shard_map/ppermute | solution.py:341
  29.3 5.5 %copy-start.2 = (bf16[1,640,1024]{2,1,0:T(8,128)(2,1)S(1)}, bf16[1,640,1024]{2,1,0:T(8,128)(2,1)}, u32[]{:S(2)}) copy-start(bf16[1,640,1024]{2,1,0:T(8,128)(2,1)} %param.10) | copy-start | bytes 3932164
  31.1 3.7 %collective-permute-start.2 = (f32[8,2,80]{2,1,0:T(2,128)S(1)}, f32[8,2,80]{2,1,0:T(2,128)S(1)}, u32[]{:S(2)}, u32[]{:S(2)}) collective-permute-start(f32[8,2,80]{2,1,0:T(2,128)S(1)} %affine.1), channel_id=1, source_target_pairs={{0,1},{1,0},{2,3},{3,2},{4,5},{5,4},{6,7},{7,6},{8,9},{9,8},{10,11... | collective-permute-start | bytes 15368 | tf_op jit(solution)/shard_map/ppermute | solution.py:323
  34.8 13.1 %collective-permute-start.6 = (bf16[3,240,640]{2,1,0:T(8,128)(2,1)}, bf16[3,240,640]{2,1,0:T(8,128)(2,1)S(1)}, u32[]{:S(2)}, u32[]{:S(2)}) collective-permute-start(bf16[3,240,640]{2,1,0:T(8,128)(2,1)} %collective-permute-done.1.refs_0_.refs_2_), channel_id=1, source_target_pairs={{0,2},{2,0},{4,6},{6,4},{8,10},{10,8},{12,14},{14,12},{16,18},{18,... | collective-permute-start | bytes 2764808 | tf_op jit(solution)/shard_map/ppermute | solution.py:364
  38.0 1.2 %copy-start.3 = (bf16[9,80,640]{2,1,0:T(8,128)(2,1)S(1)}, bf16[9,80,640]{2,1,0:T(8,128)(2,1)}, u32[]{:S(2)}) copy-start(bf16[9,80,640]{2,1,0:T(8,128)(2,1)} %param.17) | copy-start | bytes 2764804
  38.1 18.2 %collective-permute-start.11 = (bf16[3,240,640]{2,1,0:T(8,128)(2,1)}, bf16[3,240,640]{2,1,0:T(8,128)(2,1)S(1)}, u32[]{:S(2)}, u32[]{:S(2)}) collective-permute-start(bf16[3,240,640]{2,1,0:T(8,128)(2,1)} %gate.10.refs_4_), channel_id=1, source_target_pairs={{0,8},{8,16},{16,24},{24,28},{28,20},{20,12},{12,4},{4,0},{2,6},{1... | collective-permute-start | bytes 2764808 | tf_op jit(solution)/shard_map/ppermute | solution.py:341
  39.0 18.9 %collective-permute-start.8 = (bf16[3,240,640]{2,1,0:T(8,128)(2,1)}, bf16[3,240,640]{2,1,0:T(8,128)(2,1)S(1)}, u32[]{:S(2)}, u32[]{:S(2)}) collective-permute-start(bf16[3,240,640]{2,1,0:T(8,128)(2,1)} %gate.10.refs_4_), channel_id=1, source_target_pairs={{0,2},{2,0},{4,6},{6,4},{8,10},{10,8},{12,14},{14,12},{16,18},{18,... | collective-permute-start | bytes 2764808 | tf_op jit(solution)/shard_map/ppermute | solution.py:364
  46.4 14.9 %collective-permute-start.10 = (bf16[3,240,640]{2,1,0:T(8,128)(2,1)S(1)}, bf16[3,240,640]{2,1,0:T(8,128)(2,1)S(1)}, u32[]{:S(2)}, u32[]{:S(2)}) collective-permute-start(bf16[3,240,640]{2,1,0:T(8,128)(2,1)S(1)} %gate.11.refs_3_), channel_id=1, source_target_pairs={{0,2},{2,0},{4,6},{6,4},{8,10},{10,8},{12,14},{14,12},{16,18},{18,... | collective-permute-start | bytes 2764808 | tf_op jit(solution)/shard_map/ppermute | solution.py:364
  46.4 19.7 %collective-permute-start.13 = (bf16[3,240,640]{2,1,0:T(8,128)(2,1)S(1)}, bf16[3,240,640]{2,1,0:T(8,128)(2,1)S(1)}, u32[]{:S(2)}, u32[]{:S(2)}) collective-permute-start(bf16[3,240,640]{2,1,0:T(8,128)(2,1)S(1)} %gate.11.refs_3_), channel_id=1, source_target_pairs={{0,8},{8,16},{16,24},{24,28},{28,20},{20,12},{12,4},{4,0},{2,6},{1... | collective-permute-start | bytes 2764808 | tf_op jit(solution)/shard_map/ppermute | solution.py:341
  56.2 11.7 %collective-permute-start.12 = (bf16[3,240,640]{2,1,0:T(8,128)(2,1)S(1)}, bf16[3,240,640]{2,1,0:T(8,128)(2,1)S(1)}, u32[]{:S(2)}, u32[]{:S(2)}) collective-permute-start(bf16[3,240,640]{2,1,0:T(8,128)(2,1)S(1)} %gate.12.refs_3_), channel_id=1, source_target_pairs={{0,2},{2,0},{4,6},{6,4},{8,10},{10,8},{12,14},{14,12},{16,18},{18,... | collective-permute-start | bytes 2764808 | tf_op jit(solution)/shard_map/ppermute | solution.py:364
  56.3 16.4 %collective-permute-start.15 = (bf16[2,240,640]{2,1,0:T(8,128)(2,1)S(1)}, bf16[2,240,640]{2,1,0:T(8,128)(2,1)S(1)}, u32[]{:S(2)}, u32[]{:S(2)}) collective-permute-start(bf16[2,240,640]{2,1,0:T(8,128)(2,1)S(1)} %slice.8), channel_id=1, source_target_pairs={{0,8},{8,16},{16,24},{24,28},{28,20},{20,12},{12,4},{4,0},{2,6},{1... | collective-permute-start | bytes 1843208 | tf_op jit(solution)/shard_map/ppermute | solution.py:396
  64.6 3.4 %copy-start = (bf16[1,640,1024]{2,1,0:T(8,128)(2,1)S(1)}, bf16[1,640,1024]{2,1,0:T(8,128)(2,1)}, u32[]{:S(2)}) copy-start(bf16[1,640,1024]{2,1,0:T(8,128)(2,1)} %param.11) | copy-start | bytes 3932164
  66.1 6.6 %collective-permute-start.14 = (bf16[3,240,640]{2,1,0:T(8,128)(2,1)S(1)}, bf16[3,240,640]{2,1,0:T(8,128)(2,1)S(1)}, u32[]{:S(2)}, u32[]{:S(2)}) collective-permute-start(bf16[3,240,640]{2,1,0:T(8,128)(2,1)S(1)} %gate.13.refs_3_), channel_id=1, source_target_pairs={{0,2},{2,0},{4,6},{6,4},{8,10},{10,8},{12,14},{14,12},{16,18},{18,... | collective-permute-start | bytes 2764808 | tf_op jit(solution)/shard_map/ppermute | solution.py:364
  66.1 9.8 %collective-permute-start.17 = (bf16[1,240,640]{2,1,0:T(8,128)(2,1)S(1)}, bf16[1,240,640]{2,1,0:T(8,128)(2,1)S(1)}, u32[]{:S(2)}, u32[]{:S(2)}) collective-permute-start(bf16[1,240,640]{2,1,0:T(8,128)(2,1)S(1)} %slice.9), channel_id=1, source_target_pairs={{0,8},{8,16},{16,24},{24,28},{28,20},{20,12},{12,4},{4,0},{2,6},{1... | collective-permute-start | bytes 921608 | tf_op jit(solution)/shard_map/ppermute | solution.py:396
  72.7 3.5 %collective-permute-start.16 = (bf16[2,240,640]{2,1,0:T(8,128)(2,1)S(1)}, bf16[2,240,640]{2,1,0:T(8,128)(2,1)S(1)}, u32[]{:S(2)}, u32[]{:S(2)}) collective-permute-start(bf16[2,240,640]{2,1,0:T(8,128)(2,1)S(1)} %gate.14.refs_3_), channel_id=1, source_target_pairs={{0,2},{2,0},{4,6},{6,4},{8,10},{10,8},{12,14},{14,12},{16,18},{18,... | collective-permute-start | bytes 1843208 | tf_op jit(solution)/shard_map/ppermute | solution.py:364
  76.0 1.7 %collective-permute-start.18 = (bf16[1,240,640]{2,1,0:T(8,128)(2,1)S(1)}, bf16[1,240,640]{2,1,0:T(8,128)(2,1)S(1)}, u32[]{:S(2)}, u32[]{:S(2)}) collective-permute-start(bf16[1,240,640]{2,1,0:T(8,128)(2,1)S(1)} %gate.15.refs_2_), channel_id=1, source_target_pairs={{0,2},{2,0},{4,6},{6,4},{8,10},{10,8},{12,14},{14,12},{16,18},{18,... | collective-permute-start | bytes 921608 | tf_op jit(solution)/shard_map/ppermute | solution.py:364
